TPU v7x, 512 devices: a whole 4x4x16 slice. The times are simulated.
512 devices in a mesh: row: 16 (over z_lo, core), col: 16 (over y, x), layer: 2 (over z_hi).
Axes of the slice: x: 4, y: 4, z: 16 (z_hi: 2, z_lo: 8; z = z_hi * 8 + z_lo), core: 2. Of those that a mesh axis runs over, the one named last changes fastest.
Arguments:
- basis: float32 [4096, 4096], P('row', 'col'), may hold values from -1 to 1, as said below
- basis_grad: float32 [4096, 4096], P('row', 'col'), may hold values from -768 to 768
- value_grad: float32 [4096], replicated, may hold values from -384 to 384
- ranks: int32 [4096], replicated, may hold values from 0 to 4095, each once
- offsets: int32 [4096], replicated, may hold values from 0 to 3
Outputs:
- grad_matrix: float32 [4096, 4096], P(('row', 'layer'), 'col')
Inputs may be any that keep to these rules, and one draw needn't show every extreme that they name: The columns of basis are orthonormal. ranks holds every number of 0 to 4095 once, so eigenvalues of different indices differ by 1 or more.
All inputs are finite; a program needn't handle non-finite values.
Results may differ from a plain program's by a relative error of at most 0.000098.
Values sent between devices are 32-bit elements; how exact they have to be, the bound alone decides.
No kernel may reach another device: no remote copies, remote signals or barrier semaphores. Data moves between devices by JAX's collectives and lax.ppermute only.
A program may use at most 64 MiB of HBM per device.

v0:
```python
import jax
import jax.numpy as jnp
from jax import lax
from jax.sharding import Mesh
from jax.sharding import PartitionSpec as P

ROW = ("row_0", "row_1")
ROW_LAYER = ("row_0", "row_1", "layer")


def sent_to_all(x, axis):
    peers = lax.axis_size(axis)
    return lax.all_to_all(jnp.broadcast_to(x[None], (peers, *x.shape)), axis, 0, 0, tiled=True)


def in_order(pieces, dim):
    lengths = list(pieces.shape[1:])
    lengths[dim] *= pieces.shape[0]
    return jnp.moveaxis(pieces, 0, dim).reshape(lengths)


def whole_of(x, axes, dim):
    far, near = axes
    pieces = sent_to_all(sent_to_all(x, far), near)
    return in_order(pieces.swapaxes(0, 1).reshape(-1, *x.shape), dim)


def filled_up(lines, peers):
    spare = -len(lines) % peers
    return jnp.pad(lines, [(0, spare)] + [(0, 0)] * (lines.ndim - 1))


def from_root(x, axis, root):
    lines = jnp.where(lax.axis_index(axis) == root, x, jnp.zeros_like(x)).reshape(
        -1, *x.shape[1:][-1:]
    )
    padded = filled_up(lines, lax.axis_size(axis))
    own = lax.psum_scatter(padded, axis, scatter_dimension=0, tiled=True)
    return lax.all_gather(own, axis, axis=0, tiled=True)[: len(lines)].reshape(x.shape)


def cut_along(x, dim, peers):
    lengths = x.shape
    pieces = x.reshape(*lengths[:dim], peers, lengths[dim] // peers, *lengths[dim + 1 :])
    return jnp.moveaxis(pieces, dim, 0)


def summed_on_arrival(x, axis, dim):
    pieces = cut_along(x, dim, lax.axis_size(axis))
    arrived = lax.all_to_all(pieces, axis, split_axis=0, concat_axis=0, tiled=True)
    return arrived.sum(axis=0)


def gather_directly(x, axis, dim):
    return in_order(sent_to_all(x, axis), dim)


def on_device(basis, basis_grad, value_grad, ranks, offsets):
    highest = lax.Precision.HIGHEST
    rows_blk, cols_blk = basis.shape
    layers = lax.axis_size("layer")
    row_id = lax.axis_index(ROW)
    col_id = lax.axis_index("col")
    layer_id = lax.axis_index("layer")
    half_rows = rows_blk // layers
    half_cols = cols_blk // layers
    u_top = lax.dynamic_slice_in_dim(basis, layer_id * half_rows, half_rows, 0)
    du_top = lax.dynamic_slice_in_dim(basis_grad, layer_id * half_rows, half_rows, 0)
    column_strip = whole_of(u_top, ("row_0", "row_1"), 0)
    mirrored = from_root(column_strip, "col", row_id)
    section = mirrored
    inner = lax.dot_general(
        section,
        whole_of(du_top, ("row_0", "row_1"), 0),
        (((0,), (0,)), ((), ())),
        precision=highest,
        preferred_element_type=jnp.float32,
    )
    inner_half = summed_on_arrival(inner, "layer", 0)
    eigen = 4.0 * ranks.astype(jnp.float32) + offsets.astype(jnp.float32)
    row_begin = row_id * rows_blk + layer_id * half_rows
    col_begin = col_id * cols_blk
    row_index = row_begin + jnp.arange(half_rows, dtype=jnp.int32)
    col_index = col_begin + jnp.arange(cols_blk, dtype=jnp.int32)
    eigen_rows = lax.dynamic_slice_in_dim(eigen, row_begin, half_rows, 0)
    eigen_cols = lax.dynamic_slice_in_dim(eigen, col_begin, cols_blk, 0)
    grad_cols = lax.dynamic_slice_in_dim(value_grad, col_begin, cols_blk, 0)
    on_diagonal = row_index[:, None] == col_index[None, :]
    spacing = eigen_cols[None, :] - eigen_rows[:, None]
    scaled = jnp.where(
        on_diagonal,
        grad_cols[None, :],
        inner_half / jnp.where(on_diagonal, jnp.float32(1.0), spacing),
    )
    u_right = lax.dynamic_slice_in_dim(basis, layer_id * half_cols, half_cols, 1)
    u_strip = gather_directly(u_right, "col", 1)
    section = u_strip
    left_prod = jnp.dot(
        section,
        whole_of(scaled, ("row_0", "row_1"), 0),
        precision=highest,
        preferred_element_type=jnp.float32,
    )
    left_half = summed_on_arrival(left_prod, "layer", 1)
    far_rows = from_root(u_strip, ROW, col_id)
    section = far_rows
    product = lax.dot_general(
        gather_directly(left_half, "col", 1),
        section,
        (((1,), (1,)), ((), ())),
        precision=highest,
        preferred_element_type=jnp.float32,
    )
    return summed_on_arrival(product, "layer", 0)


def solution(mesh):
    torus = Mesh(
        mesh.devices.reshape(8, 2, mesh.shape["col"], mesh.shape["layer"]),
        ("row_0", "row_1", "col", "layer"),
    )
    return jax.shard_map(
        on_device,
        mesh=torus,
        in_specs=(P(ROW, "col"), P(ROW, "col"), P(), P(), P()),
        out_specs=P(ROW_LAYER, "col"),
        check_vma=False,
    )
```

profile of v0, /device:TPU:2, one launch (start us, length us, event | category | flops | bytes accessed | tf_op | source)
XLA Modules:
  0.0 460.6 jit_solution(14188077067508050847)
XLA Ops:
  9.5 12.5 %all-to-all-start.1 = ((f32[8,128,256]{1,2,0:T(8,128)}), f32[8,128,256]{1,2,0:T(8,128)S(1)}, u32[]{:S(2)}, u32[]{:S(2)}) async-start(f32[8,128,256]{1,2,0:T(8,128)} %broadcast_in_dim.34), calls=%async_computation.1 | async-start | bytes 2097152 | tf_op jit(solution)/shard_map/all_to_all | solution.py:13
  22.1 51.1 %all-to-all-done.1 = f32[8,128,256]{1,2,0:T(8,128)S(1)} async-done(((f32[8,128,256]{1,2,0:T(8,128)}), f32[8,128,256]{1,2,0:T(8,128)S(1)}, u32[]{:S(2)}, u32[]{:S(2)}) %all-to-all-start.1) | async-done | bytes 1048608 | tf_op jit(solution)/shard_map/all_to_all | solution.py:13
  74.0 6.3 %all_to_all.55 = f32[2,8,128,256]{2,1,3,0:T(8,128)} all-to-all(f32[2,8,128,256]{2,1,3,0:T(8,128)S(1)} %broadcast_in_dim.35), channel_id=1, replica_groups=mesh['row_0'=8,'row_1'=2,'col'=16,'layer'=2] {'row_1'}, dimensions={0} | all-to-all | bytes 4194304 | tf_op jit(solution)/shard_map/all_to_all | solution.py:13
  80.3 1.9 copy.17
  82.2 1.6 broadcast_select_fusion
  83.8 1.5 broadcast_in_dim.32
  85.3 7.6 %all-to-all-start = ((f32[16,256,128]{2,1,0:T(8,128)}), f32[16,256,128]{2,1,0:T(8,128)S(1)}, u32[]{:S(2)}, u32[]{:S(2)}) async-start(f32[16,256,128]{2,1,0:T(8,128)} %broadcast_in_dim.32), calls=%async_computation | async-start | bytes 4194304 | tf_op jit(solution)/shard_map/all_to_all | solution.py:13
  93.0 87.9 %reduce-scatter.3.cloned.1.call-done = f32[128,256]{1,0:T(8,128)} async-done(((f32[2048,256]{1,0:T(8,128)}), f32[128,256]{1,0:T(8,128)}) %reduce-scatter.3.cloned.1.call-update) | async-done | bytes 131088 | tf_op jit(solution)/shard_map/reduce_scatter | solution.py:38
  182.0 10.0 %all-to-all-start.3 = ((f32[8,128,256]{2,1,0:T(8,128)}), f32[8,128,256]{2,1,0:T(8,128)S(1)}, u32[]{:S(2)}, u32[]{:S(2)}) async-start(f32[8,128,256]{2,1,0:T(8,128)} %broadcast_in_dim.37), calls=%async_computation.4 | async-start | bytes 2097152 | tf_op jit(solution)/shard_map/all_to_all | solution.py:13
  192.1 1.6 bitcast_select_fusion
  193.7 55.1 %all-to-all-done.3 = f32[8,128,256]{2,1,0:T(8,128)S(1)} async-done(((f32[8,128,256]{2,1,0:T(8,128)}), f32[8,128,256]{2,1,0:T(8,128)S(1)}, u32[]{:S(2)}, u32[]{:S(2)}) %all-to-all-start.3) | async-done | bytes 1048608 | tf_op jit(solution)/shard_map/all_to_all | solution.py:13
  249.0 5.4 %all_to_all.56 = f32[2,8,128,256]{3,2,1,0:T(8,128)S(1)} all-to-all(f32[2,8,128,256]{3,2,1,0:T(8,128)S(1)} %broadcast_in_dim.38), channel_id=1, replica_groups=mesh['row_0'=8,'row_1'=2,'col'=16,'layer'=2] {'row_1'}, dimensions={0} | all-to-all | bytes 4194304 | tf_op jit(solution)/shard_map/all_to_all | solution.py:13
  254.4 1.5 copy.19
  255.9 2.9 copy.18
  258.8 4.8 %fusion.3 = f32[2,128,256]{2,1,0:T(8,128)} fusion(f32[2,128,2048]{2,1,0:T(8,128)} %bitcast.35, f32[2048,256,1]{1,0,2:T(8,128)} %bitcast.34), kind=kOutput, calls=%fused_computation.14 | convolution fusion | flops 1610612736 | bytes 4456448 | tf_op jit(solution)/shard_map/dot_general | solution.py:72
  263.6 5.3 %all-to-all-start.5 = ((f32[2,128,256]{2,1,0:T(8,128)}), f32[2,128,256]{2,1,0:T(8,128)S(1)}, u32[]{:S(2)}, u32[]{:S(2)}) async-start(f32[2,128,256]{2,1,0:T(8,128)} %fusion.3), calls=%async_computation.6 | async-start | bytes 524288 | tf_op jit(solution)/shard_map/all_to_all | solution.py:50
  269.9 15.6 %all-to-all-done.5 = f32[2,128,256]{2,1,0:T(8,128)S(1)} async-done(((f32[2,128,256]{2,1,0:T(8,128)}), f32[2,128,256]{2,1,0:T(8,128)S(1)}, u32[]{:S(2)}, u32[]{:S(2)}) %all-to-all-start.5) | async-done | bytes 262176 | tf_op jit(solution)/shard_map/all_to_all | solution.py:50
  286.8 7.8 %all-to-all-start.6 = ((f32[8,128,256]{1,2,0:T(8,128)}), f32[8,128,256]{1,2,0:T(8,128)S(1)}, u32[]{:S(2)}, u32[]{:S(2)}) async-start(f32[8,128,256]{1,2,0:T(8,128)} %broadcast_in_dim.40), calls=%async_computation.7 | async-start | bytes 2097152 | tf_op jit(solution)/shard_map/all_to_all | solution.py:13
  294.6 12.3 %reduce-scatter.5.cloned.1.call-done = f32[16,2048]{1,0:T(8,128)} async-done(((f32[256,2048]{1,0:T(8,128)}), f32[16,2048]{1,0:T(8,128)}) %reduce-scatter.5.cloned.1.call-update) | async-done | bytes 131088 | tf_op jit(solution)/shard_map/reduce_scatter | solution.py:38
  307.0 2.5 copy.14
  309.5 1.7 reshape.105
  311.2 39.8 %all-to-all-done.6 = f32[8,128,256]{1,2,0:T(8,128)S(1)} async-done(((f32[8,128,256]{1,2,0:T(8,128)}), f32[8,128,256]{1,2,0:T(8,128)S(1)}, u32[]{:S(2)}, u32[]{:S(2)}) %all-to-all-start.6) | async-done | bytes 1048608 | tf_op jit(solution)/shard_map/all_to_all | solution.py:13
  351.7 6.3 %all_to_all.57 = f32[2,8,128,256]{2,1,3,0:T(8,128)} all-to-all(f32[2,8,128,256]{2,1,3,0:T(8,128)S(1)} %broadcast_in_dim.41), channel_id=1, replica_groups=mesh['row_0'=8,'row_1'=2,'col'=16,'layer'=2] {'row_1'}, dimensions={0} | all-to-all | bytes 4194304 | tf_op jit(solution)/shard_map/all_to_all | solution.py:13
  358.0 2.9 copy.22
  361.0 2.9 copy.23
  363.9 3.5 convolution_bitcast_fusion
  367.3 20.6 %all_to_all.58 = f32[2,256,128]{2,1,0:T(8,128)S(1)} all-to-all(f32[2,256,128]{2,1,0:T(8,128)S(1)} %convolution_bitcast_fusion), channel_id=1, replica_groups=mesh['row_0'=8,'row_1'=2,'col'=16,'layer'=2] {'layer'}, dimensions={0} | all-to-all | bytes 524288 | tf_op jit(solution)/shard_map/all_to_all | solution.py:50
  388.1 34.0 %all_to_all.59 = f32[16,256,128]{2,1,0:T(8,128)S(1)} all-to-all(f32[16,256,128]{2,1,0:T(8,128)S(1)} %broadcast_in_dim.42), channel_id=1, replica_groups=mesh['row_0'=8,'row_1'=2,'col'=16,'layer'=2] {'col'}, dimensions={0} | all-to-all | bytes 4194304 | tf_op jit(solution)/shard_map/all_to_all | solution.py:13
  422.2 2.5 copy.24
  424.7 1.7 dot_general.25
  426.5 3.5 fusion
  429.9 22.6 %all_to_all.60 = f32[2,128,256]{2,1,0:T(8,128)S(1)} all-to-all(f32[2,128,256]{2,1,0:T(8,128)S(1)} %fusion), channel_id=1, replica_groups=mesh['row_0'=8,'row_1'=2,'col'=16,'layer'=2] {'layer'}, dimensions={0} | all-to-all | bytes 524288 | tf_op jit(solution)/shard_map/all_to_all | solution.py:50
  (43 shorter events, 8.2 us)
Async XLA Ops:
  7.4 1.0 copy-start
  9.5 63.7 %all-to-all-start.1 = ((f32[8,128,256]{1,2,0:T(8,128)}), f32[8,128,256]{1,2,0:T(8,128)S(1)}, u32[]{:S(2)}, u32[]{:S(2)}) async-start(f32[8,128,256]{1,2,0:T(8,128)} %broadcast_in_dim.34), calls=%async_computation.1 | async-start | bytes 2097152 | tf_op jit(solution)/shard_map/all_to_all | solution.py:13
  22.0 158.9 %reduce-scatter.3.cloned.1.call-start = ((), (), s32[]{:S(2)}) async-start(), calls=%async_computation.13 | async-start | bytes 2228224 | tf_op jit(solution)/shard_map/reduce_scatter | solution.py:38
  85.3 95.6 %copy-start.1 = (f32[256,256]{1,0:T(8,128)S(1)}, f32[256,256]{1,0:T(8,128)}, u32[]{:S(2)}) copy-start(f32[256,256]{1,0:T(8,128)} %param.6) | copy-start | bytes 786436
  85.3 95.6 %all-to-all-start = ((f32[16,256,128]{2,1,0:T(8,128)}), f32[16,256,128]{2,1,0:T(8,128)S(1)}, u32[]{:S(2)}, u32[]{:S(2)}) async-start(f32[16,256,128]{2,1,0:T(8,128)} %broadcast_in_dim.32), calls=%async_computation | async-start | bytes 4194304 | tf_op jit(solution)/shard_map/all_to_all | solution.py:13
  93.0 162.9 %all-gather.3.cloned.1.call-start = ((), (), s32[]{:S(2)}) async-start(), calls=%async_computation.14 | async-start | bytes 2228224 | tf_op jit(solution)/shard_map/all_gather | solution.py:39
  182.0 66.7 %all-to-all-start.3 = ((f32[8,128,256]{2,1,0:T(8,128)}), f32[8,128,256]{2,1,0:T(8,128)S(1)}, u32[]{:S(2)}, u32[]{:S(2)}) async-start(f32[8,128,256]{2,1,0:T(8,128)} %broadcast_in_dim.37), calls=%async_computation.4 | async-start | bytes 2097152 | tf_op jit(solution)/shard_map/all_to_all | solution.py:13
  192.0 114.9 %reduce-scatter.5.cloned.1.call-start = ((), (), s32[]{:S(2)}) async-start(), calls=%async_computation.15 | async-start | bytes 2228224 | tf_op jit(solution)/shard_map/reduce_scatter | solution.py:38
  258.8 10.9 %copy-start.2 = (s32[4096]{0:T(1024)S(1)}, s32[4096]{0:T(1024)}, u32[]{:S(2)}) copy-start(s32[4096]{0:T(1024)} %param.9) | copy-start | bytes 49156
  258.8 10.9 %copy-start.3 = (s32[4096]{0:T(1024)S(1)}, s32[4096]{0:T(1024)}, u32[]{:S(2)}) copy-start(s32[4096]{0:T(1024)} %param.8) | copy-start | bytes 49156
  263.6 21.9 %all-to-all-start.5 = ((f32[2,128,256]{2,1,0:T(8,128)}), f32[2,128,256]{2,1,0:T(8,128)S(1)}, u32[]{:S(2)}, u32[]{:S(2)}) async-start(f32[2,128,256]{2,1,0:T(8,128)} %fusion.3), calls=%async_computation.6 | async-start | bytes 524288 | tf_op jit(solution)/shard_map/all_to_all | solution.py:50
  286.8 64.2 %all-to-all-start.6 = ((f32[8,128,256]{1,2,0:T(8,128)}), f32[8,128,256]{1,2,0:T(8,128)S(1)}, u32[]{:S(2)}, u32[]{:S(2)}) async-start(f32[8,128,256]{1,2,0:T(8,128)} %broadcast_in_dim.40), calls=%async_computation.7 | async-start | bytes 2097152 | tf_op jit(solution)/shard_map/all_to_all | solution.py:13
  294.6 131.9 %all-gather.5.cloned.1.call-start = ((), (), s32[]{:S(2)}) async-start(), calls=%async_computation.16 | async-start | bytes 2228224 | tf_op jit(solution)/shard_map/all_gather | solution.py:39
Sparse Core Ops, SparseCore 0:
  83.9 96.9 reduce-scatter.2
  184.4 59.6 all-gather.2
Sparse Core Ops, SparseCore 1:
  195.5 111.3 reduce-scatter.4
  309.1 103.2 all-gather.4
where the time goes:
time: 461 us
  waiting for transfers between devices  262 us (57%)
  blocking collectives  95.2 us (21%)
  starting transfers between devices  43.4 us (9%)
  local copies, waits for them, and re-layouts  29.3 us (6%)
  between operations  15 us (3%)
  matrix products  11.7 us (3%)
    all_to_all x4, waiting for transfers between devices, sent_to_all(): lax.all_to_all(jnp.broadcast_to(x[None], (peers, *x.shape)), axis, 0, 0,...  146 us
    reduce_scatter x2, waiting for transfers between devices, from_root(): own = lax.psum_scatter(padded, axis, scatter_dimension=0, tiled=True)  100 us
    all_to_all x4, blocking collectives, sent_to_all(): lax.all_to_all(jnp.broadcast_to(x[None], (peers, *x.shape)), axis, 0, 0,...  52 us
    all_to_all x2, blocking collectives, summed_on_arrival(): lax.all_to_all(pieces, axis, split_axis=0, concat_axis=0, tiled=True)  43.2 us
    all_to_all x4, starting transfers between devices, sent_to_all(): lax.all_to_all(jnp.broadcast_to(x[None], (peers, *x.shape)), axis, 0, 0,...  37.9 us
    all_to_all x1, waiting for transfers between devices, summed_on_arrival(): lax.all_to_all(pieces, axis, split_axis=0, concat_axis=0, tiled=True)  15.6 us
  transfers between devices with their start and end apart: 9, of which 6 were waited for; matrix products, arithmetic and copies ran while one was open for 8% of the time, Pallas kernels for 0%

commit v1 on v0

v1 whole, which is shorter than its diff:
```python
import jax
import jax.numpy as jnp
from jax import lax
from jax.sharding import Mesh
from jax.sharding import PartitionSpec as P

AXES = ("zl", "co", "y", "x", "zh")
SIZES = (8, 2, 4, 4, 2)
SHIFT = 3
PREC = lax.Precision.HIGH


def place(z, co, y, x):
    return (((z % 8 * 2 + co) * 4 + y) * 4 + x) * 2 + z // 8


def moved(v, target):
    pairs = [
        (place(z, co, y, x), place(*target(z, co, y, x)))
        for z in range(16)
        for co in range(2)
        for y in range(4)
        for x in range(4)
    ]
    return lax.ppermute(v, AXES, pairs)


def other_core(z, co, y, x):
    return z, 1 - co, y, x


def other_layer(z, co, y, x):
    return (z + 8) % 16, co, y, x


def along(distance):
    def target(z, co, y, x):
        at = (z - SHIFT * co) % 16
        return ((at ^ distance) + SHIFT * co) % 16, co, y, x

    return target


def sent_to_all(v, axis):
    peers = lax.axis_size(axis)
    return lax.all_to_all(jnp.broadcast_to(v[None], (peers, *v.shape)), axis, 0, 0, tiled=True)


def dot(a, b, contract):
    return lax.dot_general(
        a, b, (contract, ((), ())), precision=PREC, preferred_element_type=jnp.float32
    )


def part(v, which, length, dim=0):
    return lax.dynamic_slice_in_dim(v, which * length, length, dim)


def joined(own, other, bit, dim=0):
    return jnp.where(
        bit == 1,
        jnp.concatenate([other, own], dim),
        jnp.concatenate([own, other], dim),
    )


def on_device(basis, basis_grad, value_grad, ranks, offsets):
    n = basis.shape[0]
    quarter = n // 4
    zl, co, y, x, zh = (lax.axis_index(a) for a in AXES)
    z = zh * 8 + zl
    at = (z - SHIFT * co) % 16
    spot = at % 8
    group = at // 8
    group_other = ((z - SHIFT * (1 - co)) % 16) // 8
    bits = [spot % 2, spot // 2 % 2, spot // 4]
    mine = 2 * co + group
    theirs = 2 * (1 - co) + group_other

    turned = jnp.stack([basis_grad.T, basis.T])
    own = part(turned, mine, quarter, 1)
    other = moved(part(turned, theirs, quarter, 1), other_core)
    both = joined(own[:, None], other[:, None], co, 1)

    wide = sent_to_all(basis, "x")
    grads = sent_to_all(both[0], "y")
    wide_other = moved(wide, other_core)

    far = both[1][None]
    for distance, bit in ((4, bits[2]), (2, bits[1]), (1, bits[0])):
        far_got = moved(far, along(distance))
        far = joined(far[:, None], far_got[:, None], bit, 1).reshape(-1, *far.shape[1:])
    far = jnp.where(co == 1, jnp.roll(far, SHIFT, 0), far)
    far = lax.all_to_all(far.reshape(4, 4, quarter, n), "y", 0, 0, tiled=True)
    far = far.swapaxes(0, 1).reshape(4, 4 * quarter, n)

    def grads_of(core):
        return lax.dynamic_index_in_dim(grads, core, 1, False).reshape(4 * quarter, n)

    def flat(w):
        return w.swapaxes(0, 1).reshape(n, 4 * n)

    wide_own = flat(wide)
    wide_oth = flat(wide_other)
    inner = dot(grads_of(co), wide_own, ((1,), (0,))) + dot(
        grads_of(1 - co), wide_oth, ((1,), (0,))
    )
    rows = 4 * quarter
    for distance, bit in ((1, bits[0]), (2, bits[1]), (4, bits[2])):
        rows //= 2
        got = moved(part(inner, 1 - bit, rows), along(distance))
        inner = part(inner, bit, rows) + got

    eigen = 4.0 * ranks.astype(jnp.float32) + offsets.astype(jnp.float32)

    def of_columns(v):
        v = part(part(v.reshape(4, 4, 4, quarter), x, 1, 1), mine, 1, 2).reshape(4 * quarter)
        return lax.dynamic_slice_in_dim(
            v, bits[0] * 8 * rows // 2 + bits[1] * 2 * rows + bits[2] * rows, rows, 0
        )

    index = jnp.arange(eigen.shape[0], dtype=jnp.int32)
    col_index = of_columns(index)
    col_eigen = of_columns(eigen)
    col_grad = of_columns(value_grad)
    row_index = part(index, y, 4 * n)
    row_eigen = part(eigen, y, 4 * n)
    on_diagonal = col_index[:, None] == row_index[None, :]
    spacing = col_eigen[:, None] - row_eigen[None, :]
    scaled = jnp.where(
        on_diagonal,
        col_grad[:, None],
        inner / jnp.where(on_diagonal, jnp.float32(1.0), spacing),
    )
    for distance, bit in ((4, bits[2]), (2, bits[1]), (1, bits[0])):
        got = moved(scaled, along(distance))
        scaled = joined(scaled, got, bit)

    left = joined(
        dot(wide_own, scaled, ((1,), (1,))), dot(wide_oth, scaled, ((1,), (1,))), co
    )
    left = lax.all_to_all(left.reshape(4, n // 2, n), "y", 0, 0, tiled=True).sum(0)
    left = sent_to_all(left, "y").reshape(2, n, n)

    def product(core):
        rows_of = lax.dynamic_index_in_dim(left, core, 0, False)
        return jnp.stack([dot(rows_of, far[i], ((1,), (0,))) for i in range(4)])

    theirs_out = moved(product(1 - co), other_core)
    out = product(co) + theirs_out
    out = lax.all_to_all(out, "x", 0, 0, tiled=True).sum(0)
    return part(out, zh, n // 2) + moved(part(out, 1 - zh, n // 2), other_layer)


def solution(mesh):
    torus = Mesh(mesh.devices.reshape(SIZES), AXES)
    return jax.shard_map(
        on_device,
        mesh=torus,
        in_specs=(P(("zl", "co"), ("y", "x")), P(("zl", "co"), ("y", "x")), P(), P(), P()),
        out_specs=P(("zl", "co", "zh"), ("y", "x")),
        check_vma=False,
    )
```

time: 461 us -> 243 us (0.53)
  the two profiles are of different devices: /device:TPU:2 before, /device:TPU:193 now
where the time goes in v1:
time: 243 us; the launch traced here: 242 us
  waiting for transfers between devices  142 us (58%)
  starting transfers between devices  76.1 us (31%)
  matrix products  8.49 us (3%)
  local copies, waits for them, and re-layouts  7.89 us (3%)
  other arithmetic  6.79 us (3%)
    ppermute x13, waiting for transfers between devices, moved(): return lax.ppermute(v, AXES, pairs)  84.6 us
    ppermute x13, starting transfers between devices, moved(): return lax.ppermute(v, AXES, pairs)  53.8 us
    all_to_all x3, waiting for transfers between devices, sent_to_all(): lax.all_to_all(jnp.broadcast_to(v[None], (peers, *v.shape)), axis, 0, 0,...  27.2 us
    all_to_all x1, waiting for transfers between devices, on_device(): out = lax.all_to_all(out, 'x', 0, 0, tiled=True).sum(0)  14.8 us
    all_to_all x3, starting transfers between devices, sent_to_all(): lax.all_to_all(jnp.broadcast_to(v[None], (peers, *v.shape)), axis, 0, 0,...  11.8 us
    all_to_all x1, waiting for transfers between devices, on_device(): far = lax.all_to_all(far.reshape(4, 4, quarter, n), 'y', 0, 0, tiled=True)  9.66 us
    dot_general x12, matrix products, dot(): lax.dot_general(a, b, (contract, ((), ())), precision=PREC, preferred_ele...  8.49 us
    all_to_all x1, waiting for transfers between devices, on_device(): lax.all_to_all(left.reshape(4, n // 2, n), 'y', 0, 0, tiled=True).sum(0)  5.63 us
  transfers between devices with their start and end apart: 19, of which 16 were waited for; matrix products, arithmetic and copies ran while one was open for 3% of the time, Pallas kernels for 0%

profile of v1, /device:TPU:193, one launch (start us, length us, event | category | flops | bytes accessed | tf_op | source)
XLA Modules:
  0.0 241.9 jit_solution(1881863384213175915)
XLA Ops:
  2.2 4.1 %all-to-all-start.1 = ((f32[4,256,256]{1,2,0:T(8,128)}), f32[4,256,256]{1,2,0:T(8,128)S(1)}, u32[]{:S(2)}, u32[]{:S(2)}) async-start(f32[4,256,256]{1,2,0:T(8,128)} %broadcast_in_dim.54), calls=%async_computation.1 | async-start | bytes 2097152 | tf_op jit(solution)/shard_map/all_to_all | solution.py:46
  6.5 2.9 %collective-permute-start = (f32[2,64,256]{1,2,0:T(8,128)S(1)}, f32[2,64,256]{1,2,0:T(8,128)S(1)}, u32[]{:S(2)}, u32[]{:S(2)}) collective-permute-start(f32[2,64,256]{1,2,0:T(8,128)S(1)} %get-tuple-element.14), channel_id=1, source_target_pairs={{0,32},{2,34},{4,36},{6,38},{8,40},{10,42},{12,44},{14,46},{16,48}... | collective-permute-start | bytes 393224 | tf_op jit(solution)/shard_map/ppermute | solution.py:25
  9.4 11.1 %all-to-all-done.1 = f32[4,256,256]{1,2,0:T(8,128)S(1)} async-done(((f32[4,256,256]{1,2,0:T(8,128)}), f32[4,256,256]{1,2,0:T(8,128)S(1)}, u32[]{:S(2)}, u32[]{:S(2)}) %all-to-all-start.1) | async-done | bytes 1048608 | tf_op jit(solution)/shard_map/all_to_all | solution.py:46
  20.5 3.8 %collective-permute-start.1 = (f32[4,256,256]{1,2,0:T(8,128)S(1)}, f32[4,256,256]{1,2,0:T(8,128)S(1)}, u32[]{:S(2)}, u32[]{:S(2)}) collective-permute-start(f32[4,256,256]{1,2,0:T(8,128)S(1)} %all-to-all-done.1), channel_id=1, source_target_pairs={{0,32},{2,34},{4,36},{6,38},{8,40},{10,42},{12,44},{14,46},{16,48}... | collective-permute-start | bytes 3145736 | tf_op jit(solution)/shard_map/ppermute | solution.py:25
  26.1 4.2 %all-to-all-start = ((f32[4,2,64,256]{3,2,1,0:T(8,128)}), f32[4,2,64,256]{3,2,1,0:T(8,128)S(1)}, u32[]{:S(2)}, u32[]{:S(2)}) async-start(f32[4,2,64,256]{3,2,1,0:T(8,128)} %broadcast_in_dim.53), calls=%async_computation | async-start | bytes 1048576 | tf_op jit(solution)/shard_map/all_to_all | solution.py:46
  30.3 9.3 %all-to-all-done = f32[4,2,64,256]{3,2,1,0:T(8,128)S(1)} async-done(((f32[4,2,64,256]{3,2,1,0:T(8,128)}), f32[4,2,64,256]{3,2,1,0:T(8,128)S(1)}, u32[]{:S(2)}, u32[]{:S(2)}) %all-to-all-start) | async-done | bytes 524320 | tf_op jit(solution)/shard_map/all_to_all | solution.py:46
  44.1 8.4 %collective-permute-done.2 = f32[128,1024]{1,0:T(8,128)S(1)} collective-permute-done((f32[128,1024]{1,0:T(8,128)}, f32[128,1024]{1,0:T(8,128)S(1)}, u32[]{:S(2)}, u32[]{:S(2)}) %collective-permute-start.2) | collective-permute-done | bytes 524320 | tf_op jit(solution)/shard_map/ppermute | solution.py:25
  52.7 2.2 collective-permute-start.3
  54.9 10.6 %collective-permute-done.3 = f32[64,1024]{1,0:T(8,128)S(1)} collective-permute-done((f32[64,1024]{1,0:T(8,128)S(1)}, f32[64,1024]{1,0:T(8,128)S(1)}, u32[]{:S(2)}, u32[]{:S(2)}) %collective-permute-start.3) | collective-permute-done | bytes 262176 | tf_op jit(solution)/shard_map/ppermute | solution.py:25
  65.6 6.4 %collective-permute-start.4 = (f32[32,1024]{1,0:T(8,128)S(1)}, f32[32,1024]{1,0:T(8,128)S(1)}, u32[]{:S(2)}, u32[]{:S(2)}) collective-permute-start(f32[32,1024]{1,0:T(8,128)S(1)} %constant_dynamic-slice_fusion.1), channel_id=1, source_target_pairs={{0,256},{2,258},{4,260},{6,262},{8,264},{10,266},{12,268},{14,270}... | collective-permute-start | bytes 393224 | tf_op jit(solution)/shard_map/ppermute | solution.py:25
  73.5 2.9 %collective-permute-start.8 = (f32[1,2,64,256]{2,3,1,0:T(8,128)S(1)}, f32[1,2,64,256]{2,3,1,0:T(8,128)S(1)}, u32[]{:S(2)}, u32[]{:S(2)}) collective-permute-start(f32[1,2,64,256]{2,3,1,0:T(8,128)S(1)} %copy-done.3), channel_id=1, source_target_pairs={{0,256},{2,258},{4,260},{6,262},{8,264},{10,266},{12,268},{14,270}... | collective-permute-start | bytes 393224 | tf_op jit(solution)/shard_map/ppermute | solution.py:25
  76.5 7.8 %collective-permute-start.5 = (f32[32,1024]{1,0:T(8,128)S(1)}, f32[32,1024]{1,0:T(8,128)S(1)}, u32[]{:S(2)}, u32[]{:S(2)}) collective-permute-start(f32[32,1024]{1,0:T(8,128)S(1)} %compare_select_fusion), channel_id=1, source_target_pairs={{0,256},{2,258},{4,260},{6,262},{8,264},{10,266},{12,268},{14,270}... | collective-permute-start | bytes 393224 | tf_op jit(solution)/shard_map/ppermute | solution.py:25
  84.3 7.6 %collective-permute-done.8 = f32[1,2,64,256]{2,3,1,0:T(8,128)S(1)} collective-permute-done((f32[1,2,64,256]{2,3,1,0:T(8,128)S(1)}, f32[1,2,64,256]{2,3,1,0:T(8,128)S(1)}, u32[]{:S(2)}, u32[]{:S(2)}) %collective-permute-start.8) | collective-permute-done | bytes 131104 | tf_op jit(solution)/shard_map/ppermute | solution.py:25
  95.3 3.0 %collective-permute-start.6 = (f32[64,1024]{1,0:T(8,128)S(1)}, f32[64,1024]{1,0:T(8,128)}, u32[]{:S(2)}, u32[]{:S(2)}) collective-permute-start(f32[64,1024]{1,0:T(8,128)S(1)} %maximum_select_fusion.10), channel_id=1, source_target_pairs={{0,128},{2,130},{4,132},{6,134},{8,136},{10,138},{12,140},{14,142}... | collective-permute-start | bytes 786440 | tf_op jit(solution)/shard_map/ppermute | solution.py:25
  98.3 24.4 %collective-permute-done.9 = f32[2,2,64,256]{2,3,1,0:T(8,128)S(1)} collective-permute-done((f32[2,2,64,256]{2,3,1,0:T(8,128)S(1)}, f32[2,2,64,256]{2,3,1,0:T(8,128)S(1)}, u32[]{:S(2)}, u32[]{:S(2)}) %collective-permute-start.9) | collective-permute-done | bytes 262176 | tf_op jit(solution)/shard_map/ppermute | solution.py:25
  123.1 1.9 collective-permute-start.10
  125.0 3.4 %collective-permute-done.6 = f32[64,1024]{1,0:T(8,128)} collective-permute-done((f32[64,1024]{1,0:T(8,128)S(1)}, f32[64,1024]{1,0:T(8,128)}, u32[]{:S(2)}, u32[]{:S(2)}) %collective-permute-start.6) | collective-permute-done | bytes 262176 | tf_op jit(solution)/shard_map/ppermute | solution.py:25
  132.3 5.4 %collective-permute-done.10 = f32[4,2,64,256]{3,2,1,0:T(8,128)S(1)} collective-permute-done((f32[4,2,64,256]{3,2,1,0:T(8,128)S(1)}, f32[4,2,64,256]{3,2,1,0:T(8,128)S(1)}, u32[]{:S(2)}, u32[]{:S(2)}) %collective-permute-start.10) | collective-permute-done | bytes 524320 | tf_op jit(solution)/shard_map/ppermute | solution.py:25
  137.8 5.5 %collective-permute-done.7 = f32[128,1024]{1,0:T(8,128)} collective-permute-done((f32[128,1024]{1,0:T(8,128)}, f32[128,1024]{1,0:T(8,128)}, u32[]{:S(2)}, u32[]{:S(2)}) %collective-permute-start.7) | collective-permute-done | bytes 524320 | tf_op jit(solution)/shard_map/ppermute | solution.py:25
  143.4 2.6 %convolution_bitcast_fusion.9 = f32[256,256]{1,0:T(8,128)S(1)} fusion(f32[256,1024]{0,1:T(8,128)S(1)} %bitcast.122, f32[128,1024]{1,0:T(8,128)} %maximum_select_fusion.6, f32[128,1024]{1,0:T(8,128)} %collective-permute-done.7, pred[]{:T(512)S(6)} %eq.37), kind=kOutput, calls=%fused_computation.10 | convolution fusion | flops 403439616 | bytes 2359297 | tf_op jit(solution)/shard_map/dot_general | solution.py:50
  145.9 2.5 %convolution_bitcast_fusion.8 = f32[256,256]{1,0:T(8,128)S(1)} fusion(f32[256,1024]{0,1:T(8,128)S(1)} %bitcast.106, f32[128,1024]{1,0:T(8,128)} %maximum_select_fusion.6, f32[128,1024]{1,0:T(8,128)} %collective-permute-done.7, pred[]{:T(512)S(6)} %eq.37), kind=kOutput, calls=%fused_computation.9 | convolution fusion | flops 403439616 | bytes 2359297 | tf_op jit(solution)/shard_map/dot_general | solution.py:50
  149.3 3.5 %all-to-all-start.2 = ((f32[4,128,256]{2,1,0:T(8,128)}), f32[4,128,256]{2,1,0:T(8,128)S(1)}, u32[]{:S(2)}, u32[]{:S(2)}) async-start(f32[4,128,256]{2,1,0:T(8,128)} %bitcast.16), calls=%async_computation.2 | async-start | bytes 1048576 | tf_op jit(solution)/shard_map/all_to_all | solution.py:142
  154.1 5.6 %all-to-all-done.2 = f32[4,128,256]{2,1,0:T(8,128)S(1)} async-done(((f32[4,128,256]{2,1,0:T(8,128)}), f32[4,128,256]{2,1,0:T(8,128)S(1)}, u32[]{:S(2)}, u32[]{:S(2)}) %all-to-all-start.2) | async-done | bytes 524320 | tf_op jit(solution)/shard_map/all_to_all | solution.py:142
  159.7 3.5 %all-to-all-start.4 = ((f32[4,4,64,256]{3,2,1,0:T(8,128)}), f32[4,4,64,256]{3,2,1,0:T(8,128)S(1)}, u32[]{:S(2)}, u32[]{:S(2)}) async-start(f32[4,4,64,256]{3,2,1,0:T(8,128)} %bitcast_select_fusion), calls=%async_computation.4 | async-start | bytes 2097152 | tf_op jit(solution)/shard_map/all_to_all | solution.py:94
  163.3 9.7 %all-to-all-done.4 = f32[4,4,64,256]{3,2,1,0:T(8,128)S(1)} async-done(((f32[4,4,64,256]{3,2,1,0:T(8,128)}), f32[4,4,64,256]{3,2,1,0:T(8,128)S(1)}, u32[]{:S(2)}, u32[]{:S(2)}) %all-to-all-start.4) | async-done | bytes 1048608 | tf_op jit(solution)/shard_map/all_to_all | solution.py:94
  173.8 3.5 %all-to-all-start.3 = ((f32[4,128,256]{2,1,0:T(8,128)}), f32[4,128,256]{2,1,0:T(8,128)S(1)}, u32[]{:S(2)}, u32[]{:S(2)}) async-start(f32[4,128,256]{2,1,0:T(8,128)} %broadcast_in_dim.56), calls=%async_computation.3 | async-start | bytes 1048576 | tf_op jit(solution)/shard_map/all_to_all | solution.py:46
  177.4 6.8 %all-to-all-done.3 = f32[4,128,256]{2,1,0:T(8,128)S(1)} async-done(((f32[4,128,256]{2,1,0:T(8,128)}), f32[4,128,256]{2,1,0:T(8,128)S(1)}, u32[]{:S(2)}, u32[]{:S(2)}) %all-to-all-start.3) | async-done | bytes 524320 | tf_op jit(solution)/shard_map/all_to_all | solution.py:46
  185.3 10.8 %collective-permute-start.11 = (f32[4,256,256]{2,1,0:T(8,128)S(1)}, f32[4,256,256]{2,1,0:T(8,128)S(1)}, u32[]{:S(2)}, u32[]{:S(2)}) collective-permute-start(f32[4,256,256]{2,1,0:T(8,128)S(1)} %pad_maximum_fusion.1), channel_id=1, source_target_pairs={{0,32},{2,34},{4,36},{6,38},{8,40},{10,42},{12,44},{14,46},{16,48}... | collective-permute-start | bytes 3145736 | tf_op jit(solution)/shard_map/ppermute | solution.py:25
  199.6 3.5 %all-to-all-start.5 = ((f32[4,256,256]{2,1,0:T(8,128)}), f32[4,256,256]{2,1,0:T(8,128)S(1)}, u32[]{:S(2)}, u32[]{:S(2)}) async-start(f32[4,256,256]{2,1,0:T(8,128)} %maximum_add_fusion), calls=%async_computation.5 | async-start | bytes 2097152 | tf_op jit(solution)/shard_map/all_to_all | solution.py:151
  203.1 14.8 %all-to-all-done.5 = f32[4,256,256]{2,1,0:T(8,128)S(1)} async-done(((f32[4,256,256]{2,1,0:T(8,128)}), f32[4,256,256]{2,1,0:T(8,128)S(1)}, u32[]{:S(2)}, u32[]{:S(2)}) %all-to-all-start.5) | async-done | bytes 1048608 | tf_op jit(solution)/shard_map/all_to_all | solution.py:151
  218.0 6.5 %collective-permute-start.12 = (f32[128,256]{1,0:T(8,128)S(1)}, f32[128,256]{1,0:T(8,128)S(1)}, u32[]{:S(2)}, u32[]{:S(2)}) collective-permute-start(f32[128,256]{1,0:T(8,128)S(1)} %constant_dynamic-slice_fusion.7), channel_id=1, source_target_pairs={{0,1},{2,3},{4,5},{6,7},{8,9},{10,11},{12,13},{14,15},{16,17},{18,... | collective-permute-start | bytes 393224 | tf_op jit(solution)/shard_map/ppermute | solution.py:25
  224.5 16.7 %collective-permute-done.12 = f32[128,256]{1,0:T(8,128)S(1)} collective-permute-done((f32[128,256]{1,0:T(8,128)S(1)}, f32[128,256]{1,0:T(8,128)S(1)}, u32[]{:S(2)}, u32[]{:S(2)}) %collective-permute-start.12) | collective-permute-done | bytes 131104 | tf_op jit(solution)/shard_map/ppermute | solution.py:25
  (84 shorter events, 26.3 us)
Async XLA Ops:
  2.2 4.2 %copy-start = (f32[256,256]{1,0:T(8,128)S(1)}, f32[256,256]{1,0:T(8,128)}, u32[]{:S(2)}) copy-start(f32[256,256]{1,0:T(8,128)} %param.5) | copy-start | bytes 786436
  2.2 4.2 %copy-start.4 = (f32[256,256]{1,0:T(8,128)S(1)}, f32[256,256]{1,0:T(8,128)}, u32[]{:S(2)}) copy-start(f32[256,256]{1,0:T(8,128)} %param.6) | copy-start | bytes 786436
  2.2 18.3 %all-to-all-start.1 = ((f32[4,256,256]{1,2,0:T(8,128)}), f32[4,256,256]{1,2,0:T(8,128)S(1)}, u32[]{:S(2)}, u32[]{:S(2)}) async-start(f32[4,256,256]{1,2,0:T(8,128)} %broadcast_in_dim.54), calls=%async_computation.1 | async-start | bytes 2097152 | tf_op jit(solution)/shard_map/all_to_all | solution.py:46
  6.5 17.7 %collective-permute-start = (f32[2,64,256]{1,2,0:T(8,128)S(1)}, f32[2,64,256]{1,2,0:T(8,128)S(1)}, u32[]{:S(2)}, u32[]{:S(2)}) collective-permute-start(f32[2,64,256]{1,2,0:T(8,128)S(1)} %get-tuple-element.14), channel_id=1, source_target_pairs={{0,32},{2,34},{4,36},{6,38},{8,40},{10,42},{12,44},{14,46},{16,48}... | collective-permute-start | bytes 393224 | tf_op jit(solution)/shard_map/ppermute | solution.py:25
  20.5 19.7 %collective-permute-start.1 = (f32[4,256,256]{1,2,0:T(8,128)S(1)}, f32[4,256,256]{1,2,0:T(8,128)S(1)}, u32[]{:S(2)}, u32[]{:S(2)}) collective-permute-start(f32[4,256,256]{1,2,0:T(8,128)S(1)} %all-to-all-done.1), channel_id=1, source_target_pairs={{0,32},{2,34},{4,36},{6,38},{8,40},{10,42},{12,44},{14,46},{16,48}... | collective-permute-start | bytes 3145736 | tf_op jit(solution)/shard_map/ppermute | solution.py:25
  26.1 13.5 %all-to-all-start = ((f32[4,2,64,256]{3,2,1,0:T(8,128)}), f32[4,2,64,256]{3,2,1,0:T(8,128)S(1)}, u32[]{:S(2)}, u32[]{:S(2)}) async-start(f32[4,2,64,256]{3,2,1,0:T(8,128)} %broadcast_in_dim.53), calls=%async_computation | async-start | bytes 1048576 | tf_op jit(solution)/shard_map/all_to_all | solution.py:46
  40.3 1.0 copy-start.1
  42.1 10.4 %collective-permute-start.2 = (f32[128,1024]{1,0:T(8,128)}, f32[128,1024]{1,0:T(8,128)S(1)}, u32[]{:S(2)}, u32[]{:S(2)}) collective-permute-start(f32[128,1024]{1,0:T(8,128)} %constant_dynamic-slice_fusion.3), channel_id=1, source_target_pairs={{0,64},{2,66},{4,68},{6,70},{8,72},{10,74},{12,76},{14,78},{16,80}... | collective-permute-start | bytes 1572872 | tf_op jit(solution)/shard_map/ppermute | solution.py:25
  52.7 12.9 %collective-permute-start.3 = (f32[64,1024]{1,0:T(8,128)S(1)}, f32[64,1024]{1,0:T(8,128)S(1)}, u32[]{:S(2)}, u32[]{:S(2)}) collective-permute-start(f32[64,1024]{1,0:T(8,128)S(1)} %constant_dynamic-slice_fusion.2), channel_id=1, source_target_pairs={{0,128},{2,130},{4,132},{6,134},{8,136},{10,138},{12,140},{14,142}... | collective-permute-start | bytes 786440 | tf_op jit(solution)/shard_map/ppermute | solution.py:25
  65.5 6.5 %copy-start.6 = (s32[4096]{0:T(1024)S(1)}, s32[4096]{0:T(1024)}, u32[]{:S(2)}) copy-start(s32[4096]{0:T(1024)} %param.9) | copy-start | bytes 49156
  65.5 6.5 %copy-start.7 = (s32[4096]{0:T(1024)S(1)}, s32[4096]{0:T(1024)}, u32[]{:S(2)}) copy-start(s32[4096]{0:T(1024)} %param.8) | copy-start | bytes 49156
  65.6 7.9 %copy-start.3 = (f32[1,2,64,256]{2,3,1,0:T(8,128)S(1)}, f32[1,2,64,256]{2,3,1,0:T(8,128)}, u32[]{:S(2)}) copy-start(f32[1,2,64,256]{2,3,1,0:T(8,128)} %get-tuple-element.13) | copy-start | bytes 393220
  65.6 10.8 %collective-permute-start.4 = (f32[32,1024]{1,0:T(8,128)S(1)}, f32[32,1024]{1,0:T(8,128)S(1)}, u32[]{:S(2)}, u32[]{:S(2)}) collective-permute-start(f32[32,1024]{1,0:T(8,128)S(1)} %constant_dynamic-slice_fusion.1), channel_id=1, source_target_pairs={{0,256},{2,258},{4,260},{6,262},{8,264},{10,266},{12,268},{14,270}... | collective-permute-start | bytes 393224 | tf_op jit(solution)/shard_map/ppermute | solution.py:25
  72.1 1.4 copy-start.5
  72.3 0.7 copy-start.8
  73.5 2.9 %dynamic-slice-start = ((f32[4096]{0:T(1024)}, s32[]{:T(128)}), f32[1024]{0:T(1024)S(1)}, s32[]{:S(2)}) async-start(f32[4096]{0:T(1024)} %copy-done.5, s32[]{:T(128)} %select_n.242), calls=%async_computation.6 | async-start | bytes 8704 | tf_op jit(solution)/shard_map/dynamic_slice | solution.py:56
  73.5 18.4 %collective-permute-start.8 = (f32[1,2,64,256]{2,3,1,0:T(8,128)S(1)}, f32[1,2,64,256]{2,3,1,0:T(8,128)S(1)}, u32[]{:S(2)}, u32[]{:S(2)}) collective-permute-start(f32[1,2,64,256]{2,3,1,0:T(8,128)S(1)} %copy-done.3), channel_id=1, source_target_pairs={{0,256},{2,258},{4,260},{6,262},{8,264},{10,266},{12,268},{14,270}... | collective-permute-start | bytes 393224 | tf_op jit(solution)/shard_map/ppermute | solution.py:25
  76.5 18.7 %collective-permute-start.5 = (f32[32,1024]{1,0:T(8,128)S(1)}, f32[32,1024]{1,0:T(8,128)S(1)}, u32[]{:S(2)}, u32[]{:S(2)}) collective-permute-start(f32[32,1024]{1,0:T(8,128)S(1)} %compare_select_fusion), channel_id=1, source_target_pairs={{0,256},{2,258},{4,260},{6,262},{8,264},{10,266},{12,268},{14,270}... | collective-permute-start | bytes 393224 | tf_op jit(solution)/shard_map/ppermute | solution.py:25
  92.0 30.7 %collective-permute-start.9 = (f32[2,2,64,256]{2,3,1,0:T(8,128)S(1)}, f32[2,2,64,256]{2,3,1,0:T(8,128)S(1)}, u32[]{:S(2)}, u32[]{:S(2)}) collective-permute-start(f32[2,2,64,256]{2,3,1,0:T(8,128)S(1)} %maximum_select_fusion.8), channel_id=1, source_target_pairs={{0,128},{2,130},{4,132},{6,134},{8,136},{10,138},{12,140},{14,142}... | collective-permute-start | bytes 786440 | tf_op jit(solution)/shard_map/ppermute | solution.py:25
  95.3 33.2 %collective-permute-start.6 = (f32[64,1024]{1,0:T(8,128)S(1)}, f32[64,1024]{1,0:T(8,128)}, u32[]{:S(2)}, u32[]{:S(2)}) collective-permute-start(f32[64,1024]{1,0:T(8,128)S(1)} %maximum_select_fusion.10), channel_id=1, source_target_pairs={{0,128},{2,130},{4,132},{6,134},{8,136},{10,138},{12,140},{14,142}... | collective-permute-start | bytes 786440 | tf_op jit(solution)/shard_map/ppermute | solution.py:25
  123.1 14.5 %collective-permute-start.10 = (f32[4,2,64,256]{3,2,1,0:T(8,128)S(1)}, f32[4,2,64,256]{3,2,1,0:T(8,128)S(1)}, u32[]{:S(2)}, u32[]{:S(2)}) collective-permute-start(f32[4,2,64,256]{3,2,1,0:T(8,128)S(1)} %bitcast.117), channel_id=1, source_target_pairs={{0,64},{2,66},{4,68},{6,70},{8,72},{10,74},{12,76},{14,78},{16,80}... | collective-permute-start | bytes 1572872 | tf_op jit(solution)/shard_map/ppermute | solution.py:25
  130.3 13.0 %collective-permute-start.7 = (f32[128,1024]{1,0:T(8,128)}, f32[128,1024]{1,0:T(8,128)}, u32[]{:S(2)}, u32[]{:S(2)}) collective-permute-start(f32[128,1024]{1,0:T(8,128)} %maximum_select_fusion.6), channel_id=1, source_target_pairs={{0,64},{2,66},{4,68},{6,70},{8,72},{10,74},{12,76},{14,78},{16,80}... | collective-permute-start | bytes 1572872 | tf_op jit(solution)/shard_map/ppermute | solution.py:25
  137.7 5.6 %copy-start.2 = (f32[4,256,256]{1,2,0:T(8,128)S(1)}, f32[4,256,256]{1,2,0:T(8,128)}, u32[]{:S(2)}) copy-start(f32[4,256,256]{1,2,0:T(8,128)} %copy-done.1) | copy-start | bytes 3145732
  149.3 10.4 %all-to-all-start.2 = ((f32[4,128,256]{2,1,0:T(8,128)}), f32[4,128,256]{2,1,0:T(8,128)S(1)}, u32[]{:S(2)}, u32[]{:S(2)}) async-start(f32[4,128,256]{2,1,0:T(8,128)} %bitcast.16), calls=%async_computation.2 | async-start | bytes 1048576 | tf_op jit(solution)/shard_map/all_to_all | solution.py:142
  159.7 13.2 %all-to-all-start.4 = ((f32[4,4,64,256]{3,2,1,0:T(8,128)}), f32[4,4,64,256]{3,2,1,0:T(8,128)S(1)}, u32[]{:S(2)}, u32[]{:S(2)}) async-start(f32[4,4,64,256]{3,2,1,0:T(8,128)} %bitcast_select_fusion), calls=%async_computation.4 | async-start | bytes 2097152 | tf_op jit(solution)/shard_map/all_to_all | solution.py:94
  173.8 10.4 %all-to-all-start.3 = ((f32[4,128,256]{2,1,0:T(8,128)}), f32[4,128,256]{2,1,0:T(8,128)S(1)}, u32[]{:S(2)}, u32[]{:S(2)}) async-start(f32[4,128,256]{2,1,0:T(8,128)} %broadcast_in_dim.56), calls=%async_computation.3 | async-start | bytes 1048576 | tf_op jit(solution)/shard_map/all_to_all | solution.py:46
  185.3 13.1 %collective-permute-start.11 = (f32[4,256,256]{2,1,0:T(8,128)S(1)}, f32[4,256,256]{2,1,0:T(8,128)S(1)}, u32[]{:S(2)}, u32[]{:S(2)}) collective-permute-start(f32[4,256,256]{2,1,0:T(8,128)S(1)} %pad_maximum_fusion.1), channel_id=1, source_target_pairs={{0,32},{2,34},{4,36},{6,38},{8,40},{10,42},{12,44},{14,46},{16,48}... | collective-permute-start | bytes 3145736 | tf_op jit(solution)/shard_map/ppermute | solution.py:25
  199.6 18.3 %all-to-all-start.5 = ((f32[4,256,256]{2,1,0:T(8,128)}), f32[4,256,256]{2,1,0:T(8,128)S(1)}, u32[]{:S(2)}, u32[]{:S(2)}) async-start(f32[4,256,256]{2,1,0:T(8,128)} %maximum_add_fusion), calls=%async_computation.5 | async-start | bytes 2097152 | tf_op jit(solution)/shard_map/all_to_all | solution.py:151
  218.0 23.2 %collective-permute-start.12 = (f32[128,256]{1,0:T(8,128)S(1)}, f32[128,256]{1,0:T(8,128)S(1)}, u32[]{:S(2)}, u32[]{:S(2)}) collective-permute-start(f32[128,256]{1,0:T(8,128)S(1)} %constant_dynamic-slice_fusion.7), channel_id=1, source_target_pairs={{0,1},{2,3},{4,5},{6,7},{8,9},{10,11},{12,13},{14,15},{16,17},{18,... | collective-permute-start | bytes 393224 | tf_op jit(solution)/shard_map/ppermute | solution.py:25

commit v2 on v1

v2 whole, which is shorter than its diff:
```python
import jax
import jax.numpy as jnp
from jax import lax
from jax.sharding import Mesh
from jax.sharding import PartitionSpec as P

AXES = ("zl", "co", "y", "x", "zh")
SIZES = (8, 2, 4, 4, 2)
SHIFT = 3
PREC = lax.Precision.HIGH


def place(z, co, y, x):
    return (((z % 8 * 2 + co) * 4 + y) * 4 + x) * 2 + z // 8


def moved(v, target):
    pairs = [
        (place(z, co, y, x), place(*target(z, co, y, x)))
        for z in range(16)
        for co in range(2)
        for y in range(4)
        for x in range(4)
    ]
    return lax.ppermute(v, AXES, pairs)


def other_core(z, co, y, x):
    return z, 1 - co, y, x


def around(step):
    def target(z, co, y, x):
        return z, co, y, (x - step) % 4

    return target


def other_layer(z, co, y, x):
    return (z + 8) % 16, co, y, x


def along(distance):
    def target(z, co, y, x):
        at = (z - SHIFT * co) % 16
        return ((at ^ distance) + SHIFT * co) % 16, co, y, x

    return target


def to_all(v, axis):
    return lax.all_to_all(v, axis, 0, 0, tiled=True)


def sent_to_all(v, axis):
    peers = lax.axis_size(axis)
    return to_all(jnp.broadcast_to(v[None], (peers, *v.shape)), axis)


def dot(a, b, contract=((1,), (0,))):
    return lax.dot_general(
        a, b, (contract, ((), ())), precision=PREC, preferred_element_type=jnp.float32
    )


def tied(*values):
    return lax.optimization_barrier(values)


def part(v, which, length, dim=0):
    return lax.dynamic_slice_in_dim(v, which * length, length, dim)


def turned_round(v, first):
    return lax.dynamic_slice_in_dim(jnp.concatenate([v, v]), first, v.shape[0], 0)


def joined(own, other, bit, dim=0):
    return jnp.where(
        bit == 1,
        jnp.concatenate([other, own], dim),
        jnp.concatenate([own, other], dim),
    )


def on_device(basis, basis_grad, value_grad, ranks, offsets):
    n = basis.shape[0]
    quarter = n // 4
    half = n // 2
    zl, co, y, x, zh = (lax.axis_index(a) for a in AXES)
    z = zh * 8 + zl
    at = (z - SHIFT * co) % 16
    group = at // 8
    group_other = ((z - SHIFT * (1 - co)) % 16) // 8
    bits = [at % 2, at // 2 % 2, at // 4 % 2]
    mine = 2 * co + group
    theirs = 2 * (1 - co) + group_other

    turned = jnp.stack([basis_grad.T, basis.T])
    own = part(turned, mine, quarter, 1)
    other = moved(part(turned, theirs, quarter, 1), other_core)

    wide_own = jnp.stack([basis] + [moved(basis, around(r)) for r in (1, 3, 2)])
    wide_oth = moved(wide_own, other_core)
    slots = [0, 1, 3, 2]

    grads = sent_to_all(jnp.stack([own[0], other[0]]), "y")

    far = joined(own[1][None], other[1][None], co)[None]
    for distance, bit in ((4, bits[2]), (2, bits[1])):
        got = moved(far, along(distance))
        far = joined(far[:, None], got[:, None], bit, 1).reshape(-1, *far.shape[1:])
    wide_oth, far = tied(wide_oth, far)
    got = moved(far, along(1))
    far = joined(far[:, None], got[:, None], bits[0], 1).reshape(-1, *far.shape[1:])

    def flat(w):
        return w.swapaxes(0, 1).reshape(n, 4 * n)

    def inner_of(t):
        g = grads[2 * t : 2 * t + 2]
        return dot(g[:, 0].reshape(half, n), flat(wide_own)) + dot(
            g[:, 1].reshape(half, n), flat(wide_oth)
        )

    inner = [inner_of(t) for t in range(2)]
    rows = half
    for distance, bit in ((1, bits[0]), (2, bits[1]), (4, bits[2])):
        rows //= 2
        for t in range(2):
            got = moved(part(inner[t], 1 - bit, rows), along(distance))
            inner[t] = part(inner[t], bit, rows) + got
        if distance == 1:
            inner[0], far = tied(inner[0], far)
            far = jnp.where(co == 1, jnp.roll(far, SHIFT, 0), far)
            far = to_all(far.reshape(4, 4, quarter, n), "y")
            far = far.swapaxes(1, 2).reshape(4 * quarter, 4 * n)
            w = jnp.concatenate([wide_own, wide_oth], 1).reshape(4, 2, 2, half, n)
            w = jnp.where(zh == 0, w[:, :, ::-1], w)
            upright = w.reshape(4, 2 * n, n).swapaxes(1, 2).reshape(4 * n, 2 * n)

    eigen = 4.0 * ranks.astype(jnp.float32) + offsets.astype(jnp.float32)
    index = jnp.arange(eigen.shape[0], dtype=jnp.int32)

    def of_columns(v):
        return part(part(v.reshape(4, 4, 4, quarter), x, 1, 1), mine, 1, 2).reshape(4 * quarter)

    def of_rows(v):
        v = turned_round(part(v.reshape(4, 4, n), y, 1)[0], x)
        return jnp.stack([v[r] for r in slots]).reshape(4 * n)

    row_index, row_eigen = of_rows(index), of_rows(eigen)
    columns = [of_columns(v) for v in (index, eigen, value_grad)]
    scaled = []
    for t in range(2):
        begin = t * half + (bits[0] * 4 + bits[1] * 2 + bits[2]) * rows
        col_index, col_eigen, col_grad = (
            lax.dynamic_slice_in_dim(v, begin, rows, 0)[:, None] for v in columns
        )
        on_diagonal = col_index == row_index[None, :]
        spacing = jnp.where(on_diagonal, jnp.float32(1.0), col_eigen - row_eigen[None, :])
        scaled.append(jnp.where(on_diagonal, col_grad, inner[t] / spacing))
    scaled[0], far, upright = tied(scaled[0], far, upright)
    for distance, bit in ((4, bits[2]), (2, bits[1]), (1, bits[0])):
        for t in range(2):
            got = moved(scaled[t], along(distance))
            scaled[t] = joined(scaled[t], got, bit)

    left = []
    for t in range(2):
        term = dot(scaled[t], upright)
        term = to_all(term.reshape(4, half // 4, 2 * n), "y").sum(0)
        left.append(sent_to_all(term, "y").reshape(half, 2 * n))

    def product(block):
        at_block = slice(block * half, (block + 1) * half)
        out = sum(
            dot(left[t][:, at_block], far[t * half : (t + 1) * half], ((0,), (0,)))
            for t in range(2)
        )
        return out.reshape(half, 4, n).swapaxes(0, 1)

    def summed(v):
        return to_all(v, "x").sum(0)

    leaving = moved(product(2), other_core)
    staying = moved(product(3), other_core)
    leaving = moved(summed(product(0) + leaving), other_layer)
    return summed(product(1) + staying) + leaving


def solution(mesh):
    torus = Mesh(mesh.devices.reshape(SIZES), AXES)
    return jax.shard_map(
        on_device,
        mesh=torus,
        in_specs=(P(("zl", "co"), ("y", "x")), P(("zl", "co"), ("y", "x")), P(), P(), P()),
        out_specs=P(("zl", "co", "zh"), ("y", "x")),
        check_vma=False,
    )
```

time: 243 us -> 273 us (1.12)
  the two profiles are of different devices: /device:TPU:193 before, /device:TPU:98 now
where the time goes in v2:
time: 273 us; the launch traced here: 272 us
  starting transfers between devices  119 us (44%)
  waiting for transfers between devices  91 us (33%)
  local copies, waits for them, and re-layouts  30.4 us (11%)
  other arithmetic  20.4 us (7%)
  matrix products  10.1 us (4%)
    ppermute x23, starting transfers between devices, moved(): return lax.ppermute(v, AXES, pairs)  84.6 us
    ppermute x23, waiting for transfers between devices, moved(): return lax.ppermute(v, AXES, pairs)  58.7 us
    all_to_all x8, starting transfers between devices, to_all(): return lax.all_to_all(v, axis, 0, 0, tiled=True)  34.1 us
    all_to_all x8, waiting for transfers between devices, to_all(): return lax.all_to_all(v, axis, 0, 0, tiled=True)  32.4 us
    dot_general x14, matrix products, dot(): lax.dot_general(a, b, (contract, ((), ())), precision=PREC, preferred_ele...  10.1 us
    rev x1, local copies, waits for them, and re-layouts, on_device(): w = jnp.where(zh == 0, w[:, :, ::-1], w)  8.02 us
  transfers between devices with their start and end apart: 31, of which 16 were waited for; matrix products, arithmetic and copies ran while one was open for 19% of the time, Pallas kernels for 0%

profile of v2, /device:TPU:98, one launch (start us, length us, event | category | flops | bytes accessed | tf_op | source)
XLA Modules:
  0.0 271.7 jit_solution(15167057851737054081)
XLA Ops:
  1.1 4.0 %collective-permute-start.3 = (f32[256,256]{0,1:T(8,128)S(1)}, f32[256,256]{0,1:T(8,128)S(1)}, u32[]{:S(2)}, u32[]{:S(2)}) collective-permute-start(f32[256,256]{0,1:T(8,128)S(1)} %copy.15), channel_id=1, source_target_pairs={{0,4},{2,6},{4,0},{6,2},{8,12},{10,14},{12,8},{14,10},{16,20},{18,... | collective-permute-start | bytes 786440 | tf_op jit(solution)/shard_map/ppermute | solution.py:25
  7.1 3.9 %collective-permute-start.1 = (f32[256,256]{0,1:T(8,128)S(1)}, f32[256,256]{0,1:T(8,128)S(1)}, u32[]{:S(2)}, u32[]{:S(2)}) collective-permute-start(f32[256,256]{0,1:T(8,128)S(1)} %copy.15), channel_id=1, source_target_pairs={{0,6},{2,0},{4,2},{6,4},{8,14},{10,8},{12,10},{14,12},{16,22},{18,... | collective-permute-start | bytes 786440 | tf_op jit(solution)/shard_map/ppermute | solution.py:25
  17.1 9.1 %collective-permute-start.5 = (f32[1,2,64,256]{2,3,1,0:T(8,128)S(1)}, f32[1,2,64,256]{2,3,1,0:T(8,128)S(1)}, u32[]{:S(2)}, u32[]{:S(2)}) collective-permute-start(f32[1,2,64,256]{2,3,1,0:T(8,128)S(1)} %maximum_select_fusion.9), channel_id=1, source_target_pairs={{0,256},{2,258},{4,260},{6,262},{8,264},{10,266},{12,268},{14,270}... | collective-permute-start | bytes 393224 | tf_op jit(solution)/shard_map/ppermute | solution.py:25
  32.0 4.5 %all-to-all-start = ((f32[4,2,64,256]{3,2,1,0:T(8,128)}), f32[4,2,64,256]{3,2,1,0:T(8,128)}, u32[]{:S(2)}, u32[]{:S(2)}) async-start(f32[4,2,64,256]{3,2,1,0:T(8,128)} %broadcast_in_dim.54), calls=%async_computation | async-start | bytes 1048576 | tf_op jit(solution)/shard_map/all_to_all | solution.py:52
  36.5 5.2 %collective-permute-done.5 = f32[1,2,64,256]{2,3,1,0:T(8,128)S(1)} collective-permute-done((f32[1,2,64,256]{2,3,1,0:T(8,128)S(1)}, f32[1,2,64,256]{2,3,1,0:T(8,128)S(1)}, u32[]{:S(2)}, u32[]{:S(2)}) %collective-permute-start.5) | collective-permute-done | bytes 131104 | tf_op jit(solution)/shard_map/ppermute | solution.py:25
  45.1 12.2 %collective-permute-done.6 = f32[2,2,64,256]{2,3,1,0:T(8,128)S(1)} collective-permute-done((f32[2,2,64,256]{2,3,1,0:T(8,128)}, f32[2,2,64,256]{2,3,1,0:T(8,128)S(1)}, u32[]{:S(2)}, u32[]{:S(2)}) %collective-permute-start.6) | collective-permute-done | bytes 262176 | tf_op jit(solution)/shard_map/ppermute | solution.py:25
  63.9 6.6 %collective-permute-start.14 = (f32[64,1024]{1,0:T(8,128)}, f32[64,1024]{1,0:T(8,128)}, u32[]{:S(2)}, u32[]{:S(2)}) collective-permute-start(f32[64,1024]{1,0:T(8,128)} %constant_dynamic-slice_fusion.2), channel_id=1, source_target_pairs={{0,64},{2,66},{4,68},{6,70},{8,72},{10,74},{12,76},{14,78},{16,80}... | collective-permute-start | bytes 786440 | tf_op jit(solution)/shard_map/ppermute | solution.py:25
  74.6 3.9 %collective-permute-start.8 = (f32[4,2,64,256]{3,2,1,0:T(8,128)S(1)}, f32[4,2,64,256]{3,2,1,0:T(8,128)}, u32[]{:S(2)}, u32[]{:S(2)}) collective-permute-start(f32[4,2,64,256]{3,2,1,0:T(8,128)S(1)} %bitcast.120), channel_id=1, source_target_pairs={{0,64},{2,66},{4,68},{6,70},{8,72},{10,74},{12,76},{14,78},{16,80}... | collective-permute-start | bytes 1572872 | tf_op jit(solution)/shard_map/ppermute | solution.py:25
  82.8 8.0 %rev.3 = f32[4,2,2,128,256]{3,2,1,4,0:T(2,128)} reverse(f32[4,2,2,128,256]{3,2,1,4,0:T(2,128)S(1)} %reshape.355), dimensions={2} | reverse | bytes 4194304 | tf_op jit(solution)/shard_map/rev | solution.py:139
  95.7 4.8 %collective-permute-done.15 = f32[32,1024]{1,0:T(8,128)S(1)} collective-permute-done((f32[32,1024]{1,0:T(8,128)S(1)}, f32[32,1024]{1,0:T(8,128)S(1)}, u32[]{:S(2)}, u32[]{:S(2)}) %collective-permute-start.15) | collective-permute-done | bytes 131104 | tf_op jit(solution)/shard_map/ppermute | solution.py:25
  101.1 7.0 %collective-permute-start.16 = (f32[16,1024]{1,0:T(8,128)}, f32[16,1024]{1,0:T(8,128)}, u32[]{:S(2)}, u32[]{:S(2)}) collective-permute-start(f32[16,1024]{1,0:T(8,128)} %constant_dynamic-slice_fusion), channel_id=1, source_target_pairs={{0,256},{2,258},{4,260},{6,262},{8,264},{10,266},{12,268},{14,270}... | collective-permute-start | bytes 196616 | tf_op jit(solution)/shard_map/ppermute | solution.py:25
  113.5 4.8 %all-to-all-start.1 = ((f32[4,4,64,256]{3,1,2,0:T(4,128)}), f32[4,4,64,256]{3,1,2,0:T(4,128)}, u32[]{:S(2)}, u32[]{:S(2)}) async-start(f32[4,4,64,256]{3,1,2,0:T(4,128)} %copy.20), calls=%async_computation.1 | async-start | bytes 2097152 | tf_op jit(solution)/shard_map/all_to_all | solution.py:52
  120.2 3.5 %collective-permute-start.10 = (f32[16,1024]{1,0:T(8,128)S(1)}, f32[16,1024]{1,0:T(8,128)S(1)}, u32[]{:S(2)}, u32[]{:S(2)}) collective-permute-start(f32[16,1024]{1,0:T(8,128)S(1)} %constant_dynamic-slice_fusion.5), channel_id=1, source_target_pairs={{0,256},{2,258},{4,260},{6,262},{8,264},{10,266},{12,268},{14,270}... | collective-permute-start | bytes 196616 | tf_op jit(solution)/shard_map/ppermute | solution.py:25
  123.8 4.0 %broadcast_select_fusion = f32[4,2,2,128,256]{3,2,1,4,0:T(2,128)} fusion(f32[4,2,2,128,256]{3,2,1,4,0:T(2,128)} %rev.3, f32[4,2,2,128,256]{3,2,1,4,0:T(2,128)S(1)} %reshape.355, pred[]{:T(512)S(6)} %eq.62), kind=kLoop, calls=%fused_computation.1 | loop fusion | flops 524288 | bytes 6291457 | tf_op jit(solution)/shard_map/jit(_where)/select_n | solution.py:139
  136.1 4.1 %collective-permute-start.11 = (f32[16,1024]{1,0:T(8,128)S(1)}, f32[16,1024]{1,0:T(8,128)S(1)}, u32[]{:S(2)}, u32[]{:S(2)}) collective-permute-start(f32[16,1024]{1,0:T(8,128)S(1)} %get-tuple-element.16), channel_id=1, source_target_pairs={{0,256},{2,258},{4,260},{6,262},{8,264},{10,266},{12,268},{14,270}... | collective-permute-start | bytes 196616 | tf_op jit(solution)/shard_map/ppermute | solution.py:25
  140.2 7.3 %collective-permute-done.11 = f32[16,1024]{1,0:T(8,128)S(1)} collective-permute-done((f32[16,1024]{1,0:T(8,128)S(1)}, f32[16,1024]{1,0:T(8,128)S(1)}, u32[]{:S(2)}, u32[]{:S(2)}) %collective-permute-start.11) | collective-permute-done | bytes 65568 | tf_op jit(solution)/shard_map/ppermute | solution.py:25
  147.5 4.3 %collective-permute-start.12 = (f32[32,1024]{1,0:T(8,128)S(1)}, f32[32,1024]{1,0:T(8,128)S(1)}, u32[]{:S(2)}, u32[]{:S(2)}) collective-permute-start(f32[32,1024]{1,0:T(8,128)S(1)} %maximum_select_fusion.12), channel_id=1, source_target_pairs={{0,128},{2,130},{4,132},{6,134},{8,136},{10,138},{12,140},{14,142}... | collective-permute-start | bytes 393224 | tf_op jit(solution)/shard_map/ppermute | solution.py:25
  159.1 3.5 %collective-permute-done.17 = f32[16,1024]{1,0:T(8,128)S(1)} collective-permute-done((f32[16,1024]{1,0:T(8,128)}, f32[16,1024]{1,0:T(8,128)S(1)}, u32[]{:S(2)}, u32[]{:S(2)}) %collective-permute-start.17) | collective-permute-done | bytes 65568 | tf_op jit(solution)/shard_map/ppermute | solution.py:25
  165.6 5.7 %collective-permute-done.18 = f32[32,1024]{1,0:T(8,128)S(1)} collective-permute-done((f32[32,1024]{1,0:T(8,128)S(1)}, f32[32,1024]{1,0:T(8,128)S(1)}, u32[]{:S(2)}, u32[]{:S(2)}) %collective-permute-start.18) | collective-permute-done | bytes 131104 | tf_op jit(solution)/shard_map/ppermute | solution.py:25
  172.0 4.8 %collective-permute-start.19 = (f32[64,1024]{1,0:T(8,128)}, f32[64,1024]{1,0:T(8,128)}, u32[]{:S(2)}, u32[]{:S(2)}) collective-permute-start(f32[64,1024]{1,0:T(8,128)} %maximum_select_fusion.11), channel_id=1, source_target_pairs={{0,64},{2,66},{4,68},{6,70},{8,72},{10,74},{12,76},{14,78},{16,80}... | collective-permute-start | bytes 786440 | tf_op jit(solution)/shard_map/ppermute | solution.py:25
  178.4 3.6 %all-to-all-start.2 = ((f32[4,32,512]{2,1,0:T(8,128)}), f32[4,32,512]{2,1,0:T(8,128)S(1)}, u32[]{:S(2)}, u32[]{:S(2)}) async-start(f32[4,32,512]{2,1,0:T(8,128)} %bitcast.135), calls=%async_computation.2 | async-start | bytes 524288 | tf_op jit(solution)/shard_map/all_to_all | solution.py:52
  184.6 3.8 %all-to-all-done.2 = f32[4,32,512]{2,1,0:T(8,128)S(1)} async-done(((f32[4,32,512]{2,1,0:T(8,128)}), f32[4,32,512]{2,1,0:T(8,128)S(1)}, u32[]{:S(2)}, u32[]{:S(2)}) %all-to-all-start.2) | async-done | bytes 262176 | tf_op jit(solution)/shard_map/all_to_all | solution.py:52
  188.4 3.4 %all-to-all-start.4 = ((f32[4,32,512]{2,1,0:T(8,128)}), f32[4,32,512]{2,1,0:T(8,128)S(1)}, u32[]{:S(2)}, u32[]{:S(2)}) async-start(f32[4,32,512]{2,1,0:T(8,128)} %bitcast.35), calls=%async_computation.4 | async-start | bytes 524288 | tf_op jit(solution)/shard_map/all_to_all | solution.py:52
  191.9 6.6 %all-to-all-done.4 = f32[4,32,512]{2,1,0:T(8,128)S(1)} async-done(((f32[4,32,512]{2,1,0:T(8,128)}), f32[4,32,512]{2,1,0:T(8,128)S(1)}, u32[]{:S(2)}, u32[]{:S(2)}) %all-to-all-start.4) | async-done | bytes 262176 | tf_op jit(solution)/shard_map/all_to_all | solution.py:52
  202.7 6.6 %all-to-all-done.3 = f32[4,32,512]{2,1,0:T(8,128)S(1)} async-done(((f32[4,32,512]{2,1,0:T(8,128)}), f32[4,32,512]{2,1,0:T(8,128)S(1)}, u32[]{:S(2)}, u32[]{:S(2)}) %all-to-all-start.3) | async-done | bytes 262176 | tf_op jit(solution)/shard_map/all_to_all | solution.py:52
  210.0 3.4 %all-to-all-start.5 = ((f32[4,32,512]{2,1,0:T(8,128)}), f32[4,32,512]{2,1,0:T(8,128)S(1)}, u32[]{:S(2)}, u32[]{:S(2)}) async-start(f32[4,32,512]{2,1,0:T(8,128)} %broadcast_in_dim.61), calls=%async_computation.5 | async-start | bytes 524288 | tf_op jit(solution)/shard_map/all_to_all | solution.py:52
  214.3 5.8 %all-to-all-done.5 = f32[4,32,512]{2,1,0:T(8,128)S(1)} async-done(((f32[4,32,512]{2,1,0:T(8,128)}), f32[4,32,512]{2,1,0:T(8,128)S(1)}, u32[]{:S(2)}, u32[]{:S(2)}) %all-to-all-start.5) | async-done | bytes 262176 | tf_op jit(solution)/shard_map/all_to_all | solution.py:52
  228.3 6.1 %all-to-all-start.7 = ((f32[4,128,256]{2,1,0:T(8,128)}), f32[4,128,256]{2,1,0:T(8,128)S(1)}, u32[]{:S(2)}, u32[]{:S(2)}) async-start(f32[4,128,256]{2,1,0:T(8,128)} %fusion), calls=%async_computation.7 | async-start | bytes 1048576 | tf_op jit(solution)/shard_map/all_to_all | solution.py:52
  235.8 7.1 %all-to-all-done.7 = f32[4,128,256]{2,1,0:T(8,128)S(1)} async-done(((f32[4,128,256]{2,1,0:T(8,128)}), f32[4,128,256]{2,1,0:T(8,128)S(1)}, u32[]{:S(2)}, u32[]{:S(2)}) %all-to-all-start.7) | async-done | bytes 524320 | tf_op jit(solution)/shard_map/all_to_all | solution.py:52
  242.9 4.9 %all-to-all-start.6 = ((f32[4,128,256]{2,1,0:T(8,128)}), f32[4,128,256]{2,1,0:T(8,128)S(1)}, u32[]{:S(2)}, u32[]{:S(2)}) async-start(f32[4,128,256]{2,1,0:T(8,128)} %fusion.1), calls=%async_computation.6 | async-start | bytes 1048576 | tf_op jit(solution)/shard_map/all_to_all | solution.py:52
  247.8 7.4 %collective-permute-start.22 = (f32[128,256]{1,0:T(8,128)S(1)}, f32[128,256]{1,0:T(8,128)S(1)}, u32[]{:S(2)}, u32[]{:S(2)}) collective-permute-start(f32[128,256]{1,0:T(8,128)S(1)} %reduce_sum.39), channel_id=1, source_target_pairs={{0,1},{2,3},{4,5},{6,7},{8,9},{10,11},{12,13},{14,15},{16,17},{18,... | collective-permute-start | bytes 393224 | tf_op jit(solution)/shard_map/ppermute | solution.py:25
  255.5 15.6 %collective-permute-done.22 = f32[128,256]{1,0:T(8,128)S(1)} collective-permute-done((f32[128,256]{1,0:T(8,128)S(1)}, f32[128,256]{1,0:T(8,128)S(1)}, u32[]{:S(2)}, u32[]{:S(2)}) %collective-permute-start.22) | collective-permute-done | bytes 131104 | tf_op jit(solution)/shard_map/ppermute | solution.py:25
  (156 shorter events, 84.9 us)
Async XLA Ops:
  0.0 15.4 %copy-start.11 = (f32[4096]{0:T(1024)S(1)}, f32[4096]{0:T(1024)}, u32[]{:S(2)}) copy-start(f32[4096]{0:T(1024)} %param.7) | copy-start | bytes 49156
  1.1 25.1 %collective-permute-start.3 = (f32[256,256]{0,1:T(8,128)S(1)}, f32[256,256]{0,1:T(8,128)S(1)}, u32[]{:S(2)}, u32[]{:S(2)}) collective-permute-start(f32[256,256]{0,1:T(8,128)S(1)} %copy.15), channel_id=1, source_target_pairs={{0,4},{2,6},{4,0},{6,2},{8,12},{10,14},{12,8},{14,10},{16,20},{18,... | collective-permute-start | bytes 786440 | tf_op jit(solution)/shard_map/ppermute | solution.py:25
  5.1 21.1 %collective-permute-start.2 = (f32[256,256]{0,1:T(8,128)S(1)}, f32[256,256]{0,1:T(8,128)S(1)}, u32[]{:S(2)}, u32[]{:S(2)}) collective-permute-start(f32[256,256]{0,1:T(8,128)S(1)} %copy.15), channel_id=1, source_target_pairs={{0,2},{2,4},{4,6},{6,0},{8,10},{10,12},{12,14},{14,8},{16,18},{18,... | collective-permute-start | bytes 786440 | tf_op jit(solution)/shard_map/ppermute | solution.py:25
  7.1 19.2 %collective-permute-start.1 = (f32[256,256]{0,1:T(8,128)S(1)}, f32[256,256]{0,1:T(8,128)S(1)}, u32[]{:S(2)}, u32[]{:S(2)}) collective-permute-start(f32[256,256]{0,1:T(8,128)S(1)} %copy.15), channel_id=1, source_target_pairs={{0,6},{2,0},{4,2},{6,4},{8,14},{10,8},{12,10},{14,12},{16,22},{18,... | collective-permute-start | bytes 786440 | tf_op jit(solution)/shard_map/ppermute | solution.py:25
  12.4 4.0 %collective-permute-start = (f32[2,64,256]{1,2,0:T(8,128)S(1)}, f32[2,64,256]{1,2,0:T(8,128)S(1)}, u32[]{:S(2)}, u32[]{:S(2)}) collective-permute-start(f32[2,64,256]{1,2,0:T(8,128)S(1)} %get-tuple-element.24), channel_id=1, source_target_pairs={{0,32},{2,34},{4,36},{6,38},{8,40},{10,42},{12,44},{14,46},{16,48}... | collective-permute-start | bytes 393224 | tf_op jit(solution)/shard_map/ppermute | solution.py:25
  17.1 24.6 %collective-permute-start.5 = (f32[1,2,64,256]{2,3,1,0:T(8,128)S(1)}, f32[1,2,64,256]{2,3,1,0:T(8,128)S(1)}, u32[]{:S(2)}, u32[]{:S(2)}) collective-permute-start(f32[1,2,64,256]{2,3,1,0:T(8,128)S(1)} %maximum_select_fusion.9), channel_id=1, source_target_pairs={{0,256},{2,258},{4,260},{6,262},{8,264},{10,266},{12,268},{14,270}... | collective-permute-start | bytes 393224 | tf_op jit(solution)/shard_map/ppermute | solution.py:25
  27.2 34.6 %collective-permute-start.4 = (f32[4,256,256]{1,2,0:T(8,128)S(1)}, f32[4,256,256]{1,2,0:T(8,128)S(1)}, u32[]{:S(2)}, u32[]{:S(2)}) collective-permute-start(f32[4,256,256]{1,2,0:T(8,128)S(1)} %pad_maximum_fusion.1), channel_id=1, source_target_pairs={{0,32},{2,34},{4,36},{6,38},{8,40},{10,42},{12,44},{14,46},{16,48}... | collective-permute-start | bytes 3145736 | tf_op jit(solution)/shard_map/ppermute | solution.py:25
  32.0 28.6 %all-to-all-start = ((f32[4,2,64,256]{3,2,1,0:T(8,128)}), f32[4,2,64,256]{3,2,1,0:T(8,128)}, u32[]{:S(2)}, u32[]{:S(2)}) async-start(f32[4,2,64,256]{3,2,1,0:T(8,128)} %broadcast_in_dim.54), calls=%async_computation | async-start | bytes 1048576 | tf_op jit(solution)/shard_map/all_to_all | solution.py:52
  42.5 14.8 %collective-permute-start.6 = (f32[2,2,64,256]{2,3,1,0:T(8,128)}, f32[2,2,64,256]{2,3,1,0:T(8,128)S(1)}, u32[]{:S(2)}, u32[]{:S(2)}) collective-permute-start(f32[2,2,64,256]{2,3,1,0:T(8,128)} %maximum_select_fusion.3), channel_id=1, source_target_pairs={{0,128},{2,130},{4,132},{6,134},{8,136},{10,138},{12,140},{14,142}... | collective-permute-start | bytes 786440 | tf_op jit(solution)/shard_map/ppermute | solution.py:25
  63.9 26.9 %collective-permute-start.14 = (f32[64,1024]{1,0:T(8,128)}, f32[64,1024]{1,0:T(8,128)}, u32[]{:S(2)}, u32[]{:S(2)}) collective-permute-start(f32[64,1024]{1,0:T(8,128)} %constant_dynamic-slice_fusion.2), channel_id=1, source_target_pairs={{0,64},{2,66},{4,68},{6,70},{8,72},{10,74},{12,76},{14,78},{16,80}... | collective-permute-start | bytes 786440 | tf_op jit(solution)/shard_map/ppermute | solution.py:25
  72.6 22.1 %collective-permute-start.7 = (f32[64,1024]{1,0:T(8,128)}, f32[64,1024]{1,0:T(8,128)}, u32[]{:S(2)}, u32[]{:S(2)}) collective-permute-start(f32[64,1024]{1,0:T(8,128)} %constant_dynamic-slice_fusion.7), channel_id=1, source_target_pairs={{0,64},{2,66},{4,68},{6,70},{8,72},{10,74},{12,76},{14,78},{16,80}... | collective-permute-start | bytes 786440 | tf_op jit(solution)/shard_map/ppermute | solution.py:25
  74.6 33.6 %collective-permute-start.8 = (f32[4,2,64,256]{3,2,1,0:T(8,128)S(1)}, f32[4,2,64,256]{3,2,1,0:T(8,128)}, u32[]{:S(2)}, u32[]{:S(2)}) collective-permute-start(f32[4,2,64,256]{3,2,1,0:T(8,128)S(1)} %bitcast.120), channel_id=1, source_target_pairs={{0,64},{2,66},{4,68},{6,70},{8,72},{10,74},{12,76},{14,78},{16,80}... | collective-permute-start | bytes 1572872 | tf_op jit(solution)/shard_map/ppermute | solution.py:25
  91.9 8.6 %collective-permute-start.15 = (f32[32,1024]{1,0:T(8,128)S(1)}, f32[32,1024]{1,0:T(8,128)S(1)}, u32[]{:S(2)}, u32[]{:S(2)}) collective-permute-start(f32[32,1024]{1,0:T(8,128)S(1)} %constant_dynamic-slice_fusion.1), channel_id=1, source_target_pairs={{0,128},{2,130},{4,132},{6,134},{8,136},{10,138},{12,140},{14,142}... | collective-permute-start | bytes 393224 | tf_op jit(solution)/shard_map/ppermute | solution.py:25
  101.1 29.7 %collective-permute-start.16 = (f32[16,1024]{1,0:T(8,128)}, f32[16,1024]{1,0:T(8,128)}, u32[]{:S(2)}, u32[]{:S(2)}) collective-permute-start(f32[16,1024]{1,0:T(8,128)} %constant_dynamic-slice_fusion), channel_id=1, source_target_pairs={{0,256},{2,258},{4,260},{6,262},{8,264},{10,266},{12,268},{14,270}... | collective-permute-start | bytes 196616 | tf_op jit(solution)/shard_map/ppermute | solution.py:25
  109.6 10.6 %collective-permute-start.9 = (f32[32,1024]{1,0:T(8,128)S(1)}, f32[32,1024]{1,0:T(8,128)S(1)}, u32[]{:S(2)}, u32[]{:S(2)}) collective-permute-start(f32[32,1024]{1,0:T(8,128)S(1)} %constant_dynamic-slice_fusion.6), channel_id=1, source_target_pairs={{0,128},{2,130},{4,132},{6,134},{8,136},{10,138},{12,140},{14,142}... | collective-permute-start | bytes 393224 | tf_op jit(solution)/shard_map/ppermute | solution.py:25
  113.5 21.2 %all-to-all-start.1 = ((f32[4,4,64,256]{3,1,2,0:T(4,128)}), f32[4,4,64,256]{3,1,2,0:T(4,128)}, u32[]{:S(2)}, u32[]{:S(2)}) async-start(f32[4,4,64,256]{3,1,2,0:T(4,128)} %copy.20), calls=%async_computation.1 | async-start | bytes 2097152 | tf_op jit(solution)/shard_map/all_to_all | solution.py:52
  120.2 10.6 %collective-permute-start.10 = (f32[16,1024]{1,0:T(8,128)S(1)}, f32[16,1024]{1,0:T(8,128)S(1)}, u32[]{:S(2)}, u32[]{:S(2)}) collective-permute-start(f32[16,1024]{1,0:T(8,128)S(1)} %constant_dynamic-slice_fusion.5), channel_id=1, source_target_pairs={{0,256},{2,258},{4,260},{6,262},{8,264},{10,266},{12,268},{14,270}... | collective-permute-start | bytes 196616 | tf_op jit(solution)/shard_map/ppermute | solution.py:25
  136.1 11.4 %collective-permute-start.11 = (f32[16,1024]{1,0:T(8,128)S(1)}, f32[16,1024]{1,0:T(8,128)S(1)}, u32[]{:S(2)}, u32[]{:S(2)}) collective-permute-start(f32[16,1024]{1,0:T(8,128)S(1)} %get-tuple-element.16), channel_id=1, source_target_pairs={{0,256},{2,258},{4,260},{6,262},{8,264},{10,266},{12,268},{14,270}... | collective-permute-start | bytes 196616 | tf_op jit(solution)/shard_map/ppermute | solution.py:25
  147.5 9.2 %collective-permute-start.12 = (f32[32,1024]{1,0:T(8,128)S(1)}, f32[32,1024]{1,0:T(8,128)S(1)}, u32[]{:S(2)}, u32[]{:S(2)}) collective-permute-start(f32[32,1024]{1,0:T(8,128)S(1)} %maximum_select_fusion.12), channel_id=1, source_target_pairs={{0,128},{2,130},{4,132},{6,134},{8,136},{10,138},{12,140},{14,142}... | collective-permute-start | bytes 393224 | tf_op jit(solution)/shard_map/ppermute | solution.py:25
  151.8 10.8 %collective-permute-start.17 = (f32[16,1024]{1,0:T(8,128)}, f32[16,1024]{1,0:T(8,128)S(1)}, u32[]{:S(2)}, u32[]{:S(2)}) collective-permute-start(f32[16,1024]{1,0:T(8,128)} %get-tuple-element.29), channel_id=1, source_target_pairs={{0,256},{2,258},{4,260},{6,262},{8,264},{10,266},{12,268},{14,270}... | collective-permute-start | bytes 196616 | tf_op jit(solution)/shard_map/ppermute | solution.py:25
  156.7 20.1 %collective-permute-start.13 = (f32[64,1024]{1,0:T(8,128)S(1)}, f32[64,1024]{1,0:T(8,128)S(1)}, u32[]{:S(2)}, u32[]{:S(2)}) collective-permute-start(f32[64,1024]{1,0:T(8,128)S(1)} %maximum_select_fusion.10), channel_id=1, source_target_pairs={{0,64},{2,66},{4,68},{6,70},{8,72},{10,74},{12,76},{14,78},{16,80}... | collective-permute-start | bytes 786440 | tf_op jit(solution)/shard_map/ppermute | solution.py:25
  163.5 7.8 %collective-permute-start.18 = (f32[32,1024]{1,0:T(8,128)S(1)}, f32[32,1024]{1,0:T(8,128)S(1)}, u32[]{:S(2)}, u32[]{:S(2)}) collective-permute-start(f32[32,1024]{1,0:T(8,128)S(1)} %maximum_select_fusion.13), channel_id=1, source_target_pairs={{0,128},{2,130},{4,132},{6,134},{8,136},{10,138},{12,140},{14,142}... | collective-permute-start | bytes 393224 | tf_op jit(solution)/shard_map/ppermute | solution.py:25
  172.0 10.0 %collective-permute-start.19 = (f32[64,1024]{1,0:T(8,128)}, f32[64,1024]{1,0:T(8,128)}, u32[]{:S(2)}, u32[]{:S(2)}) collective-permute-start(f32[64,1024]{1,0:T(8,128)} %maximum_select_fusion.11), channel_id=1, source_target_pairs={{0,64},{2,66},{4,68},{6,70},{8,72},{10,74},{12,76},{14,78},{16,80}... | collective-permute-start | bytes 786440 | tf_op jit(solution)/shard_map/ppermute | solution.py:25
  178.4 10.1 %all-to-all-start.2 = ((f32[4,32,512]{2,1,0:T(8,128)}), f32[4,32,512]{2,1,0:T(8,128)S(1)}, u32[]{:S(2)}, u32[]{:S(2)}) async-start(f32[4,32,512]{2,1,0:T(8,128)} %bitcast.135), calls=%async_computation.2 | async-start | bytes 524288 | tf_op jit(solution)/shard_map/all_to_all | solution.py:52
  188.4 10.1 %all-to-all-start.4 = ((f32[4,32,512]{2,1,0:T(8,128)}), f32[4,32,512]{2,1,0:T(8,128)S(1)}, u32[]{:S(2)}, u32[]{:S(2)}) async-start(f32[4,32,512]{2,1,0:T(8,128)} %bitcast.35), calls=%async_computation.4 | async-start | bytes 524288 | tf_op jit(solution)/shard_map/all_to_all | solution.py:52
  199.2 10.1 %all-to-all-start.3 = ((f32[4,32,512]{2,1,0:T(8,128)}), f32[4,32,512]{2,1,0:T(8,128)S(1)}, u32[]{:S(2)}, u32[]{:S(2)}) async-start(f32[4,32,512]{2,1,0:T(8,128)} %broadcast_in_dim.59), calls=%async_computation.3 | async-start | bytes 524288 | tf_op jit(solution)/shard_map/all_to_all | solution.py:52
  210.0 10.1 %all-to-all-start.5 = ((f32[4,32,512]{2,1,0:T(8,128)}), f32[4,32,512]{2,1,0:T(8,128)S(1)}, u32[]{:S(2)}, u32[]{:S(2)}) async-start(f32[4,32,512]{2,1,0:T(8,128)} %broadcast_in_dim.61), calls=%async_computation.5 | async-start | bytes 524288 | tf_op jit(solution)/shard_map/all_to_all | solution.py:52
  221.0 6.5 %collective-permute-start.21 = (f32[4,128,256]{2,1,0:T(8,128)S(1)}, f32[4,128,256]{2,1,0:T(8,128)S(1)}, u32[]{:S(2)}, u32[]{:S(2)}) collective-permute-start(f32[4,128,256]{2,1,0:T(8,128)S(1)} %bitcast.144), channel_id=1, source_target_pairs={{0,32},{2,34},{4,36},{6,38},{8,40},{10,42},{12,44},{14,46},{16,48}... | collective-permute-start | bytes 1572872 | tf_op jit(solution)/shard_map/ppermute | solution.py:25
  224.2 10.6 %collective-permute-start.20 = (f32[4,128,256]{2,1,0:T(8,128)}, f32[4,128,256]{2,1,0:T(8,128)S(1)}, u32[]{:S(2)}, u32[]{:S(2)}) collective-permute-start(f32[4,128,256]{2,1,0:T(8,128)} %bitcast.99), channel_id=1, source_target_pairs={{0,32},{2,34},{4,36},{6,38},{8,40},{10,42},{12,44},{14,46},{16,48}... | collective-permute-start | bytes 1572872 | tf_op jit(solution)/shard_map/ppermute | solution.py:25
  228.3 14.6 %all-to-all-start.7 = ((f32[4,128,256]{2,1,0:T(8,128)}), f32[4,128,256]{2,1,0:T(8,128)S(1)}, u32[]{:S(2)}, u32[]{:S(2)}) async-start(f32[4,128,256]{2,1,0:T(8,128)} %fusion), calls=%async_computation.7 | async-start | bytes 1048576 | tf_op jit(solution)/shard_map/all_to_all | solution.py:52
  242.9 12.5 %all-to-all-start.6 = ((f32[4,128,256]{2,1,0:T(8,128)}), f32[4,128,256]{2,1,0:T(8,128)S(1)}, u32[]{:S(2)}, u32[]{:S(2)}) async-start(f32[4,128,256]{2,1,0:T(8,128)} %fusion.1), calls=%async_computation.6 | async-start | bytes 1048576 | tf_op jit(solution)/shard_map/all_to_all | solution.py:52
  247.8 23.2 %collective-permute-start.22 = (f32[128,256]{1,0:T(8,128)S(1)}, f32[128,256]{1,0:T(8,128)S(1)}, u32[]{:S(2)}, u32[]{:S(2)}) collective-permute-start(f32[128,256]{1,0:T(8,128)S(1)} %reduce_sum.39), channel_id=1, source_target_pairs={{0,1},{2,3},{4,5},{6,7},{8,9},{10,11},{12,13},{14,15},{16,17},{18,... | collective-permute-start | bytes 393224 | tf_op jit(solution)/shard_map/ppermute | solution.py:25
  (17 other events, 67.9 us)

commit v3 on v1

v3 whole, which is shorter than its diff:
```python
import jax
import jax.numpy as jnp
from jax import lax
from jax.sharding import Mesh
from jax.sharding import PartitionSpec as P

AXES = ("zl", "co", "y", "x", "zh")
SIZES = (8, 2, 4, 4, 2)
SHIFT = 3
PREC = lax.Precision.HIGH


def place(z, co, y, x):
    return (((z % 8 * 2 + co) * 4 + y) * 4 + x) * 2 + z // 8


def moved(v, target):
    pairs = [
        (place(z, co, y, x), place(*target(z, co, y, x)))
        for z in range(16)
        for co in range(2)
        for y in range(4)
        for x in range(4)
    ]
    return lax.ppermute(v, AXES, pairs)


def other_core(z, co, y, x):
    return z, 1 - co, y, x


def other_layer(z, co, y, x):
    return (z + 8) % 16, co, y, x


def along(distance):
    def target(z, co, y, x):
        at = (z - SHIFT * co) % 16
        return ((at ^ distance) + SHIFT * co) % 16, co, y, x

    return target


def to_all(v, axis):
    return lax.all_to_all(v, axis, 0, 0, tiled=True)


def sent_to_all(v, axis):
    peers = lax.axis_size(axis)
    return to_all(jnp.broadcast_to(v[None], (peers, *v.shape)), axis)


def turned_round(v, first):
    return lax.dynamic_slice_in_dim(jnp.concatenate([v, v]), first, v.shape[0], 0)


def dot(a, b, contract=((1,), (0,))):
    return lax.dot_general(
        a, b, (contract, ((), ())), precision=PREC, preferred_element_type=jnp.float32
    )


def tied(*values):
    return lax.optimization_barrier(values)


def part(v, which, length, dim=0):
    return lax.dynamic_slice_in_dim(v, which * length, length, dim)


def joined(own, other, bit, dim=0):
    return jnp.where(
        bit == 1,
        jnp.concatenate([other, own], dim),
        jnp.concatenate([own, other], dim),
    )


def on_device(basis, basis_grad, value_grad, ranks, offsets):
    n = basis.shape[0]
    quarter = n // 4
    half = n // 2
    zl, co, y, x, zh = (lax.axis_index(a) for a in AXES)
    z = zh * 8 + zl
    at = (z - SHIFT * co) % 16
    group = at // 8
    group_other = ((z - SHIFT * (1 - co)) % 16) // 8
    bits = [at % 2, at // 2 % 2, at // 4 % 2]
    mine = 2 * co + group
    theirs = 2 * (1 - co) + group_other

    turned = jnp.stack([basis_grad.T, basis.T])
    own = part(turned, mine, quarter, 1)
    other = moved(part(turned, theirs, quarter, 1), other_core)

    wide = sent_to_all(basis, "x")
    grads = jnp.broadcast_to(jnp.stack([own[0], other[0]])[None], (4, 2, quarter, n))
    far = joined(own[1][None], other[1][None], co)
    far = joined(far[None], moved(far, along(4))[None], bits[2])
    wide, grads, far = tied(wide, grads, far)
    (wide,) = tied(wide.swapaxes(0, 1).reshape(n, 4 * n))
    wide_oth = moved(wide, other_core)
    grads = to_all(grads, "y")

    far = joined(far[:, None], moved(far, along(2))[:, None], bits[1], 1)
    grads, far = tied(grads, far.reshape(4, 2, quarter, n))
    far = turned_round(far, (4 - co * ((SHIFT + bits[0]) // 2)) % 4)

    def inner_of(which):
        g = part(grads, which, 2)
        return dot(g[:, 0].reshape(half, n), wide) + dot(g[:, 1].reshape(half, n), wide_oth)

    got = moved(inner_of(1 - bits[0]), along(1))
    kept = inner_of(bits[0])
    rows = half
    for distance, bit in ((2, bits[1]), (4, bits[2])):
        rows //= 2
        leaving = part(kept, 1 - bit, rows) + part(got, 1 - bit, rows)
        kept = part(kept, bit, rows) + part(got, bit, rows)
        got = moved(leaving, along(distance))
    inner = kept + got

    eigen = 4.0 * ranks.astype(jnp.float32) + offsets.astype(jnp.float32)
    index = jnp.arange(eigen.shape[0], dtype=jnp.int32)

    def of_columns(v):
        v = part(part(v.reshape(4, 4, 4, quarter), x, 1, 1), mine, 1, 2).reshape(4 * quarter)
        return part(v, bits[0] * 4 + bits[1] * 2 + bits[2], rows)[:, None]

    row_index, row_eigen = (part(v, y, 4 * n)[None, :] for v in (index, eigen))
    on_diagonal = of_columns(index) == row_index
    spacing = jnp.where(on_diagonal, jnp.float32(1.0), of_columns(eigen) - row_eigen)
    scaled = jnp.where(on_diagonal, of_columns(value_grad), inner / spacing)

    scaled, far = tied(scaled, far)
    far = to_all(far, "y")
    for distance, bit in ((4, bits[2]), (2, bits[1])):
        scaled = joined(scaled, moved(scaled, along(distance)), bit)
    scaled_oth = moved(scaled, along(1))

    def left_of(s):
        return jnp.concatenate([dot(w, s, ((1,), (1,))) for w in (wide, wide_oth)])

    left = jnp.concatenate([left_of(scaled), left_of(scaled_oth)], 1)
    left, far = tied(left, far)
    far_oth = moved(far, along(1))
    left = to_all(left.reshape(4, half, n), "y").sum(0)
    left = sent_to_all(left, "y").reshape(2 * n, n)

    far = joined(far[None], far_oth[None], z % 2)
    far = far.transpose(1, 3, 0, 2, 4).reshape(2, half, 4 * n)
    (far,) = tied(jnp.where(bits[0] == 1, jnp.stack([far[1], far[0]]), far).reshape(n, 4 * n))

    def product(rows_of):
        return dot(rows_of, far).reshape(n, 4, n).swapaxes(0, 1)

    theirs_out = moved(product(left[n:]), other_core)
    out = to_all(product(left[:n]) + theirs_out, "x").sum(0)
    return part(out, zh, half) + moved(part(out, 1 - zh, half), other_layer)


def solution(mesh):
    torus = Mesh(mesh.devices.reshape(SIZES), AXES)
    return jax.shard_map(
        on_device,
        mesh=torus,
        in_specs=(P(("zl", "co"), ("y", "x")), P(("zl", "co"), ("y", "x")), P(), P(), P()),
        out_specs=P(("zl", "co", "zh"), ("y", "x")),
        check_vma=False,
    )
```

time: 243 us -> 212 us (0.87)
  the two profiles are of different devices: /device:TPU:193 before, /device:TPU:64 now
where the time goes in v3:
time: 212 us; the launch traced here: 211 us
  waiting for transfers between devices  104 us (49%)
  starting transfers between devices  81.1 us (38%)
  local copies, waits for them, and re-layouts  11.7 us (6%)
  matrix products  8.83 us (4%)
  other arithmetic  4.3 us (2%)
    ppermute x13, waiting for transfers between devices, moved(): return lax.ppermute(v, AXES, pairs)  76.1 us
    ppermute x13, starting transfers between devices, moved(): return lax.ppermute(v, AXES, pairs)  55.8 us
    all_to_all x6, waiting for transfers between devices, to_all(): return lax.all_to_all(v, axis, 0, 0, tiled=True)  28 us
    all_to_all x6, starting transfers between devices, to_all(): return lax.all_to_all(v, axis, 0, 0, tiled=True)  25.3 us
    dot_general x10, matrix products, dot(): lax.dot_general(a, b, (contract, ((), ())), precision=PREC, preferred_ele...  8.83 us
  transfers between devices with their start and end apart: 19, of which 14 were waited for; matrix products, arithmetic and copies ran while one was open for 8% of the time, Pallas kernels for 0%

profile of v3, /device:TPU:64, one launch (start us, length us, event | category | flops | bytes accessed | tf_op | source)
XLA Modules:
  0.0 210.8 jit_solution(14054877733070036171)
XLA Ops:
  2.2 4.4 %all-to-all-start = ((f32[4,256,256]{1,2,0:T(8,128)}), f32[4,256,256]{1,2,0:T(8,128)S(1)}, u32[]{:S(2)}, u32[]{:S(2)}) async-start(f32[4,256,256]{1,2,0:T(8,128)} %broadcast_in_dim.28), calls=%async_computation | async-start | bytes 2097152 | tf_op jit(solution)/shard_map/all_to_all | solution.py:45
  6.8 1.9 collective-permute-start
  10.1 9.1 %collective-permute-start.1 = (f32[2,64,256]{2,1,0:T(8,128)S(1)}, f32[2,64,256]{2,1,0:T(8,128)S(1)}, u32[]{:S(2)}, u32[]{:S(2)}) collective-permute-start(f32[2,64,256]{2,1,0:T(8,128)S(1)} %maximum_select_fusion.5), channel_id=1, source_target_pairs={{0,256},{2,258},{4,260},{6,262},{8,264},{10,266},{12,268},{14,270}... | collective-permute-start | bytes 393224 | tf_op jit(solution)/shard_map/ppermute | solution.py:25
  19.2 7.0 %collective-permute-done.1 = f32[2,64,256]{2,1,0:T(8,128)S(1)} collective-permute-done((f32[2,64,256]{2,1,0:T(8,128)S(1)}, f32[2,64,256]{2,1,0:T(8,128)S(1)}, u32[]{:S(2)}, u32[]{:S(2)}) %collective-permute-start.1) | collective-permute-done | bytes 131104 | tf_op jit(solution)/shard_map/ppermute | solution.py:25
  27.1 2.0 collective-permute-start.3
  29.0 4.5 %all-to-all-start.1 = ((f32[4,2,64,256]{3,2,1,0:T(8,128)}), f32[4,2,64,256]{3,2,1,0:T(8,128)S(1)}, u32[]{:S(2)}, u32[]{:S(2)}) async-start(f32[4,2,64,256]{3,2,1,0:T(8,128)} %broadcast_in_dim.29), calls=%async_computation.1 | async-start | bytes 1048576 | tf_op jit(solution)/shard_map/all_to_all | solution.py:45
  33.5 2.9 %collective-permute-start.2 = (f32[2,2,64,256]{3,2,1,0:T(8,128)S(1)}, f32[2,2,64,256]{3,2,1,0:T(8,128)S(1)}, u32[]{:S(2)}, u32[]{:S(2)}) collective-permute-start(f32[2,2,64,256]{3,2,1,0:T(8,128)S(1)} %maximum_select_fusion.3), channel_id=1, source_target_pairs={{0,128},{2,130},{4,132},{6,134},{8,136},{10,138},{12,140},{14,142}... | collective-permute-start | bytes 786440 | tf_op jit(solution)/shard_map/ppermute | solution.py:25
  36.4 11.0 %collective-permute-done.2 = f32[2,2,64,256]{3,2,1,0:T(8,128)S(1)} collective-permute-done((f32[2,2,64,256]{3,2,1,0:T(8,128)S(1)}, f32[2,2,64,256]{3,2,1,0:T(8,128)S(1)}, u32[]{:S(2)}, u32[]{:S(2)}) %collective-permute-start.2) | collective-permute-done | bytes 262176 | tf_op jit(solution)/shard_map/ppermute | solution.py:25
  50.6 3.3 %collective-permute-start.4 = (f32[128,1024]{1,0:T(8,128)S(1)}, f32[128,1024]{1,0:T(8,128)S(1)}, u32[]{:S(2)}, u32[]{:S(2)}) collective-permute-start(f32[128,1024]{1,0:T(8,128)S(1)} %convolution_add_fusion), channel_id=1, source_target_pairs={{0,64},{2,66},{4,68},{6,70},{8,72},{10,74},{12,76},{14,78},{16,80}... | collective-permute-start | bytes 1572872 | tf_op jit(solution)/shard_map/ppermute | solution.py:25
  55.2 6.5 %collective-permute-done.4 = f32[128,1024]{1,0:T(8,128)S(1)} collective-permute-done((f32[128,1024]{1,0:T(8,128)S(1)}, f32[128,1024]{1,0:T(8,128)S(1)}, u32[]{:S(2)}, u32[]{:S(2)}) %collective-permute-start.4) | collective-permute-done | bytes 524320 | tf_op jit(solution)/shard_map/ppermute | solution.py:25
  61.8 3.3 %collective-permute-start.5 = (f32[64,1024]{1,0:T(8,128)S(1)}, f32[64,1024]{1,0:T(8,128)S(1)}, u32[]{:S(2)}, u32[]{:S(2)}) collective-permute-start(f32[64,1024]{1,0:T(8,128)S(1)} %get-tuple-element.26), channel_id=1, source_target_pairs={{0,128},{2,130},{4,132},{6,134},{8,136},{10,138},{12,140},{14,142}... | collective-permute-start | bytes 786440 | tf_op jit(solution)/shard_map/ppermute | solution.py:25
  65.2 11.3 %collective-permute-done.5 = f32[64,1024]{1,0:T(8,128)S(1)} collective-permute-done((f32[64,1024]{1,0:T(8,128)S(1)}, f32[64,1024]{1,0:T(8,128)S(1)}, u32[]{:S(2)}, u32[]{:S(2)}) %collective-permute-start.5) | collective-permute-done | bytes 262176 | tf_op jit(solution)/shard_map/ppermute | solution.py:25
  76.5 4.2 %collective-permute-start.6 = (f32[32,1024]{1,0:T(8,128)S(1)}, f32[32,1024]{1,0:T(8,128)S(1)}, u32[]{:S(2)}, u32[]{:S(2)}) collective-permute-start(f32[32,1024]{1,0:T(8,128)S(1)} %dynamic-slice_add_fusion.3), channel_id=1, source_target_pairs={{0,256},{2,258},{4,260},{6,262},{8,264},{10,266},{12,268},{14,270}... | collective-permute-start | bytes 393224 | tf_op jit(solution)/shard_map/ppermute | solution.py:25
  83.0 5.9 %collective-permute-done.6 = f32[32,1024]{1,0:T(8,128)S(1)} collective-permute-done((f32[32,1024]{1,0:T(8,128)S(1)}, f32[32,1024]{1,0:T(8,128)S(1)}, u32[]{:S(2)}, u32[]{:S(2)}) %collective-permute-start.6) | collective-permute-done | bytes 131104 | tf_op jit(solution)/shard_map/ppermute | solution.py:25
  89.0 2.6 %collective-permute-start.7 = (f32[32,1024]{1,0:T(8,128)S(1)}, f32[32,1024]{1,0:T(8,128)S(1)}, u32[]{:S(2)}, u32[]{:S(2)}) collective-permute-start(f32[32,1024]{1,0:T(8,128)S(1)} %compare_select_fusion), channel_id=1, source_target_pairs={{0,256},{2,258},{4,260},{6,262},{8,264},{10,266},{12,268},{14,270}... | collective-permute-start | bytes 393224 | tf_op jit(solution)/shard_map/ppermute | solution.py:25
  91.5 11.1 %collective-permute-done.7 = f32[32,1024]{1,0:T(8,128)S(1)} collective-permute-done((f32[32,1024]{1,0:T(8,128)S(1)}, f32[32,1024]{1,0:T(8,128)S(1)}, u32[]{:S(2)}, u32[]{:S(2)}) %collective-permute-start.7) | collective-permute-done | bytes 131104 | tf_op jit(solution)/shard_map/ppermute | solution.py:25
  102.7 7.1 %collective-permute-start.8 = (f32[64,1024]{1,0:T(8,128)S(1)}, f32[64,1024]{1,0:T(8,128)S(1)}, u32[]{:S(2)}, u32[]{:S(2)}) collective-permute-start(f32[64,1024]{1,0:T(8,128)S(1)} %maximum_select_fusion.4), channel_id=1, source_target_pairs={{0,128},{2,130},{4,132},{6,134},{8,136},{10,138},{12,140},{14,142}... | collective-permute-start | bytes 786440 | tf_op jit(solution)/shard_map/ppermute | solution.py:25
  109.8 4.3 %all-to-all-start.2 = ((f32[4,2,64,256]{3,2,1,0:T(8,128)}), f32[4,2,64,256]{3,2,1,0:T(8,128)S(1)}, u32[]{:S(2)}, u32[]{:S(2)}) async-start(f32[4,2,64,256]{3,2,1,0:T(8,128)} %fusion.2), calls=%async_computation.2 | async-start | bytes 1048576 | tf_op jit(solution)/shard_map/all_to_all | solution.py:45
  114.0 2.9 %collective-permute-done.8 = f32[64,1024]{1,0:T(8,128)S(1)} collective-permute-done((f32[64,1024]{1,0:T(8,128)S(1)}, f32[64,1024]{1,0:T(8,128)S(1)}, u32[]{:S(2)}, u32[]{:S(2)}) %collective-permute-start.8) | collective-permute-done | bytes 262176 | tf_op jit(solution)/shard_map/ppermute | solution.py:25
  117.0 1.9 collective-permute-start.9
  120.9 7.2 %collective-permute-done.9 = f32[128,1024]{1,0:T(8,128)S(1)} collective-permute-done((f32[128,1024]{1,0:T(8,128)S(1)}, f32[128,1024]{1,0:T(8,128)S(1)}, u32[]{:S(2)}, u32[]{:S(2)}) %collective-permute-start.9) | collective-permute-done | bytes 524320 | tf_op jit(solution)/shard_map/ppermute | solution.py:25
  130.9 1.9 collective-permute-start.10
  132.8 3.7 %all-to-all-start.3 = ((f32[4,128,256]{2,1,0:T(8,128)}), f32[4,128,256]{2,1,0:T(8,128)S(1)}, u32[]{:S(2)}, u32[]{:S(2)}) async-start(f32[4,128,256]{2,1,0:T(8,128)} %bitcast.16), calls=%async_computation.3 | async-start | bytes 1048576 | tf_op jit(solution)/shard_map/all_to_all | solution.py:45
  136.5 9.8 %all-to-all-done.3 = f32[4,128,256]{2,1,0:T(8,128)S(1)} async-done(((f32[4,128,256]{2,1,0:T(8,128)}), f32[4,128,256]{2,1,0:T(8,128)S(1)}, u32[]{:S(2)}, u32[]{:S(2)}) %all-to-all-start.3) | async-done | bytes 524320 | tf_op jit(solution)/shard_map/all_to_all | solution.py:45
  147.3 3.6 %all-to-all-start.4 = ((f32[4,128,256]{2,1,0:T(8,128)}), f32[4,128,256]{2,1,0:T(8,128)S(1)}, u32[]{:S(2)}, u32[]{:S(2)}) async-start(f32[4,128,256]{2,1,0:T(8,128)} %broadcast_in_dim.58), calls=%async_computation.4 | async-start | bytes 1048576 | tf_op jit(solution)/shard_map/all_to_all | solution.py:45
  156.9 2.8 %all-to-all-done.4 = f32[4,128,256]{2,1,0:T(8,128)S(1)} async-done(((f32[4,128,256]{2,1,0:T(8,128)}), f32[4,128,256]{2,1,0:T(8,128)S(1)}, u32[]{:S(2)}, u32[]{:S(2)}) %all-to-all-start.4) | async-done | bytes 524320 | tf_op jit(solution)/shard_map/all_to_all | solution.py:45
  160.3 1.9 collective-permute-start.11
  162.3 2.6 %collective-permute-done.11 = f32[4,256,256]{2,1,0:T(8,128)S(1)} collective-permute-done((f32[4,256,256]{2,1,0:T(8,128)S(1)}, f32[4,256,256]{2,1,0:T(8,128)S(1)}, u32[]{:S(2)}, u32[]{:S(2)}) %collective-permute-start.11) | collective-permute-done | bytes 1048608 | tf_op jit(solution)/shard_map/ppermute | solution.py:25
  166.5 4.8 %all-to-all-start.5 = ((f32[4,256,256]{2,1,0:T(8,128)}), f32[4,256,256]{2,1,0:T(8,128)S(1)}, u32[]{:S(2)}, u32[]{:S(2)}) async-start(f32[4,256,256]{2,1,0:T(8,128)} %fusion), calls=%async_computation.5 | async-start | bytes 2097152 | tf_op jit(solution)/shard_map/all_to_all | solution.py:45
  171.3 15.4 %all-to-all-done.5 = f32[4,256,256]{2,1,0:T(8,128)S(1)} async-done(((f32[4,256,256]{2,1,0:T(8,128)}), f32[4,256,256]{2,1,0:T(8,128)S(1)}, u32[]{:S(2)}, u32[]{:S(2)}) %all-to-all-start.5) | async-done | bytes 1048608 | tf_op jit(solution)/shard_map/all_to_all | solution.py:45
  186.8 13.7 %collective-permute-start.12 = (f32[128,256]{1,0:T(8,128)S(1)}, f32[128,256]{1,0:T(8,128)S(1)}, u32[]{:S(2)}, u32[]{:S(2)}) collective-permute-start(f32[128,256]{1,0:T(8,128)S(1)} %constant_dynamic-slice_fusion.1), channel_id=1, source_target_pairs={{0,1},{2,3},{4,5},{6,7},{8,9},{10,11},{12,13},{14,15},{16,17},{18,... | collective-permute-start | bytes 393224 | tf_op jit(solution)/shard_map/ppermute | solution.py:25
  200.6 9.5 %collective-permute-done.12 = f32[128,256]{1,0:T(8,128)S(1)} collective-permute-done((f32[128,256]{1,0:T(8,128)S(1)}, f32[128,256]{1,0:T(8,128)S(1)}, u32[]{:S(2)}, u32[]{:S(2)}) %collective-permute-start.12) | collective-permute-done | bytes 131104 | tf_op jit(solution)/shard_map/ppermute | solution.py:25
  (79 shorter events, 26.1 us)
Async XLA Ops:
  2.2 4.4 %copy-start = (f32[256,256]{1,0:T(8,128)S(1)}, f32[256,256]{1,0:T(8,128)}, u32[]{:S(2)}) copy-start(f32[256,256]{1,0:T(8,128)} %param.6) | copy-start | bytes 786436
  2.2 24.0 %all-to-all-start = ((f32[4,256,256]{1,2,0:T(8,128)}), f32[4,256,256]{1,2,0:T(8,128)S(1)}, u32[]{:S(2)}, u32[]{:S(2)}) async-start(f32[4,256,256]{1,2,0:T(8,128)} %broadcast_in_dim.28), calls=%async_computation | async-start | bytes 2097152 | tf_op jit(solution)/shard_map/all_to_all | solution.py:45
  6.8 3.2 %collective-permute-start = (f32[2,64,256]{2,1,0:T(8,128)S(1)}, f32[2,64,256]{2,1,0:T(8,128)S(1)}, u32[]{:S(2)}, u32[]{:S(2)}) collective-permute-start(f32[2,64,256]{2,1,0:T(8,128)S(1)} %get-tuple-element.34), channel_id=1, source_target_pairs={{0,32},{2,34},{4,36},{6,38},{8,40},{10,42},{12,44},{14,46},{16,48}... | collective-permute-start | bytes 393224 | tf_op jit(solution)/shard_map/ppermute | solution.py:25
  10.1 16.1 %collective-permute-start.1 = (f32[2,64,256]{2,1,0:T(8,128)S(1)}, f32[2,64,256]{2,1,0:T(8,128)S(1)}, u32[]{:S(2)}, u32[]{:S(2)}) collective-permute-start(f32[2,64,256]{2,1,0:T(8,128)S(1)} %maximum_select_fusion.5), channel_id=1, source_target_pairs={{0,256},{2,258},{4,260},{6,262},{8,264},{10,266},{12,268},{14,270}... | collective-permute-start | bytes 393224 | tf_op jit(solution)/shard_map/ppermute | solution.py:25
  27.1 22.9 %collective-permute-start.3 = (f32[256,1024]{0,1:T(8,128)S(1)}, f32[256,1024]{0,1:T(8,128)S(1)}, u32[]{:S(2)}, u32[]{:S(2)}) collective-permute-start(f32[256,1024]{0,1:T(8,128)S(1)} %bitcast.62), channel_id=1, source_target_pairs={{0,32},{2,34},{4,36},{6,38},{8,40},{10,42},{12,44},{14,46},{16,48}... | collective-permute-start | bytes 3145736 | tf_op jit(solution)/shard_map/ppermute | solution.py:25
  29.0 20.2 %all-to-all-start.1 = ((f32[4,2,64,256]{3,2,1,0:T(8,128)}), f32[4,2,64,256]{3,2,1,0:T(8,128)S(1)}, u32[]{:S(2)}, u32[]{:S(2)}) async-start(f32[4,2,64,256]{3,2,1,0:T(8,128)} %broadcast_in_dim.29), calls=%async_computation.1 | async-start | bytes 1048576 | tf_op jit(solution)/shard_map/all_to_all | solution.py:45
  33.5 13.9 %collective-permute-start.2 = (f32[2,2,64,256]{3,2,1,0:T(8,128)S(1)}, f32[2,2,64,256]{3,2,1,0:T(8,128)S(1)}, u32[]{:S(2)}, u32[]{:S(2)}) collective-permute-start(f32[2,2,64,256]{3,2,1,0:T(8,128)S(1)} %maximum_select_fusion.3), channel_id=1, source_target_pairs={{0,128},{2,130},{4,132},{6,134},{8,136},{10,138},{12,140},{14,142}... | collective-permute-start | bytes 786440 | tf_op jit(solution)/shard_map/ppermute | solution.py:25
  47.4 0.7 copy-start.1
  50.6 11.1 %collective-permute-start.4 = (f32[128,1024]{1,0:T(8,128)S(1)}, f32[128,1024]{1,0:T(8,128)S(1)}, u32[]{:S(2)}, u32[]{:S(2)}) collective-permute-start(f32[128,1024]{1,0:T(8,128)S(1)} %convolution_add_fusion), channel_id=1, source_target_pairs={{0,64},{2,66},{4,68},{6,70},{8,72},{10,74},{12,76},{14,78},{16,80}... | collective-permute-start | bytes 1572872 | tf_op jit(solution)/shard_map/ppermute | solution.py:25
  61.7 3.4 %copy-start.4 = (s32[4096]{0:T(1024)S(1)}, s32[4096]{0:T(1024)}, u32[]{:S(2)}) copy-start(s32[4096]{0:T(1024)} %param.8) | copy-start | bytes 49156
  61.7 3.4 %copy-start.3 = (s32[4096]{0:T(1024)S(1)}, s32[4096]{0:T(1024)}, u32[]{:S(2)}) copy-start(s32[4096]{0:T(1024)} %param.9) | copy-start | bytes 49156
  61.8 14.7 %collective-permute-start.5 = (f32[64,1024]{1,0:T(8,128)S(1)}, f32[64,1024]{1,0:T(8,128)S(1)}, u32[]{:S(2)}, u32[]{:S(2)}) collective-permute-start(f32[64,1024]{1,0:T(8,128)S(1)} %get-tuple-element.26), channel_id=1, source_target_pairs={{0,128},{2,130},{4,132},{6,134},{8,136},{10,138},{12,140},{14,142}... | collective-permute-start | bytes 786440 | tf_op jit(solution)/shard_map/ppermute | solution.py:25
  65.1 15.5 %copy-start.2 = (f32[4096]{0:T(1024)}, f32[4096]{0:T(1024)S(1)}, u32[]{:S(2)}) copy-start(f32[4096]{0:T(1024)S(1)} %convert_add_fusion) | copy-start | bytes 49156
  76.5 12.4 %collective-permute-start.6 = (f32[32,1024]{1,0:T(8,128)S(1)}, f32[32,1024]{1,0:T(8,128)S(1)}, u32[]{:S(2)}, u32[]{:S(2)}) collective-permute-start(f32[32,1024]{1,0:T(8,128)S(1)} %dynamic-slice_add_fusion.3), channel_id=1, source_target_pairs={{0,256},{2,258},{4,260},{6,262},{8,264},{10,266},{12,268},{14,270}... | collective-permute-start | bytes 393224 | tf_op jit(solution)/shard_map/ppermute | solution.py:25
  80.8 0.7 copy-start.5
  82.1 6.7 %dynamic-slice-start = ((f32[4096]{0:T(1024)}, s32[]{:T(128)}), f32[1024]{0:T(1024)S(1)}, s32[]{:S(2)}) async-start(f32[4096]{0:T(1024)} %copy-done.2, s32[]{:T(128)} %select_n.211), calls=%async_computation.6 | async-start | bytes 8704 | tf_op jit(solution)/shard_map/dynamic_slice | solution.py:68
  89.0 13.6 %collective-permute-start.7 = (f32[32,1024]{1,0:T(8,128)S(1)}, f32[32,1024]{1,0:T(8,128)S(1)}, u32[]{:S(2)}, u32[]{:S(2)}) collective-permute-start(f32[32,1024]{1,0:T(8,128)S(1)} %compare_select_fusion), channel_id=1, source_target_pairs={{0,256},{2,258},{4,260},{6,262},{8,264},{10,266},{12,268},{14,270}... | collective-permute-start | bytes 393224 | tf_op jit(solution)/shard_map/ppermute | solution.py:25
  102.7 14.3 %collective-permute-start.8 = (f32[64,1024]{1,0:T(8,128)S(1)}, f32[64,1024]{1,0:T(8,128)S(1)}, u32[]{:S(2)}, u32[]{:S(2)}) collective-permute-start(f32[64,1024]{1,0:T(8,128)S(1)} %maximum_select_fusion.4), channel_id=1, source_target_pairs={{0,128},{2,130},{4,132},{6,134},{8,136},{10,138},{12,140},{14,142}... | collective-permute-start | bytes 786440 | tf_op jit(solution)/shard_map/ppermute | solution.py:25
  109.8 21.1 %all-to-all-start.2 = ((f32[4,2,64,256]{3,2,1,0:T(8,128)}), f32[4,2,64,256]{3,2,1,0:T(8,128)S(1)}, u32[]{:S(2)}, u32[]{:S(2)}) async-start(f32[4,2,64,256]{3,2,1,0:T(8,128)} %fusion.2), calls=%async_computation.2 | async-start | bytes 1048576 | tf_op jit(solution)/shard_map/all_to_all | solution.py:45
  117.0 11.1 %collective-permute-start.9 = (f32[128,1024]{1,0:T(8,128)S(1)}, f32[128,1024]{1,0:T(8,128)S(1)}, u32[]{:S(2)}, u32[]{:S(2)}) collective-permute-start(f32[128,1024]{1,0:T(8,128)S(1)} %maximum_select_fusion.2), channel_id=1, source_target_pairs={{0,64},{2,66},{4,68},{6,70},{8,72},{10,74},{12,76},{14,78},{16,80}... | collective-permute-start | bytes 1572872 | tf_op jit(solution)/shard_map/ppermute | solution.py:25
  130.9 20.0 %collective-permute-start.10 = (f32[4,2,64,256]{3,2,1,0:T(8,128)S(1)}, f32[4,2,64,256]{3,2,1,0:T(8,128)S(1)}, u32[]{:S(2)}, u32[]{:S(2)}) collective-permute-start(f32[4,2,64,256]{3,2,1,0:T(8,128)S(1)} %all-to-all-done.2), channel_id=1, source_target_pairs={{0,64},{2,66},{4,68},{6,70},{8,72},{10,74},{12,76},{14,78},{16,80}... | collective-permute-start | bytes 1572872 | tf_op jit(solution)/shard_map/ppermute | solution.py:25
  132.8 13.6 %all-to-all-start.3 = ((f32[4,128,256]{2,1,0:T(8,128)}), f32[4,128,256]{2,1,0:T(8,128)S(1)}, u32[]{:S(2)}, u32[]{:S(2)}) async-start(f32[4,128,256]{2,1,0:T(8,128)} %bitcast.16), calls=%async_computation.3 | async-start | bytes 1048576 | tf_op jit(solution)/shard_map/all_to_all | solution.py:45
  147.3 12.4 %all-to-all-start.4 = ((f32[4,128,256]{2,1,0:T(8,128)}), f32[4,128,256]{2,1,0:T(8,128)S(1)}, u32[]{:S(2)}, u32[]{:S(2)}) async-start(f32[4,128,256]{2,1,0:T(8,128)} %broadcast_in_dim.58), calls=%async_computation.4 | async-start | bytes 1048576 | tf_op jit(solution)/shard_map/all_to_all | solution.py:45
  160.3 4.6 %collective-permute-start.11 = (f32[4,256,256]{2,1,0:T(8,128)S(1)}, f32[4,256,256]{2,1,0:T(8,128)S(1)}, u32[]{:S(2)}, u32[]{:S(2)}) collective-permute-start(f32[4,256,256]{2,1,0:T(8,128)S(1)} %convolution_bitcast_fusion), channel_id=1, source_target_pairs={{0,32},{2,34},{4,36},{6,38},{8,40},{10,42},{12,44},{14,46},{16,48}... | collective-permute-start | bytes 3145736 | tf_op jit(solution)/shard_map/ppermute | solution.py:25
  166.5 20.2 %all-to-all-start.5 = ((f32[4,256,256]{2,1,0:T(8,128)}), f32[4,256,256]{2,1,0:T(8,128)S(1)}, u32[]{:S(2)}, u32[]{:S(2)}) async-start(f32[4,256,256]{2,1,0:T(8,128)} %fusion), calls=%async_computation.5 | async-start | bytes 2097152 | tf_op jit(solution)/shard_map/all_to_all | solution.py:45
  186.8 23.2 %collective-permute-start.12 = (f32[128,256]{1,0:T(8,128)S(1)}, f32[128,256]{1,0:T(8,128)S(1)}, u32[]{:S(2)}, u32[]{:S(2)}) collective-permute-start(f32[128,256]{1,0:T(8,128)S(1)} %constant_dynamic-slice_fusion.1), channel_id=1, source_target_pairs={{0,1},{2,3},{4,5},{6,7},{8,9},{10,11},{12,13},{14,15},{16,17},{18,... | collective-permute-start | bytes 393224 | tf_op jit(solution)/shard_map/ppermute | solution.py:25

commit v4 on v3

--- a/solution.py
+++ b/solution.py
@@ -4,8 +4,8 @@
 from jax.sharding import Mesh
 from jax.sharding import PartitionSpec as P
 
-AXES = ("zl", "co", "y", "x", "zh")
-SIZES = (8, 2, 4, 4, 2)
+AXES = ("zq", "zp", "co", "y", "x", "zh")
+SIZES = (4, 2, 2, 4, 4, 2)
 SHIFT = 3
 PREC = lax.Precision.HIGH
 
@@ -50,10 +50,6 @@
     return to_all(jnp.broadcast_to(v[None], (peers, *v.shape)), axis)
 
 
-def turned_round(v, first):
-    return lax.dynamic_slice_in_dim(jnp.concatenate([v, v]), first, v.shape[0], 0)
-
-
 def dot(a, b, contract=((1,), (0,))):
     return lax.dot_general(
         a, b, (contract, ((), ())), precision=PREC, preferred_element_type=jnp.float32
@@ -80,8 +76,8 @@
     n = basis.shape[0]
     quarter = n // 4
     half = n // 2
-    zl, co, y, x, zh = (lax.axis_index(a) for a in AXES)
-    z = zh * 8 + zl
+    zq, zp, co, y, x, zh = (lax.axis_index(a) for a in AXES)
+    z = zh * 8 + zq * 2 + zp
     at = (z - SHIFT * co) % 16
     group = at // 8
     group_other = ((z - SHIFT * (1 - co)) % 16) // 8
@@ -89,22 +85,25 @@
     mine = 2 * co + group
     theirs = 2 * (1 - co) + group_other
 
-    turned = jnp.stack([basis_grad.T, basis.T])
-    own = part(turned, mine, quarter, 1)
-    other = moved(part(turned, theirs, quarter, 1), other_core)
+    def shares(of_grads, core):
+        return jnp.concatenate(
+            [part(basis_grad.T, of_grads, quarter), part(basis.T, core, half)]
+        )
+
+    own = shares(mine, co)
+    other = moved(shares(theirs, 1 - co), other_core)
 
     wide = sent_to_all(basis, "x")
-    grads = jnp.broadcast_to(jnp.stack([own[0], other[0]])[None], (4, 2, quarter, n))
-    far = joined(own[1][None], other[1][None], co)
-    far = joined(far[None], moved(far, along(4))[None], bits[2])
-    wide, grads, far = tied(wide, grads, far)
+    grads = jnp.broadcast_to(
+        jnp.stack([own[:quarter], other[:quarter]])[None], (4, 2, quarter, n)
+    )
+    far = joined(own[None, quarter:], other[None, quarter:], co).reshape(2, 2, quarter, n)
+    grads, far = tied(grads, far)
+    far = lax.all_gather(far, "zq")
+    wide, grads = tied(wide, grads)
     (wide,) = tied(wide.swapaxes(0, 1).reshape(n, 4 * n))
     wide_oth = moved(wide, other_core)
     grads = to_all(grads, "y")
-
-    far = joined(far[:, None], moved(far, along(2))[:, None], bits[1], 1)
-    grads, far = tied(grads, far.reshape(4, 2, quarter, n))
-    far = turned_round(far, (4 - co * ((SHIFT + bits[0]) // 2)) % 4)
 
     def inner_of(which):
         g = part(grads, which, 2)
@@ -132,10 +131,10 @@
     spacing = jnp.where(on_diagonal, jnp.float32(1.0), of_columns(eigen) - row_eigen)
     scaled = jnp.where(on_diagonal, of_columns(value_grad), inner / spacing)
 
+    scaled = joined(scaled, moved(scaled, along(4)), bits[2])
+    scaled = joined(scaled, moved(scaled, along(2)), bits[1])
     scaled, far = tied(scaled, far)
-    far = to_all(far, "y")
-    for distance, bit in ((4, bits[2]), (2, bits[1])):
-        scaled = joined(scaled, moved(scaled, along(distance)), bit)
+    far = to_all(lax.dynamic_index_in_dim(far, group, 2, False), "y")
     scaled_oth = moved(scaled, along(1))
 
     def left_of(s):
@@ -155,8 +154,11 @@
         return dot(rows_of, far).reshape(n, 4, n).swapaxes(0, 1)
 
     theirs_out = moved(product(left[n:]), other_core)
-    out = to_all(product(left[:n]) + theirs_out, "x").sum(0)
-    return part(out, zh, half) + moved(part(out, 1 - zh, half), other_layer)
+    out = product(left[:n]) + theirs_out
+    leaving = to_all(part(out, 1 - zh, half, 1), "x").sum(0)
+    staying, leaving = tied(part(out, zh, half, 1), leaving)
+    staying = to_all(staying, "x")
+    return staying.sum(0) + moved(leaving, other_layer)
 
 
 def solution(mesh):
@@ -164,7 +166,7 @@
     return jax.shard_map(
         on_device,
         mesh=torus,
-        in_specs=(P(("zl", "co"), ("y", "x")), P(("zl", "co"), ("y", "x")), P(), P(), P()),
-        out_specs=P(("zl", "co", "zh"), ("y", "x")),
+        in_specs=(P(("zq", "zp", "co"), ("y", "x")), P(("zq", "zp", "co"), ("y", "x")), P(), P(), P()),
+        out_specs=P(("zq", "zp", "co", "zh"), ("y", "x")),
         check_vma=False,
     )

time: 212 us -> 250 us (1.18)
  the two profiles are of different devices: /device:TPU:64 before, /device:TPU:34 now
where the time goes in v4:
time: 250 us; the launch traced here: 249 us
  waiting for transfers between devices  110 us (44%)
  starting transfers between devices  86.7 us (35%)
  local copies, waits for them, and re-layouts  15.8 us (6%)
  between operations  14 us (6%)
  blocking collectives  11.4 us (5%)
  matrix products  7.82 us (3%)
  other arithmetic  2.99 us (1%)
    ppermute x11, waiting for transfers between devices, moved(): return lax.ppermute(v, AXES, pairs)  77.6 us
    ppermute x11, starting transfers between devices, moved(): return lax.ppermute(v, AXES, pairs)  59.9 us
    all_to_all x6, waiting for transfers between devices, to_all(): return lax.all_to_all(v, axis, 0, 0, tiled=True)  31.7 us
    all_to_all x6, starting transfers between devices, to_all(): return lax.all_to_all(v, axis, 0, 0, tiled=True)  26.8 us
    all_to_all x1, blocking collectives, to_all(): return lax.all_to_all(v, axis, 0, 0, tiled=True)  11.4 us
    dot_general x10, matrix products, dot(): lax.dot_general(a, b, (contract, ((), ())), precision=PREC, preferred_ele...  7.82 us
  transfers between devices with their start and end apart: 18, of which 13 were waited for; matrix products, arithmetic and copies ran while one was open for 7% of the time, Pallas kernels for 0%

profile of v4, /device:TPU:34, one launch (start us, length us, event | category | flops | bytes accessed | tf_op | source)
XLA Modules:
  0.0 248.7 jit_solution(12285763293605978561)
XLA Ops:
  8.7 4.8 %all-to-all-start = ((f32[4,256,256]{1,2,0:T(8,128)}), f32[4,256,256]{1,2,0:T(8,128)S(1)}, u32[]{:S(2)}, u32[]{:S(2)}) async-start(f32[4,256,256]{1,2,0:T(8,128)} %broadcast_in_dim.19), calls=%async_computation | async-start | bytes 2097152 | tf_op jit(solution)/shard_map/all_to_all | solution.py:45
  14.7 1.9 collective-permute-start
  16.8 1.3 collective-permute-done
  21.3 5.9 %all-to-all-done = f32[4,256,256]{1,2,0:T(8,128)S(1)} async-done(((f32[4,256,256]{1,2,0:T(8,128)}), f32[4,256,256]{1,2,0:T(8,128)S(1)}, u32[]{:S(2)}, u32[]{:S(2)}) %all-to-all-start) | async-done | bytes 1048608 | tf_op jit(solution)/shard_map/all_to_all | solution.py:45
  27.2 1.9 collective-permute-start.1
  29.1 4.5 %all-to-all-start.1 = ((f32[4,2,64,256]{3,2,1,0:T(8,128)}), f32[4,2,64,256]{3,2,1,0:T(8,128)S(1)}, u32[]{:S(2)}, u32[]{:S(2)}) async-start(f32[4,2,64,256]{3,2,1,0:T(8,128)} %broadcast_in_dim.23), calls=%async_computation.1 | async-start | bytes 1048576 | tf_op jit(solution)/shard_map/all_to_all | solution.py:45
  34.3 9.4 %all-to-all-done.1 = f32[4,2,64,256]{3,2,1,0:T(8,128)S(1)} async-done(((f32[4,2,64,256]{3,2,1,0:T(8,128)}), f32[4,2,64,256]{3,2,1,0:T(8,128)S(1)}, u32[]{:S(2)}, u32[]{:S(2)}) %all-to-all-start.1) | async-done | bytes 524320 | tf_op jit(solution)/shard_map/all_to_all | solution.py:45
  45.1 2.0 collective-permute-start.2
  48.4 7.7 %collective-permute-done.2 = f32[128,1024]{1,0:T(8,128)S(1)} collective-permute-done((f32[128,1024]{1,0:T(8,128)S(1)}, f32[128,1024]{1,0:T(8,128)S(1)}, u32[]{:S(2)}, u32[]{:S(2)}) %collective-permute-start.2) | collective-permute-done | bytes 524320 | tf_op jit(solution)/shard_map/ppermute | solution.py:25
  56.2 5.2 %collective-permute-start.3 = (f32[64,1024]{1,0:T(8,128)S(1)}, f32[64,1024]{1,0:T(8,128)S(1)}, u32[]{:S(2)}, u32[]{:S(2)}) collective-permute-start(f32[64,1024]{1,0:T(8,128)S(1)} %get-tuple-element.30), channel_id=1, source_target_pairs={{0,128},{2,130},{4,132},{6,134},{8,136},{10,138},{12,140},{14,142}... | collective-permute-start | bytes 786440 | tf_op jit(solution)/shard_map/ppermute | solution.py:25
  61.5 17.5 %collective-permute-done.3 = f32[64,1024]{1,0:T(8,128)S(1)} collective-permute-done((f32[64,1024]{1,0:T(8,128)S(1)}, f32[64,1024]{1,0:T(8,128)S(1)}, u32[]{:S(2)}, u32[]{:S(2)}) %collective-permute-start.3) | collective-permute-done | bytes 262176 | tf_op jit(solution)/shard_map/ppermute | solution.py:25
  79.0 10.8 %collective-permute-start.4 = (f32[32,1024]{1,0:T(8,128)S(1)}, f32[32,1024]{1,0:T(8,128)S(1)}, u32[]{:S(2)}, u32[]{:S(2)}) collective-permute-start(f32[32,1024]{1,0:T(8,128)S(1)} %dynamic-slice_add_fusion.2), channel_id=1, source_target_pairs={{0,256},{2,258},{4,260},{6,262},{8,264},{10,266},{12,268},{14,270}... | collective-permute-start | bytes 393224 | tf_op jit(solution)/shard_map/ppermute | solution.py:25
  91.2 7.0 %collective-permute-done.4 = f32[32,1024]{1,0:T(8,128)S(1)} collective-permute-done((f32[32,1024]{1,0:T(8,128)S(1)}, f32[32,1024]{1,0:T(8,128)S(1)}, u32[]{:S(2)}, u32[]{:S(2)}) %collective-permute-start.4) | collective-permute-done | bytes 131104 | tf_op jit(solution)/shard_map/ppermute | solution.py:25
  98.4 5.1 %collective-permute-start.5 = (f32[32,1024]{1,0:T(8,128)S(1)}, f32[32,1024]{1,0:T(8,128)S(1)}, u32[]{:S(2)}, u32[]{:S(2)}) collective-permute-start(f32[32,1024]{1,0:T(8,128)S(1)} %compare_select_fusion), channel_id=1, source_target_pairs={{0,256},{2,258},{4,260},{6,262},{8,264},{10,266},{12,268},{14,270}... | collective-permute-start | bytes 393224 | tf_op jit(solution)/shard_map/ppermute | solution.py:25
  103.5 17.7 %collective-permute-done.5 = f32[32,1024]{1,0:T(8,128)S(1)} collective-permute-done((f32[32,1024]{1,0:T(8,128)S(1)}, f32[32,1024]{1,0:T(8,128)S(1)}, u32[]{:S(2)}, u32[]{:S(2)}) %collective-permute-start.5) | collective-permute-done | bytes 131104 | tf_op jit(solution)/shard_map/ppermute | solution.py:25
  121.3 1.9 collective-permute-start.6
  123.2 1.3 copy.25
  124.6 7.4 %collective-permute-done.6 = f32[64,1024]{1,0:T(8,128)S(1)} collective-permute-done((f32[64,1024]{1,0:T(8,128)S(1)}, f32[64,1024]{1,0:T(8,128)S(1)}, u32[]{:S(2)}, u32[]{:S(2)}) %collective-permute-start.6) | collective-permute-done | bytes 262176 | tf_op jit(solution)/shard_map/ppermute | solution.py:25
  132.8 3.5 %all-to-all-start.2 = ((f32[4,2,64,256]{3,2,1,0:T(8,128)}), f32[4,2,64,256]{3,2,1,0:T(8,128)S(1)}, u32[]{:S(2)}, u32[]{:S(2)}) async-start(f32[4,2,64,256]{3,2,1,0:T(8,128)} %dynamic-slice_bitcast_fusion), calls=%async_computation.2 | async-start | bytes 1048576 | tf_op jit(solution)/shard_map/all_to_all | solution.py:45
  136.3 10.7 %collective-permute-start.7 = (f32[128,1024]{1,0:T(8,128)S(1)}, f32[128,1024]{1,0:T(8,128)S(1)}, u32[]{:S(2)}, u32[]{:S(2)}) collective-permute-start(f32[128,1024]{1,0:T(8,128)S(1)} %maximum_select_fusion.1), channel_id=1, source_target_pairs={{0,64},{2,66},{4,68},{6,70},{8,72},{10,74},{12,76},{14,78},{16,80}... | collective-permute-start | bytes 1572872 | tf_op jit(solution)/shard_map/ppermute | solution.py:25
  149.0 5.1 %collective-permute-done.7 = f32[128,1024]{1,0:T(8,128)S(1)} collective-permute-done((f32[128,1024]{1,0:T(8,128)S(1)}, f32[128,1024]{1,0:T(8,128)S(1)}, u32[]{:S(2)}, u32[]{:S(2)}) %collective-permute-start.7) | collective-permute-done | bytes 524320 | tf_op jit(solution)/shard_map/ppermute | solution.py:25
  157.0 3.9 %collective-permute-start.8 = (f32[4,2,64,256]{3,2,1,0:T(8,128)S(1)}, f32[4,2,64,256]{3,2,1,0:T(8,128)S(1)}, u32[]{:S(2)}, u32[]{:S(2)}) collective-permute-start(f32[4,2,64,256]{3,2,1,0:T(8,128)S(1)} %all-to-all-done.2), channel_id=1, source_target_pairs={{0,64},{2,66},{4,68},{6,70},{8,72},{10,74},{12,76},{14,78},{16,80}... | collective-permute-start | bytes 1572872 | tf_op jit(solution)/shard_map/ppermute | solution.py:25
  160.9 4.8 %all-to-all-start.3 = ((f32[4,128,256]{2,1,0:T(8,128)}), f32[4,128,256]{2,1,0:T(8,128)S(1)}, u32[]{:S(2)}, u32[]{:S(2)}) async-start(f32[4,128,256]{2,1,0:T(8,128)} %bitcast.17), calls=%async_computation.3 | async-start | bytes 1048576 | tf_op jit(solution)/shard_map/all_to_all | solution.py:45
  165.7 9.7 %all-to-all-done.3 = f32[4,128,256]{2,1,0:T(8,128)S(1)} async-done(((f32[4,128,256]{2,1,0:T(8,128)}), f32[4,128,256]{2,1,0:T(8,128)S(1)}, u32[]{:S(2)}, u32[]{:S(2)}) %all-to-all-start.3) | async-done | bytes 524320 | tf_op jit(solution)/shard_map/all_to_all | solution.py:45
  176.3 4.3 %all-to-all-start.4 = ((f32[4,128,256]{2,1,0:T(8,128)}), f32[4,128,256]{2,1,0:T(8,128)}, u32[]{:S(2)}, u32[]{:S(2)}) async-start(f32[4,128,256]{2,1,0:T(8,128)} %broadcast_in_dim.26), calls=%async_computation.4 | async-start | bytes 1048576 | tf_op jit(solution)/shard_map/all_to_all | solution.py:45
  184.8 6.6 %all-to-all-done.4 = f32[4,128,256]{2,1,0:T(8,128)} async-done(((f32[4,128,256]{2,1,0:T(8,128)}), f32[4,128,256]{2,1,0:T(8,128)}, u32[]{:S(2)}, u32[]{:S(2)}) %all-to-all-start.4) | async-done | bytes 524320 | tf_op jit(solution)/shard_map/all_to_all | solution.py:45
  193.1 2.0 collective-permute-start.9
  195.2 2.5 %collective-permute-done.9 = f32[4,256,256]{2,1,0:T(8,128)S(1)} collective-permute-done((f32[4,256,256]{2,1,0:T(8,128)S(1)}, f32[4,256,256]{2,1,0:T(8,128)S(1)}, u32[]{:S(2)}, u32[]{:S(2)}) %collective-permute-start.9) | collective-permute-done | bytes 1048608 | tf_op jit(solution)/shard_map/ppermute | solution.py:25
  199.2 11.4 %all_to_all.35 = f32[4,128,256]{2,1,0:T(8,128)S(1)} all-to-all(f32[4,128,256]{2,1,0:T(8,128)S(1)} %get-tuple-element.25), channel_id=1, replica_groups=mesh['zq'=4,'zp'=2,'co'=2,'y'=4,'x'=4,'zh'=2] {'x'}, dimensions={0} | all-to-all | bytes 1048576 | tf_op jit(solution)/shard_map/all_to_all | solution.py:45
  210.6 4.9 %all-to-all-start.6 = ((f32[4,128,256]{2,1,0:T(8,128)}), f32[4,128,256]{2,1,0:T(8,128)S(1)}, u32[]{:S(2)}, u32[]{:S(2)}) async-start(f32[4,128,256]{2,1,0:T(8,128)} %get-tuple-element.23), calls=%async_computation.6 | async-start | bytes 1048576 | tf_op jit(solution)/shard_map/all_to_all | solution.py:45
  215.5 14.5 %collective-permute-start.10 = (f32[128,256]{1,0:T(8,128)S(1)}, f32[128,256]{1,0:T(8,128)S(1)}, u32[]{:S(2)}, u32[]{:S(2)}) collective-permute-start(f32[128,256]{1,0:T(8,128)S(1)} %reduce_sum.28), channel_id=1, source_target_pairs={{0,1},{2,3},{4,5},{6,7},{8,9},{10,11},{12,13},{14,15},{16,17},{18,... | collective-permute-start | bytes 393224 | tf_op jit(solution)/shard_map/ppermute | solution.py:25
  230.1 11.2 %collective-permute-done.10 = f32[128,256]{1,0:T(8,128)S(1)} collective-permute-done((f32[128,256]{1,0:T(8,128)S(1)}, f32[128,256]{1,0:T(8,128)S(1)}, u32[]{:S(2)}, u32[]{:S(2)}) %collective-permute-start.10) | collective-permute-done | bytes 131104 | tf_op jit(solution)/shard_map/ppermute | solution.py:25
  (82 shorter events, 26.1 us)
Async XLA Ops:
  8.7 18.5 %all-to-all-start = ((f32[4,256,256]{1,2,0:T(8,128)}), f32[4,256,256]{1,2,0:T(8,128)S(1)}, u32[]{:S(2)}, u32[]{:S(2)}) async-start(f32[4,256,256]{1,2,0:T(8,128)} %broadcast_in_dim.19), calls=%async_computation | async-start | bytes 2097152 | tf_op jit(solution)/shard_map/all_to_all | solution.py:45
  13.5 0.9 copy-start.1
  14.7 3.3 %collective-permute-start = (f32[192,256]{1,0:T(8,128)S(1)}, f32[192,256]{1,0:T(8,128)S(1)}, u32[]{:S(2)}, u32[]{:S(2)}) collective-permute-start(f32[192,256]{1,0:T(8,128)S(1)} %pad_maximum_fusion.1), channel_id=1, source_target_pairs={{0,32},{2,34},{4,36},{6,38},{8,40},{10,42},{12,44},{14,46},{16,48}... | collective-permute-start | bytes 589832 | tf_op jit(solution)/shard_map/ppermute | solution.py:25
  18.1 0.7 copy-start
  18.8 0.9 slice-start
  27.2 17.2 %collective-permute-start.1 = (f32[256,1024]{0,1:T(8,128)S(1)}, f32[256,1024]{0,1:T(8,128)S(1)}, u32[]{:S(2)}, u32[]{:S(2)}) collective-permute-start(f32[256,1024]{0,1:T(8,128)S(1)} %bitcast.63), channel_id=1, source_target_pairs={{0,32},{2,34},{4,36},{6,38},{8,40},{10,42},{12,44},{14,46},{16,48}... | collective-permute-start | bytes 3145736 | tf_op jit(solution)/shard_map/ppermute | solution.py:25
  29.1 14.6 %all-to-all-start.1 = ((f32[4,2,64,256]{3,2,1,0:T(8,128)}), f32[4,2,64,256]{3,2,1,0:T(8,128)S(1)}, u32[]{:S(2)}, u32[]{:S(2)}) async-start(f32[4,2,64,256]{3,2,1,0:T(8,128)} %broadcast_in_dim.23), calls=%async_computation.1 | async-start | bytes 1048576 | tf_op jit(solution)/shard_map/all_to_all | solution.py:45
  33.6 89.6 %all-gather.3.cloned.1.call-start = ((), (), s32[]{:S(2)}) async-start(), calls=%async_computation.7 | async-start | bytes 1310720 | tf_op jit(solution)/shard_map/all_gather | solution.py:102
  45.1 11.1 %collective-permute-start.2 = (f32[128,1024]{1,0:T(8,128)S(1)}, f32[128,1024]{1,0:T(8,128)S(1)}, u32[]{:S(2)}, u32[]{:S(2)}) collective-permute-start(f32[128,1024]{1,0:T(8,128)S(1)} %convolution_add_fusion), channel_id=1, source_target_pairs={{0,64},{2,66},{4,68},{6,70},{8,72},{10,74},{12,76},{14,78},{16,80}... | collective-permute-start | bytes 1572872 | tf_op jit(solution)/shard_map/ppermute | solution.py:25
  56.2 22.8 %collective-permute-start.3 = (f32[64,1024]{1,0:T(8,128)S(1)}, f32[64,1024]{1,0:T(8,128)S(1)}, u32[]{:S(2)}, u32[]{:S(2)}) collective-permute-start(f32[64,1024]{1,0:T(8,128)S(1)} %get-tuple-element.30), channel_id=1, source_target_pairs={{0,128},{2,130},{4,132},{6,134},{8,136},{10,138},{12,140},{14,142}... | collective-permute-start | bytes 786440 | tf_op jit(solution)/shard_map/ppermute | solution.py:25
  79.0 10.8 %copy-start.3 = (s32[4096]{0:T(1024)S(1)}, s32[4096]{0:T(1024)}, u32[]{:S(2)}) copy-start(s32[4096]{0:T(1024)} %param.9) | copy-start | bytes 49156
  79.0 10.8 %copy-start.4 = (s32[4096]{0:T(1024)S(1)}, s32[4096]{0:T(1024)}, u32[]{:S(2)}) copy-start(s32[4096]{0:T(1024)} %param.8) | copy-start | bytes 49156
  79.0 19.2 %collective-permute-start.4 = (f32[32,1024]{1,0:T(8,128)S(1)}, f32[32,1024]{1,0:T(8,128)S(1)}, u32[]{:S(2)}, u32[]{:S(2)}) collective-permute-start(f32[32,1024]{1,0:T(8,128)S(1)} %dynamic-slice_add_fusion.2), channel_id=1, source_target_pairs={{0,256},{2,258},{4,260},{6,262},{8,264},{10,266},{12,268},{14,270}... | collective-permute-start | bytes 393224 | tf_op jit(solution)/shard_map/ppermute | solution.py:25
  89.8 1.4 copy-start.2
  90.0 0.7 copy-start.5
  91.2 7.0 %dynamic-slice-start = ((f32[4096]{0:T(1024)}, s32[]{:T(128)}), f32[1024]{0:T(1024)S(1)}, s32[]{:S(2)}) async-start(f32[4096]{0:T(1024)} %copy-done.2, s32[]{:T(128)} %select_n.179), calls=%async_computation.9 | async-start | bytes 8704 | tf_op jit(solution)/shard_map/dynamic_slice | solution.py:64
  98.4 22.9 %collective-permute-start.5 = (f32[32,1024]{1,0:T(8,128)S(1)}, f32[32,1024]{1,0:T(8,128)S(1)}, u32[]{:S(2)}, u32[]{:S(2)}) collective-permute-start(f32[32,1024]{1,0:T(8,128)S(1)} %compare_select_fusion), channel_id=1, source_target_pairs={{0,256},{2,258},{4,260},{6,262},{8,264},{10,266},{12,268},{14,270}... | collective-permute-start | bytes 393224 | tf_op jit(solution)/shard_map/ppermute | solution.py:25
  121.3 10.7 %collective-permute-start.6 = (f32[64,1024]{1,0:T(8,128)S(1)}, f32[64,1024]{1,0:T(8,128)S(1)}, u32[]{:S(2)}, u32[]{:S(2)}) collective-permute-start(f32[64,1024]{1,0:T(8,128)S(1)} %maximum_select_fusion.3), channel_id=1, source_target_pairs={{0,128},{2,130},{4,132},{6,134},{8,136},{10,138},{12,140},{14,142}... | collective-permute-start | bytes 786440 | tf_op jit(solution)/shard_map/ppermute | solution.py:25
  132.8 24.1 %all-to-all-start.2 = ((f32[4,2,64,256]{3,2,1,0:T(8,128)}), f32[4,2,64,256]{3,2,1,0:T(8,128)S(1)}, u32[]{:S(2)}, u32[]{:S(2)}) async-start(f32[4,2,64,256]{3,2,1,0:T(8,128)} %dynamic-slice_bitcast_fusion), calls=%async_computation.2 | async-start | bytes 1048576 | tf_op jit(solution)/shard_map/all_to_all | solution.py:45
  136.3 17.8 %collective-permute-start.7 = (f32[128,1024]{1,0:T(8,128)S(1)}, f32[128,1024]{1,0:T(8,128)S(1)}, u32[]{:S(2)}, u32[]{:S(2)}) collective-permute-start(f32[128,1024]{1,0:T(8,128)S(1)} %maximum_select_fusion.1), channel_id=1, source_target_pairs={{0,64},{2,66},{4,68},{6,70},{8,72},{10,74},{12,76},{14,78},{16,80}... | collective-permute-start | bytes 1572872 | tf_op jit(solution)/shard_map/ppermute | solution.py:25
  157.0 23.7 %collective-permute-start.8 = (f32[4,2,64,256]{3,2,1,0:T(8,128)S(1)}, f32[4,2,64,256]{3,2,1,0:T(8,128)S(1)}, u32[]{:S(2)}, u32[]{:S(2)}) collective-permute-start(f32[4,2,64,256]{3,2,1,0:T(8,128)S(1)} %all-to-all-done.2), channel_id=1, source_target_pairs={{0,64},{2,66},{4,68},{6,70},{8,72},{10,74},{12,76},{14,78},{16,80}... | collective-permute-start | bytes 1572872 | tf_op jit(solution)/shard_map/ppermute | solution.py:25
  160.9 14.6 %all-to-all-start.3 = ((f32[4,128,256]{2,1,0:T(8,128)}), f32[4,128,256]{2,1,0:T(8,128)S(1)}, u32[]{:S(2)}, u32[]{:S(2)}) async-start(f32[4,128,256]{2,1,0:T(8,128)} %bitcast.17), calls=%async_computation.3 | async-start | bytes 1048576 | tf_op jit(solution)/shard_map/all_to_all | solution.py:45
  176.3 15.1 %all-to-all-start.4 = ((f32[4,128,256]{2,1,0:T(8,128)}), f32[4,128,256]{2,1,0:T(8,128)}, u32[]{:S(2)}, u32[]{:S(2)}) async-start(f32[4,128,256]{2,1,0:T(8,128)} %broadcast_in_dim.26), calls=%async_computation.4 | async-start | bytes 1048576 | tf_op jit(solution)/shard_map/all_to_all | solution.py:45
  193.1 4.6 %collective-permute-start.9 = (f32[4,256,256]{2,1,0:T(8,128)S(1)}, f32[4,256,256]{2,1,0:T(8,128)S(1)}, u32[]{:S(2)}, u32[]{:S(2)}) collective-permute-start(f32[4,256,256]{2,1,0:T(8,128)S(1)} %convolution_bitcast_fusion), channel_id=1, source_target_pairs={{0,32},{2,34},{4,36},{6,38},{8,40},{10,42},{12,44},{14,46},{16,48}... | collective-permute-start | bytes 3145736 | tf_op jit(solution)/shard_map/ppermute | solution.py:25
  210.6 19.4 %all-to-all-start.6 = ((f32[4,128,256]{2,1,0:T(8,128)}), f32[4,128,256]{2,1,0:T(8,128)S(1)}, u32[]{:S(2)}, u32[]{:S(2)}) async-start(f32[4,128,256]{2,1,0:T(8,128)} %get-tuple-element.23), calls=%async_computation.6 | async-start | bytes 1048576 | tf_op jit(solution)/shard_map/all_to_all | solution.py:45
  215.5 25.7 %collective-permute-start.10 = (f32[128,256]{1,0:T(8,128)S(1)}, f32[128,256]{1,0:T(8,128)S(1)}, u32[]{:S(2)}, u32[]{:S(2)}) collective-permute-start(f32[128,256]{1,0:T(8,128)S(1)} %reduce_sum.28), channel_id=1, source_target_pairs={{0,1},{2,3},{4,5},{6,7},{8,9},{10,11},{12,13},{14,15},{16,17},{18,... | collective-permute-start | bytes 393224 | tf_op jit(solution)/shard_map/ppermute | solution.py:25
Sparse Core Ops, SparseCore 0:
  36.5 61.8 all-gather.2

commit v5 on v3

--- a/solution.py
+++ b/solution.py
@@ -95,16 +95,15 @@
 
     wide = sent_to_all(basis, "x")
     grads = jnp.broadcast_to(jnp.stack([own[0], other[0]])[None], (4, 2, quarter, n))
+
     far = joined(own[1][None], other[1][None], co)
     far = joined(far[None], moved(far, along(4))[None], bits[2])
     wide, grads, far = tied(wide, grads, far)
     (wide,) = tied(wide.swapaxes(0, 1).reshape(n, 4 * n))
     wide_oth = moved(wide, other_core)
     grads = to_all(grads, "y")
-
     far = joined(far[:, None], moved(far, along(2))[:, None], bits[1], 1)
     grads, far = tied(grads, far.reshape(4, 2, quarter, n))
-    far = turned_round(far, (4 - co * ((SHIFT + bits[0]) // 2)) % 4)
 
     def inner_of(which):
         g = part(grads, which, 2)
@@ -112,6 +111,7 @@
 
     got = moved(inner_of(1 - bits[0]), along(1))
     kept = inner_of(bits[0])
+    far = turned_round(far, (4 - co * ((SHIFT + bits[0]) // 2)) % 4)
     rows = half
     for distance, bit in ((2, bits[1]), (4, bits[2])):
         rows //= 2
@@ -139,24 +139,27 @@
     scaled_oth = moved(scaled, along(1))
 
     def left_of(s):
-        return jnp.concatenate([dot(w, s, ((1,), (1,))) for w in (wide, wide_oth)])
+        terms = [dot(w, s, ((1,), (1,))).reshape(2, half, half) for w in (wide, wide_oth)]
+        return to_all(jnp.concatenate(terms), "y")
 
-    left = jnp.concatenate([left_of(scaled), left_of(scaled_oth)], 1)
-    left, far = tied(left, far)
+    left = left_of(scaled)
+    scaled_oth, left, far = tied(scaled_oth, left, far)
     far_oth = moved(far, along(1))
-    left = to_all(left.reshape(4, half, n), "y").sum(0)
-    left = sent_to_all(left, "y").reshape(2 * n, n)
+    left = jnp.concatenate([left.sum(0), left_of(scaled_oth).sum(0)], 1)
+    left = sent_to_all(left, "y")
 
     far = joined(far[None], far_oth[None], z % 2)
     far = far.transpose(1, 3, 0, 2, 4).reshape(2, half, 4 * n)
     (far,) = tied(jnp.where(bits[0] == 1, jnp.stack([far[1], far[0]]), far).reshape(n, 4 * n))
 
-    def product(rows_of):
-        return dot(rows_of, far).reshape(n, 4, n).swapaxes(0, 1)
+    def product(core, which):
+        rows_of = lax.dynamic_index_in_dim(left, 2 * core + which, 0, False)
+        return dot(rows_of, far).reshape(half, 4, n).swapaxes(0, 1)
 
-    theirs_out = moved(product(left[n:]), other_core)
-    out = to_all(product(left[:n]) + theirs_out, "x").sum(0)
-    return part(out, zh, half) + moved(part(out, 1 - zh, half), other_layer)
+    leaving = product(0, 1 - zh) + moved(product(1, 1 - zh), other_core)
+    leaving = to_all(leaving, "x").sum(0)
+    staying, leaving = tied(moved(product(1, zh), other_core), leaving)
+    return to_all(product(0, zh) + staying, "x").sum(0) + moved(leaving, other_layer)
 
 
 def solution(mesh):

time: 212 us -> 219 us (1.033)
  the two profiles are of different devices: /device:TPU:64 before, /device:TPU:2 now
where the time goes in v5:
time: 219 us; the launch traced here: 218 us
  starting transfers between devices  94 us (43%)
  waiting for transfers between devices  80.8 us (37%)
  matrix products  12.9 us (6%)
  local copies, waits for them, and re-layouts  11.5 us (5%)
  blocking collectives  11.2 us (5%)
  other arithmetic  6.85 us (3%)
    ppermute x14, waiting for transfers between devices, moved(): return lax.ppermute(v, AXES, pairs)  63.8 us
    ppermute x14, starting transfers between devices, moved(): return lax.ppermute(v, AXES, pairs)  54.3 us
    all_to_all x7, starting transfers between devices, to_all(): return lax.all_to_all(v, axis, 0, 0, tiled=True)  39.6 us
    all_to_all x7, waiting for transfers between devices, to_all(): return lax.all_to_all(v, axis, 0, 0, tiled=True)  17.1 us
    dot_general x12, matrix products, dot(): lax.dot_general(a, b, (contract, ((), ())), precision=PREC, preferred_ele...  12.9 us
    all_to_all x1, blocking collectives, to_all(): return lax.all_to_all(v, axis, 0, 0, tiled=True)  11.2 us
  transfers between devices with their start and end apart: 21, of which 12 were waited for; matrix products, arithmetic and copies ran while one was open for 10% of the time, Pallas kernels for 0%

profile of v5, /device:TPU:2, one launch (start us, length us, event | category | flops | bytes accessed | tf_op | source)
XLA Modules:
  0.0 218.1 jit_solution(4270728548382313305)
XLA Ops:
  1.3 1.9 collective-permute-start
  4.3 9.4 %all-to-all-start = ((f32[4,256,256]{1,2,0:T(8,128)}), f32[4,256,256]{1,2,0:T(8,128)S(1)}, u32[]{:S(2)}, u32[]{:S(2)}) async-start(f32[4,256,256]{1,2,0:T(8,128)} %broadcast_in_dim.29), calls=%async_computation | async-start | bytes 2097152 | tf_op jit(solution)/shard_map/all_to_all | solution.py:45
  13.8 4.5 %collective-permute-start.1 = (f32[2,64,256]{2,1,0:T(8,128)S(1)}, f32[2,64,256]{2,1,0:T(8,128)S(1)}, u32[]{:S(2)}, u32[]{:S(2)}) collective-permute-start(f32[2,64,256]{2,1,0:T(8,128)S(1)} %maximum_select_fusion.5), channel_id=1, source_target_pairs={{0,256},{2,258},{4,260},{6,262},{8,264},{10,266},{12,268},{14,270}... | collective-permute-start | bytes 393224 | tf_op jit(solution)/shard_map/ppermute | solution.py:25
  18.4 9.1 %collective-permute-done.1 = f32[2,64,256]{2,1,0:T(8,128)S(1)} collective-permute-done((f32[2,64,256]{2,1,0:T(8,128)S(1)}, f32[2,64,256]{2,1,0:T(8,128)S(1)}, u32[]{:S(2)}, u32[]{:S(2)}) %collective-permute-start.1) | collective-permute-done | bytes 131104 | tf_op jit(solution)/shard_map/ppermute | solution.py:25
  31.1 3.5 %all-to-all-start.1 = ((f32[4,2,64,256]{3,2,1,0:T(8,128)}), f32[4,2,64,256]{3,2,1,0:T(8,128)S(1)}, u32[]{:S(2)}, u32[]{:S(2)}) async-start(f32[4,2,64,256]{3,2,1,0:T(8,128)} %broadcast_in_dim.30), calls=%async_computation.1 | async-start | bytes 1048576 | tf_op jit(solution)/shard_map/all_to_all | solution.py:45
  34.6 3.2 %collective-permute-start.2 = (f32[2,2,64,256]{3,2,1,0:T(8,128)S(1)}, f32[2,2,64,256]{3,2,1,0:T(8,128)S(1)}, u32[]{:S(2)}, u32[]{:S(2)}) collective-permute-start(f32[2,2,64,256]{3,2,1,0:T(8,128)S(1)} %maximum_select_fusion.3), channel_id=1, source_target_pairs={{0,128},{2,130},{4,132},{6,134},{8,136},{10,138},{12,140},{14,142}... | collective-permute-start | bytes 786440 | tf_op jit(solution)/shard_map/ppermute | solution.py:25
  37.8 11.1 %collective-permute-done.2 = f32[2,2,64,256]{3,2,1,0:T(8,128)S(1)} collective-permute-done((f32[2,2,64,256]{3,2,1,0:T(8,128)S(1)}, f32[2,2,64,256]{3,2,1,0:T(8,128)S(1)}, u32[]{:S(2)}, u32[]{:S(2)}) %collective-permute-start.2) | collective-permute-done | bytes 262176 | tf_op jit(solution)/shard_map/ppermute | solution.py:25
  52.2 1.9 collective-permute-start.4
  55.4 7.8 %collective-permute-done.4 = f32[128,1024]{1,0:T(8,128)S(1)} collective-permute-done((f32[128,1024]{1,0:T(8,128)S(1)}, f32[128,1024]{1,0:T(8,128)S(1)}, u32[]{:S(2)}, u32[]{:S(2)}) %collective-permute-start.4) | collective-permute-done | bytes 524320 | tf_op jit(solution)/shard_map/ppermute | solution.py:25
  63.3 2.8 %collective-permute-start.5 = (f32[64,1024]{1,0:T(8,128)S(1)}, f32[64,1024]{1,0:T(8,128)S(1)}, u32[]{:S(2)}, u32[]{:S(2)}) collective-permute-start(f32[64,1024]{1,0:T(8,128)S(1)} %get-tuple-element.32), channel_id=1, source_target_pairs={{0,128},{2,130},{4,132},{6,134},{8,136},{10,138},{12,140},{14,142}... | collective-permute-start | bytes 786440 | tf_op jit(solution)/shard_map/ppermute | solution.py:25
  66.2 11.3 %collective-permute-done.5 = f32[64,1024]{1,0:T(8,128)S(1)} collective-permute-done((f32[64,1024]{1,0:T(8,128)S(1)}, f32[64,1024]{1,0:T(8,128)S(1)}, u32[]{:S(2)}, u32[]{:S(2)}) %collective-permute-start.5) | collective-permute-done | bytes 262176 | tf_op jit(solution)/shard_map/ppermute | solution.py:25
  77.6 5.0 %collective-permute-start.6 = (f32[32,1024]{1,0:T(8,128)S(1)}, f32[32,1024]{1,0:T(8,128)S(1)}, u32[]{:S(2)}, u32[]{:S(2)}) collective-permute-start(f32[32,1024]{1,0:T(8,128)S(1)} %dynamic-slice_add_fusion.2), channel_id=1, source_target_pairs={{0,256},{2,258},{4,260},{6,262},{8,264},{10,266},{12,268},{14,270}... | collective-permute-start | bytes 393224 | tf_op jit(solution)/shard_map/ppermute | solution.py:25
  84.8 5.4 %collective-permute-done.6 = f32[32,1024]{1,0:T(8,128)S(1)} collective-permute-done((f32[32,1024]{1,0:T(8,128)S(1)}, f32[32,1024]{1,0:T(8,128)S(1)}, u32[]{:S(2)}, u32[]{:S(2)}) %collective-permute-start.6) | collective-permute-done | bytes 131104 | tf_op jit(solution)/shard_map/ppermute | solution.py:25
  90.3 6.1 %collective-permute-start.7 = (f32[32,1024]{1,0:T(8,128)S(1)}, f32[32,1024]{1,0:T(8,128)S(1)}, u32[]{:S(2)}, u32[]{:S(2)}) collective-permute-start(f32[32,1024]{1,0:T(8,128)S(1)} %compare_select_fusion), channel_id=1, source_target_pairs={{0,256},{2,258},{4,260},{6,262},{8,264},{10,266},{12,268},{14,270}... | collective-permute-start | bytes 393224 | tf_op jit(solution)/shard_map/ppermute | solution.py:25
  96.4 5.5 %collective-permute-done.7 = f32[32,1024]{1,0:T(8,128)S(1)} collective-permute-done((f32[32,1024]{1,0:T(8,128)S(1)}, f32[32,1024]{1,0:T(8,128)S(1)}, u32[]{:S(2)}, u32[]{:S(2)}) %collective-permute-start.7) | collective-permute-done | bytes 131104 | tf_op jit(solution)/shard_map/ppermute | solution.py:25
  101.9 1.9 collective-permute-start.8
  103.8 6.9 %all-to-all-start.3 = ((f32[4,2,64,256]{3,2,1,0:T(8,128)}), f32[4,2,64,256]{3,2,1,0:T(8,128)S(1)}, u32[]{:S(2)}, u32[]{:S(2)}) async-start(f32[4,2,64,256]{3,2,1,0:T(8,128)} %fusion.2), calls=%async_computation.3 | async-start | bytes 1048576 | tf_op jit(solution)/shard_map/all_to_all | solution.py:45
  113.2 6.8 %collective-permute-start.9 = (f32[128,1024]{1,0:T(8,128)S(1)}, f32[128,1024]{1,0:T(8,128)}, u32[]{:S(2)}, u32[]{:S(2)}) collective-permute-start(f32[128,1024]{1,0:T(8,128)S(1)} %maximum_select_fusion.2), channel_id=1, source_target_pairs={{0,64},{2,66},{4,68},{6,70},{8,72},{10,74},{12,76},{14,78},{16,80}... | collective-permute-start | bytes 1572872 | tf_op jit(solution)/shard_map/ppermute | solution.py:25
  121.8 11.2 %all_to_all.40 = f32[4,128,128]{2,1,0:T(8,128)S(1)} all-to-all(f32[4,128,128]{2,1,0:T(8,128)} %pad_maximum_fusion.1), channel_id=1, replica_groups=mesh['zl'=8,'co'=2,'y'=4,'x'=4,'zh'=2] {'y'}, dimensions={0} | all-to-all | bytes 524288 | tf_op jit(solution)/shard_map/all_to_all | solution.py:45
  133.0 2.0 fusion.30
  135.0 3.9 %collective-permute-start.10 = (f32[4,2,64,256]{3,2,1,0:T(8,128)S(1)}, f32[4,2,64,256]{3,2,1,0:T(8,128)S(1)}, u32[]{:S(2)}, u32[]{:S(2)}) collective-permute-start(f32[4,2,64,256]{3,2,1,0:T(8,128)S(1)} %all-to-all-done.3), channel_id=1, source_target_pairs={{0,64},{2,66},{4,68},{6,70},{8,72},{10,74},{12,76},{14,78},{16,80}... | collective-permute-start | bytes 1572872 | tf_op jit(solution)/shard_map/ppermute | solution.py:25
  139.0 2.0 fusion.31
  141.7 3.4 %all-to-all-start.4 = ((f32[4,128,128]{2,1,0:T(8,128)}), f32[4,128,128]{2,1,0:T(8,128)S(1)}, u32[]{:S(2)}, u32[]{:S(2)}) async-start(f32[4,128,128]{2,1,0:T(8,128)} %pad_maximum_fusion.2), calls=%async_computation.4 | async-start | bytes 524288 | tf_op jit(solution)/shard_map/all_to_all | solution.py:45
  145.2 6.6 %all-to-all-done.4 = f32[4,128,128]{2,1,0:T(8,128)S(1)} async-done(((f32[4,128,128]{2,1,0:T(8,128)}), f32[4,128,128]{2,1,0:T(8,128)S(1)}, u32[]{:S(2)}, u32[]{:S(2)}) %all-to-all-start.4) | async-done | bytes 262176 | tf_op jit(solution)/shard_map/all_to_all | solution.py:45
  152.7 3.6 %all-to-all-start.5 = ((f32[4,128,256]{2,1,0:T(8,128)}), f32[4,128,256]{2,1,0:T(8,128)S(1)}, u32[]{:S(2)}, u32[]{:S(2)}) async-start(f32[4,128,256]{2,1,0:T(8,128)} %broadcast_in_dim.58), calls=%async_computation.5 | async-start | bytes 1048576 | tf_op jit(solution)/shard_map/all_to_all | solution.py:45
  162.4 2.1 all-to-all-done.5
  168.6 2.4 %collective-permute-start.11 = (f32[4,128,256]{2,1,0:T(8,128)}, f32[4,128,256]{2,1,0:T(8,128)S(1)}, u32[]{:S(2)}, u32[]{:S(2)}) collective-permute-start(f32[4,128,256]{2,1,0:T(8,128)} %convolution_bitcast_fusion.2), channel_id=1, source_target_pairs={{0,32},{2,34},{4,36},{6,38},{8,40},{10,42},{12,44},{14,46},{16,48}... | collective-permute-start | bytes 1572872 | tf_op jit(solution)/shard_map/ppermute | solution.py:25
  172.4 7.9 %all-to-all-start.6 = ((f32[4,128,256]{2,1,0:T(8,128)}), f32[4,128,256]{2,1,0:T(8,128)S(1)}, u32[]{:S(2)}, u32[]{:S(2)}) async-start(f32[4,128,256]{2,1,0:T(8,128)} %fusion), calls=%async_computation.6 | async-start | bytes 1048576 | tf_op jit(solution)/shard_map/all_to_all | solution.py:45
  181.0 7.5 %all-to-all-done.6 = f32[4,128,256]{2,1,0:T(8,128)S(1)} async-done(((f32[4,128,256]{2,1,0:T(8,128)}), f32[4,128,256]{2,1,0:T(8,128)S(1)}, u32[]{:S(2)}, u32[]{:S(2)}) %all-to-all-start.6) | async-done | bytes 524320 | tf_op jit(solution)/shard_map/all_to_all | solution.py:45
  189.5 4.9 %all-to-all-start.7 = ((f32[4,128,256]{2,1,0:T(8,128)}), f32[4,128,256]{2,1,0:T(8,128)S(1)}, u32[]{:S(2)}, u32[]{:S(2)}) async-start(f32[4,128,256]{2,1,0:T(8,128)} %add.212), calls=%async_computation.7 | async-start | bytes 1048576 | tf_op jit(solution)/shard_map/all_to_all | solution.py:45
  194.4 10.0 %collective-permute-start.13 = (f32[128,256]{1,0:T(8,128)S(1)}, f32[128,256]{1,0:T(8,128)S(1)}, u32[]{:S(2)}, u32[]{:S(2)}) collective-permute-start(f32[128,256]{1,0:T(8,128)S(1)} %reduce_sum.38), channel_id=1, source_target_pairs={{0,1},{2,3},{4,5},{6,7},{8,9},{10,11},{12,13},{14,15},{16,17},{18,... | collective-permute-start | bytes 393224 | tf_op jit(solution)/shard_map/ppermute | solution.py:25
  204.4 13.0 %collective-permute-done.13 = f32[128,256]{1,0:T(8,128)S(1)} collective-permute-done((f32[128,256]{1,0:T(8,128)S(1)}, f32[128,256]{1,0:T(8,128)S(1)}, u32[]{:S(2)}, u32[]{:S(2)}) %collective-permute-start.13) | collective-permute-done | bytes 131104 | tf_op jit(solution)/shard_map/ppermute | solution.py:25
  (89 shorter events, 32.3 us)
Async XLA Ops:
  0.0 1.1 copy-start
  1.3 12.5 %collective-permute-start = (f32[2,64,256]{2,1,0:T(8,128)S(1)}, f32[2,64,256]{2,1,0:T(8,128)S(1)}, u32[]{:S(2)}, u32[]{:S(2)}) collective-permute-start(f32[2,64,256]{2,1,0:T(8,128)S(1)} %get-tuple-element.38), channel_id=1, source_target_pairs={{0,32},{2,34},{4,36},{6,38},{8,40},{10,42},{12,44},{14,46},{16,48}... | collective-permute-start | bytes 393224 | tf_op jit(solution)/shard_map/ppermute | solution.py:25
  4.3 24.0 %all-to-all-start = ((f32[4,256,256]{1,2,0:T(8,128)}), f32[4,256,256]{1,2,0:T(8,128)S(1)}, u32[]{:S(2)}, u32[]{:S(2)}) async-start(f32[4,256,256]{1,2,0:T(8,128)} %broadcast_in_dim.29), calls=%async_computation | async-start | bytes 2097152 | tf_op jit(solution)/shard_map/all_to_all | solution.py:45
  13.8 13.7 %collective-permute-start.1 = (f32[2,64,256]{2,1,0:T(8,128)S(1)}, f32[2,64,256]{2,1,0:T(8,128)S(1)}, u32[]{:S(2)}, u32[]{:S(2)}) collective-permute-start(f32[2,64,256]{2,1,0:T(8,128)S(1)} %maximum_select_fusion.5), channel_id=1, source_target_pairs={{0,256},{2,258},{4,260},{6,262},{8,264},{10,266},{12,268},{14,270}... | collective-permute-start | bytes 393224 | tf_op jit(solution)/shard_map/ppermute | solution.py:25
  29.2 22.3 %collective-permute-start.3 = (f32[256,1024]{0,1:T(8,128)S(1)}, f32[256,1024]{0,1:T(8,128)S(1)}, u32[]{:S(2)}, u32[]{:S(2)}) collective-permute-start(f32[256,1024]{0,1:T(8,128)S(1)} %bitcast.83), channel_id=1, source_target_pairs={{0,32},{2,34},{4,36},{6,38},{8,40},{10,42},{12,44},{14,46},{16,48}... | collective-permute-start | bytes 3145736 | tf_op jit(solution)/shard_map/ppermute | solution.py:25
  31.1 19.7 %all-to-all-start.1 = ((f32[4,2,64,256]{3,2,1,0:T(8,128)}), f32[4,2,64,256]{3,2,1,0:T(8,128)S(1)}, u32[]{:S(2)}, u32[]{:S(2)}) async-start(f32[4,2,64,256]{3,2,1,0:T(8,128)} %broadcast_in_dim.30), calls=%async_computation.1 | async-start | bytes 1048576 | tf_op jit(solution)/shard_map/all_to_all | solution.py:45
  34.6 14.4 %collective-permute-start.2 = (f32[2,2,64,256]{3,2,1,0:T(8,128)S(1)}, f32[2,2,64,256]{3,2,1,0:T(8,128)S(1)}, u32[]{:S(2)}, u32[]{:S(2)}) collective-permute-start(f32[2,2,64,256]{3,2,1,0:T(8,128)S(1)} %maximum_select_fusion.3), channel_id=1, source_target_pairs={{0,128},{2,130},{4,132},{6,134},{8,136},{10,138},{12,140},{14,142}... | collective-permute-start | bytes 786440 | tf_op jit(solution)/shard_map/ppermute | solution.py:25
  49.0 0.7 copy-start.1
  52.2 11.1 %collective-permute-start.4 = (f32[128,1024]{1,0:T(8,128)S(1)}, f32[128,1024]{1,0:T(8,128)S(1)}, u32[]{:S(2)}, u32[]{:S(2)}) collective-permute-start(f32[128,1024]{1,0:T(8,128)S(1)} %convolution_add_fusion), channel_id=1, source_target_pairs={{0,64},{2,66},{4,68},{6,70},{8,72},{10,74},{12,76},{14,78},{16,80}... | collective-permute-start | bytes 1572872 | tf_op jit(solution)/shard_map/ppermute | solution.py:25
  63.2 2.9 %copy-start.4 = (s32[4096]{0:T(1024)S(1)}, s32[4096]{0:T(1024)}, u32[]{:S(2)}) copy-start(s32[4096]{0:T(1024)} %param.8) | copy-start | bytes 49156
  63.3 2.9 %copy-start.3 = (s32[4096]{0:T(1024)S(1)}, s32[4096]{0:T(1024)}, u32[]{:S(2)}) copy-start(s32[4096]{0:T(1024)} %param.9) | copy-start | bytes 49156
  63.3 14.2 %collective-permute-start.5 = (f32[64,1024]{1,0:T(8,128)S(1)}, f32[64,1024]{1,0:T(8,128)S(1)}, u32[]{:S(2)}, u32[]{:S(2)}) collective-permute-start(f32[64,1024]{1,0:T(8,128)S(1)} %get-tuple-element.32), channel_id=1, source_target_pairs={{0,128},{2,130},{4,132},{6,134},{8,136},{10,138},{12,140},{14,142}... | collective-permute-start | bytes 786440 | tf_op jit(solution)/shard_map/ppermute | solution.py:25
  66.2 16.5 %copy-start.2 = (f32[4096]{0:T(1024)}, f32[4096]{0:T(1024)S(1)}, u32[]{:S(2)}) copy-start(f32[4096]{0:T(1024)S(1)} %convert_add_fusion) | copy-start | bytes 49156
  77.6 12.6 %collective-permute-start.6 = (f32[32,1024]{1,0:T(8,128)S(1)}, f32[32,1024]{1,0:T(8,128)S(1)}, u32[]{:S(2)}, u32[]{:S(2)}) collective-permute-start(f32[32,1024]{1,0:T(8,128)S(1)} %dynamic-slice_add_fusion.2), channel_id=1, source_target_pairs={{0,256},{2,258},{4,260},{6,262},{8,264},{10,266},{12,268},{14,270}... | collective-permute-start | bytes 393224 | tf_op jit(solution)/shard_map/ppermute | solution.py:25
  82.7 0.7 copy-start.5
  83.9 6.3 %dynamic-slice-start = ((f32[4096]{0:T(1024)}, s32[]{:T(128)}), f32[1024]{0:T(1024)S(1)}, s32[]{:S(2)}) async-start(f32[4096]{0:T(1024)} %copy-done.2, s32[]{:T(128)} %select_n.208), calls=%async_computation.8 | async-start | bytes 8704 | tf_op jit(solution)/shard_map/dynamic_slice | solution.py:68
  90.3 11.5 %collective-permute-start.7 = (f32[32,1024]{1,0:T(8,128)S(1)}, f32[32,1024]{1,0:T(8,128)S(1)}, u32[]{:S(2)}, u32[]{:S(2)}) collective-permute-start(f32[32,1024]{1,0:T(8,128)S(1)} %compare_select_fusion), channel_id=1, source_target_pairs={{0,256},{2,258},{4,260},{6,262},{8,264},{10,266},{12,268},{14,270}... | collective-permute-start | bytes 393224 | tf_op jit(solution)/shard_map/ppermute | solution.py:25
  101.9 9.3 %collective-permute-start.8 = (f32[64,1024]{1,0:T(8,128)S(1)}, f32[64,1024]{1,0:T(8,128)}, u32[]{:S(2)}, u32[]{:S(2)}) collective-permute-start(f32[64,1024]{1,0:T(8,128)S(1)} %maximum_select_fusion.4), channel_id=1, source_target_pairs={{0,128},{2,130},{4,132},{6,134},{8,136},{10,138},{12,140},{14,142}... | collective-permute-start | bytes 786440 | tf_op jit(solution)/shard_map/ppermute | solution.py:25
  103.8 18.0 %all-to-all-start.3 = ((f32[4,2,64,256]{3,2,1,0:T(8,128)}), f32[4,2,64,256]{3,2,1,0:T(8,128)S(1)}, u32[]{:S(2)}, u32[]{:S(2)}) async-start(f32[4,2,64,256]{3,2,1,0:T(8,128)} %fusion.2), calls=%async_computation.3 | async-start | bytes 1048576 | tf_op jit(solution)/shard_map/all_to_all | solution.py:45
  113.2 19.8 %collective-permute-start.9 = (f32[128,1024]{1,0:T(8,128)S(1)}, f32[128,1024]{1,0:T(8,128)}, u32[]{:S(2)}, u32[]{:S(2)}) collective-permute-start(f32[128,1024]{1,0:T(8,128)S(1)} %maximum_select_fusion.2), channel_id=1, source_target_pairs={{0,64},{2,66},{4,68},{6,70},{8,72},{10,74},{12,76},{14,78},{16,80}... | collective-permute-start | bytes 1572872 | tf_op jit(solution)/shard_map/ppermute | solution.py:25
  135.0 21.3 %collective-permute-start.10 = (f32[4,2,64,256]{3,2,1,0:T(8,128)S(1)}, f32[4,2,64,256]{3,2,1,0:T(8,128)S(1)}, u32[]{:S(2)}, u32[]{:S(2)}) collective-permute-start(f32[4,2,64,256]{3,2,1,0:T(8,128)S(1)} %all-to-all-done.3), channel_id=1, source_target_pairs={{0,64},{2,66},{4,68},{6,70},{8,72},{10,74},{12,76},{14,78},{16,80}... | collective-permute-start | bytes 1572872 | tf_op jit(solution)/shard_map/ppermute | solution.py:25
  141.7 10.1 %all-to-all-start.4 = ((f32[4,128,128]{2,1,0:T(8,128)}), f32[4,128,128]{2,1,0:T(8,128)S(1)}, u32[]{:S(2)}, u32[]{:S(2)}) async-start(f32[4,128,128]{2,1,0:T(8,128)} %pad_maximum_fusion.2), calls=%async_computation.4 | async-start | bytes 524288 | tf_op jit(solution)/shard_map/all_to_all | solution.py:45
  152.7 11.8 %all-to-all-start.5 = ((f32[4,128,256]{2,1,0:T(8,128)}), f32[4,128,256]{2,1,0:T(8,128)S(1)}, u32[]{:S(2)}, u32[]{:S(2)}) async-start(f32[4,128,256]{2,1,0:T(8,128)} %broadcast_in_dim.58), calls=%async_computation.5 | async-start | bytes 1048576 | tf_op jit(solution)/shard_map/all_to_all | solution.py:45
  165.2 5.8 %collective-permute-start.12 = (f32[4,128,256]{2,1,0:T(8,128)S(1)}, f32[4,128,256]{2,1,0:T(8,128)S(1)}, u32[]{:S(2)}, u32[]{:S(2)}) collective-permute-start(f32[4,128,256]{2,1,0:T(8,128)S(1)} %convolution_bitcast_fusion), channel_id=1, source_target_pairs={{0,32},{2,34},{4,36},{6,38},{8,40},{10,42},{12,44},{14,46},{16,48}... | collective-permute-start | bytes 1572872 | tf_op jit(solution)/shard_map/ppermute | solution.py:25
  168.6 20.0 %collective-permute-start.11 = (f32[4,128,256]{2,1,0:T(8,128)}, f32[4,128,256]{2,1,0:T(8,128)S(1)}, u32[]{:S(2)}, u32[]{:S(2)}) collective-permute-start(f32[4,128,256]{2,1,0:T(8,128)} %convolution_bitcast_fusion.2), channel_id=1, source_target_pairs={{0,32},{2,34},{4,36},{6,38},{8,40},{10,42},{12,44},{14,46},{16,48}... | collective-permute-start | bytes 1572872 | tf_op jit(solution)/shard_map/ppermute | solution.py:25
  172.4 16.1 %all-to-all-start.6 = ((f32[4,128,256]{2,1,0:T(8,128)}), f32[4,128,256]{2,1,0:T(8,128)S(1)}, u32[]{:S(2)}, u32[]{:S(2)}) async-start(f32[4,128,256]{2,1,0:T(8,128)} %fusion), calls=%async_computation.6 | async-start | bytes 1048576 | tf_op jit(solution)/shard_map/all_to_all | solution.py:45
  189.5 14.9 %all-to-all-start.7 = ((f32[4,128,256]{2,1,0:T(8,128)}), f32[4,128,256]{2,1,0:T(8,128)S(1)}, u32[]{:S(2)}, u32[]{:S(2)}) async-start(f32[4,128,256]{2,1,0:T(8,128)} %add.212), calls=%async_computation.7 | async-start | bytes 1048576 | tf_op jit(solution)/shard_map/all_to_all | solution.py:45
  194.4 23.0 %collective-permute-start.13 = (f32[128,256]{1,0:T(8,128)S(1)}, f32[128,256]{1,0:T(8,128)S(1)}, u32[]{:S(2)}, u32[]{:S(2)}) collective-permute-start(f32[128,256]{1,0:T(8,128)S(1)} %reduce_sum.38), channel_id=1, source_target_pairs={{0,1},{2,3},{4,5},{6,7},{8,9},{10,11},{12,13},{14,15},{16,17},{18,... | collective-permute-start | bytes 393224 | tf_op jit(solution)/shard_map/ppermute | solution.py:25

commit v6 on v3

--- a/solution.py
+++ b/solution.py
@@ -102,16 +102,14 @@
     wide_oth = moved(wide, other_core)
     grads = to_all(grads, "y")
 
-    far = joined(far[:, None], moved(far, along(2))[:, None], bits[1], 1)
-    grads, far = tied(grads, far.reshape(4, 2, quarter, n))
-    far = turned_round(far, (4 - co * ((SHIFT + bits[0]) // 2)) % 4)
+    far_got = moved(far, along(2))
 
     def inner_of(which):
         g = part(grads, which, 2)
         return dot(g[:, 0].reshape(half, n), wide) + dot(g[:, 1].reshape(half, n), wide_oth)
 
     got = moved(inner_of(1 - bits[0]), along(1))
-    kept = inner_of(bits[0])
+    kept, far_got = tied(inner_of(bits[0]), far_got)
     rows = half
     for distance, bit in ((2, bits[1]), (4, bits[2])):
         rows //= 2
@@ -132,6 +130,8 @@
     spacing = jnp.where(on_diagonal, jnp.float32(1.0), of_columns(eigen) - row_eigen)
     scaled = jnp.where(on_diagonal, of_columns(value_grad), inner / spacing)
 
+    far = joined(far[:, None], far_got[:, None], bits[1], 1).reshape(4, 2, quarter, n)
+    far = turned_round(far, (4 - co * ((SHIFT + bits[0]) // 2)) % 4)
     scaled, far = tied(scaled, far)
     far = to_all(far, "y")
     for distance, bit in ((4, bits[2]), (2, bits[1])):

time: 212 us -> 208 us (0.981)
  waiting for transfers between devices: 104 us -> 91.5 us
  starting transfers between devices: 81.1 us -> 91.7 us
    ppermute x13, waiting for transfers between devices: 76.1 us -> 55.4 us  [moved(): return lax.ppermute(v, AXES, pairs)]
    ppermute x13, starting transfers between devices: 55.8 us -> 64.6 us  [moved(): return lax.ppermute(v, AXES, pairs)]
    all_to_all x6, waiting for transfers between devices: 28 us -> 36.1 us  [to_all(): return lax.all_to_all(v, axis, 0, 0, tiled=True)]
where the time goes in v6:
time: 208 us; the launch traced here: 207 us
  starting transfers between devices  91.7 us (44%)
  waiting for transfers between devices  91.5 us (44%)
  local copies, waits for them, and re-layouts  11 us (5%)
  matrix products  8.83 us (4%)
  other arithmetic  3.27 us (2%)
    ppermute x13, starting transfers between devices, moved(): return lax.ppermute(v, AXES, pairs)  64.6 us
    ppermute x13, waiting for transfers between devices, moved(): return lax.ppermute(v, AXES, pairs)  55.4 us
    all_to_all x6, waiting for transfers between devices, to_all(): return lax.all_to_all(v, axis, 0, 0, tiled=True)  36.1 us
    all_to_all x6, starting transfers between devices, to_all(): return lax.all_to_all(v, axis, 0, 0, tiled=True)  27.1 us
    dot_general x10, matrix products, dot(): lax.dot_general(a, b, (contract, ((), ())), precision=PREC, preferred_ele...  8.83 us
  transfers between devices with their start and end apart: 19, of which 14 were waited for; matrix products, arithmetic and copies ran while one was open for 8% of the time, Pallas kernels for 0%

profile of v6, /device:TPU:64, one launch (start us, length us, event | category | flops | bytes accessed | tf_op | source)
XLA Modules:
  0.0 206.8 jit_solution(11004168115963955456)
XLA Ops:
  2.2 4.4 %all-to-all-start = ((f32[4,256,256]{1,2,0:T(8,128)}), f32[4,256,256]{1,2,0:T(8,128)S(1)}, u32[]{:S(2)}, u32[]{:S(2)}) async-start(f32[4,256,256]{1,2,0:T(8,128)} %broadcast_in_dim.28), calls=%async_computation | async-start | bytes 2097152 | tf_op jit(solution)/shard_map/all_to_all | solution.py:45
  6.8 1.9 collective-permute-start
  10.1 9.1 %collective-permute-start.1 = (f32[2,64,256]{2,1,0:T(8,128)S(1)}, f32[2,64,256]{2,1,0:T(8,128)S(1)}, u32[]{:S(2)}, u32[]{:S(2)}) collective-permute-start(f32[2,64,256]{2,1,0:T(8,128)S(1)} %maximum_select_fusion.5), channel_id=1, source_target_pairs={{0,256},{2,258},{4,260},{6,262},{8,264},{10,266},{12,268},{14,270}... | collective-permute-start | bytes 393224 | tf_op jit(solution)/shard_map/ppermute | solution.py:25
  19.2 7.0 %collective-permute-done.1 = f32[2,64,256]{2,1,0:T(8,128)S(1)} collective-permute-done((f32[2,64,256]{2,1,0:T(8,128)S(1)}, f32[2,64,256]{2,1,0:T(8,128)S(1)}, u32[]{:S(2)}, u32[]{:S(2)}) %collective-permute-start.1) | collective-permute-done | bytes 131104 | tf_op jit(solution)/shard_map/ppermute | solution.py:25
  27.1 2.0 collective-permute-start.2
  29.0 4.5 %all-to-all-start.1 = ((f32[4,2,64,256]{3,2,1,0:T(8,128)}), f32[4,2,64,256]{3,2,1,0:T(8,128)S(1)}, u32[]{:S(2)}, u32[]{:S(2)}) async-start(f32[4,2,64,256]{3,2,1,0:T(8,128)} %broadcast_in_dim.29), calls=%async_computation.1 | async-start | bytes 1048576 | tf_op jit(solution)/shard_map/all_to_all | solution.py:45
  33.5 3.0 %collective-permute-start.3 = (f32[2,2,64,256]{3,2,1,0:T(8,128)S(1)}, f32[2,2,64,256]{3,2,1,0:T(8,128)S(1)}, u32[]{:S(2)}, u32[]{:S(2)}) collective-permute-start(f32[2,2,64,256]{3,2,1,0:T(8,128)S(1)} %maximum_select_fusion.3), channel_id=1, source_target_pairs={{0,128},{2,130},{4,132},{6,134},{8,136},{10,138},{12,140},{14,142}... | collective-permute-start | bytes 786440 | tf_op jit(solution)/shard_map/ppermute | solution.py:25
  36.5 7.0 %all-to-all-done.1 = f32[4,2,64,256]{3,2,1,0:T(8,128)S(1)} async-done(((f32[4,2,64,256]{3,2,1,0:T(8,128)}), f32[4,2,64,256]{3,2,1,0:T(8,128)S(1)}, u32[]{:S(2)}, u32[]{:S(2)}) %all-to-all-start.1) | async-done | bytes 524320 | tf_op jit(solution)/shard_map/all_to_all | solution.py:45
  44.9 5.0 %collective-permute-start.4 = (f32[128,1024]{1,0:T(8,128)S(1)}, f32[128,1024]{1,0:T(8,128)S(1)}, u32[]{:S(2)}, u32[]{:S(2)}) collective-permute-start(f32[128,1024]{1,0:T(8,128)S(1)} %convolution_add_fusion), channel_id=1, source_target_pairs={{0,64},{2,66},{4,68},{6,70},{8,72},{10,74},{12,76},{14,78},{16,80}... | collective-permute-start | bytes 1572872 | tf_op jit(solution)/shard_map/ppermute | solution.py:25
  51.2 5.8 %collective-permute-done.4 = f32[128,1024]{1,0:T(8,128)S(1)} collective-permute-done((f32[128,1024]{1,0:T(8,128)S(1)}, f32[128,1024]{1,0:T(8,128)S(1)}, u32[]{:S(2)}, u32[]{:S(2)}) %collective-permute-start.4) | collective-permute-done | bytes 524320 | tf_op jit(solution)/shard_map/ppermute | solution.py:25
  57.1 2.2 %collective-permute-start.5 = (f32[64,1024]{1,0:T(8,128)S(1)}, f32[64,1024]{1,0:T(8,128)S(1)}, u32[]{:S(2)}, u32[]{:S(2)}) collective-permute-start(f32[64,1024]{1,0:T(8,128)S(1)} %get-tuple-element.26), channel_id=1, source_target_pairs={{0,128},{2,130},{4,132},{6,134},{8,136},{10,138},{12,140},{14,142}... | collective-permute-start | bytes 786440 | tf_op jit(solution)/shard_map/ppermute | solution.py:25
  60.7 10.7 %collective-permute-done.5 = f32[64,1024]{1,0:T(8,128)S(1)} collective-permute-done((f32[64,1024]{1,0:T(8,128)S(1)}, f32[64,1024]{1,0:T(8,128)S(1)}, u32[]{:S(2)}, u32[]{:S(2)}) %collective-permute-start.5) | collective-permute-done | bytes 262176 | tf_op jit(solution)/shard_map/ppermute | solution.py:25
  71.4 4.1 %collective-permute-start.6 = (f32[32,1024]{1,0:T(8,128)S(1)}, f32[32,1024]{1,0:T(8,128)S(1)}, u32[]{:S(2)}, u32[]{:S(2)}) collective-permute-start(f32[32,1024]{1,0:T(8,128)S(1)} %dynamic-slice_add_fusion.3), channel_id=1, source_target_pairs={{0,256},{2,258},{4,260},{6,262},{8,264},{10,266},{12,268},{14,270}... | collective-permute-start | bytes 393224 | tf_op jit(solution)/shard_map/ppermute | solution.py:25
  76.5 5.8 %collective-permute-done.6 = f32[32,1024]{1,0:T(8,128)S(1)} collective-permute-done((f32[32,1024]{1,0:T(8,128)S(1)}, f32[32,1024]{1,0:T(8,128)S(1)}, u32[]{:S(2)}, u32[]{:S(2)}) %collective-permute-start.6) | collective-permute-done | bytes 131104 | tf_op jit(solution)/shard_map/ppermute | solution.py:25
  82.4 5.5 %collective-permute-start.7 = (f32[32,1024]{1,0:T(8,128)S(1)}, f32[32,1024]{1,0:T(8,128)S(1)}, u32[]{:S(2)}, u32[]{:S(2)}) collective-permute-start(f32[32,1024]{1,0:T(8,128)S(1)} %compare_select_fusion), channel_id=1, source_target_pairs={{0,256},{2,258},{4,260},{6,262},{8,264},{10,266},{12,268},{14,270}... | collective-permute-start | bytes 393224 | tf_op jit(solution)/shard_map/ppermute | solution.py:25
  87.9 5.4 %collective-permute-done.7 = f32[32,1024]{1,0:T(8,128)S(1)} collective-permute-done((f32[32,1024]{1,0:T(8,128)S(1)}, f32[32,1024]{1,0:T(8,128)S(1)}, u32[]{:S(2)}, u32[]{:S(2)}) %collective-permute-start.7) | collective-permute-done | bytes 131104 | tf_op jit(solution)/shard_map/ppermute | solution.py:25
  93.3 5.6 %collective-permute-start.8 = (f32[64,1024]{1,0:T(8,128)S(1)}, f32[64,1024]{1,0:T(8,128)S(1)}, u32[]{:S(2)}, u32[]{:S(2)}) collective-permute-start(f32[64,1024]{1,0:T(8,128)S(1)} %maximum_select_fusion.4), channel_id=1, source_target_pairs={{0,128},{2,130},{4,132},{6,134},{8,136},{10,138},{12,140},{14,142}... | collective-permute-start | bytes 786440 | tf_op jit(solution)/shard_map/ppermute | solution.py:25
  98.9 6.4 %all-to-all-start.2 = ((f32[4,2,64,256]{3,2,1,0:T(8,128)}), f32[4,2,64,256]{3,2,1,0:T(8,128)S(1)}, u32[]{:S(2)}, u32[]{:S(2)}) async-start(f32[4,2,64,256]{3,2,1,0:T(8,128)} %fusion.2), calls=%async_computation.2 | async-start | bytes 1048576 | tf_op jit(solution)/shard_map/all_to_all | solution.py:45
  106.1 6.2 %collective-permute-start.9 = (f32[128,1024]{1,0:T(8,128)S(1)}, f32[128,1024]{1,0:T(8,128)S(1)}, u32[]{:S(2)}, u32[]{:S(2)}) collective-permute-start(f32[128,1024]{1,0:T(8,128)S(1)} %maximum_select_fusion.2), channel_id=1, source_target_pairs={{0,64},{2,66},{4,68},{6,70},{8,72},{10,74},{12,76},{14,78},{16,80}... | collective-permute-start | bytes 1572872 | tf_op jit(solution)/shard_map/ppermute | solution.py:25
  114.3 5.2 %collective-permute-done.9 = f32[128,1024]{1,0:T(8,128)S(1)} collective-permute-done((f32[128,1024]{1,0:T(8,128)S(1)}, f32[128,1024]{1,0:T(8,128)S(1)}, u32[]{:S(2)}, u32[]{:S(2)}) %collective-permute-start.9) | collective-permute-done | bytes 524320 | tf_op jit(solution)/shard_map/ppermute | solution.py:25
  122.3 3.9 %collective-permute-start.10 = (f32[4,2,64,256]{3,2,1,0:T(8,128)S(1)}, f32[4,2,64,256]{3,2,1,0:T(8,128)S(1)}, u32[]{:S(2)}, u32[]{:S(2)}) collective-permute-start(f32[4,2,64,256]{3,2,1,0:T(8,128)S(1)} %all-to-all-done.2), channel_id=1, source_target_pairs={{0,64},{2,66},{4,68},{6,70},{8,72},{10,74},{12,76},{14,78},{16,80}... | collective-permute-start | bytes 1572872 | tf_op jit(solution)/shard_map/ppermute | solution.py:25
  126.2 3.5 %all-to-all-start.3 = ((f32[4,128,256]{2,1,0:T(8,128)}), f32[4,128,256]{2,1,0:T(8,128)S(1)}, u32[]{:S(2)}, u32[]{:S(2)}) async-start(f32[4,128,256]{2,1,0:T(8,128)} %bitcast.16), calls=%async_computation.3 | async-start | bytes 1048576 | tf_op jit(solution)/shard_map/all_to_all | solution.py:45
  129.7 10.3 %all-to-all-done.3 = f32[4,128,256]{2,1,0:T(8,128)S(1)} async-done(((f32[4,128,256]{2,1,0:T(8,128)}), f32[4,128,256]{2,1,0:T(8,128)S(1)}, u32[]{:S(2)}, u32[]{:S(2)}) %all-to-all-start.3) | async-done | bytes 524320 | tf_op jit(solution)/shard_map/all_to_all | solution.py:45
  140.9 3.6 %all-to-all-start.4 = ((f32[4,128,256]{2,1,0:T(8,128)}), f32[4,128,256]{2,1,0:T(8,128)S(1)}, u32[]{:S(2)}, u32[]{:S(2)}) async-start(f32[4,128,256]{2,1,0:T(8,128)} %broadcast_in_dim.58), calls=%async_computation.4 | async-start | bytes 1048576 | tf_op jit(solution)/shard_map/all_to_all | solution.py:45
  150.6 3.3 %all-to-all-done.4 = f32[4,128,256]{2,1,0:T(8,128)S(1)} async-done(((f32[4,128,256]{2,1,0:T(8,128)}), f32[4,128,256]{2,1,0:T(8,128)S(1)}, u32[]{:S(2)}, u32[]{:S(2)}) %all-to-all-start.4) | async-done | bytes 524320 | tf_op jit(solution)/shard_map/all_to_all | solution.py:45
  154.6 1.9 collective-permute-start.11
  156.5 2.6 %collective-permute-done.11 = f32[4,256,256]{2,1,0:T(8,128)S(1)} collective-permute-done((f32[4,256,256]{2,1,0:T(8,128)S(1)}, f32[4,256,256]{2,1,0:T(8,128)S(1)}, u32[]{:S(2)}, u32[]{:S(2)}) %collective-permute-start.11) | collective-permute-done | bytes 1048608 | tf_op jit(solution)/shard_map/ppermute | solution.py:25
  159.1 1.6 fusion
  160.8 4.7 %all-to-all-start.5 = ((f32[4,256,256]{2,1,0:T(8,128)}), f32[4,256,256]{2,1,0:T(8,128)S(1)}, u32[]{:S(2)}, u32[]{:S(2)}) async-start(f32[4,256,256]{2,1,0:T(8,128)} %fusion), calls=%async_computation.5 | async-start | bytes 2097152 | tf_op jit(solution)/shard_map/all_to_all | solution.py:45
  165.4 15.4 %all-to-all-done.5 = f32[4,256,256]{2,1,0:T(8,128)S(1)} async-done(((f32[4,256,256]{2,1,0:T(8,128)}), f32[4,256,256]{2,1,0:T(8,128)S(1)}, u32[]{:S(2)}, u32[]{:S(2)}) %all-to-all-start.5) | async-done | bytes 1048608 | tf_op jit(solution)/shard_map/all_to_all | solution.py:45
  180.9 14.1 %collective-permute-start.12 = (f32[128,256]{1,0:T(8,128)S(1)}, f32[128,256]{1,0:T(8,128)S(1)}, u32[]{:S(2)}, u32[]{:S(2)}) collective-permute-start(f32[128,256]{1,0:T(8,128)S(1)} %constant_dynamic-slice_fusion.1), channel_id=1, source_target_pairs={{0,1},{2,3},{4,5},{6,7},{8,9},{10,11},{12,13},{14,15},{16,17},{18,... | collective-permute-start | bytes 393224 | tf_op jit(solution)/shard_map/ppermute | solution.py:25
  195.1 11.0 %collective-permute-done.12 = f32[128,256]{1,0:T(8,128)S(1)} collective-permute-done((f32[128,256]{1,0:T(8,128)S(1)}, f32[128,256]{1,0:T(8,128)S(1)}, u32[]{:S(2)}, u32[]{:S(2)}) %collective-permute-start.12) | collective-permute-done | bytes 131104 | tf_op jit(solution)/shard_map/ppermute | solution.py:25
  (77 shorter events, 23.4 us)
Async XLA Ops:
  2.2 4.4 %copy-start = (f32[256,256]{1,0:T(8,128)S(1)}, f32[256,256]{1,0:T(8,128)}, u32[]{:S(2)}) copy-start(f32[256,256]{1,0:T(8,128)} %param.6) | copy-start | bytes 786436
  2.2 24.0 %all-to-all-start = ((f32[4,256,256]{1,2,0:T(8,128)}), f32[4,256,256]{1,2,0:T(8,128)S(1)}, u32[]{:S(2)}, u32[]{:S(2)}) async-start(f32[4,256,256]{1,2,0:T(8,128)} %broadcast_in_dim.28), calls=%async_computation | async-start | bytes 2097152 | tf_op jit(solution)/shard_map/all_to_all | solution.py:45
  6.8 3.2 %collective-permute-start = (f32[2,64,256]{2,1,0:T(8,128)S(1)}, f32[2,64,256]{2,1,0:T(8,128)S(1)}, u32[]{:S(2)}, u32[]{:S(2)}) collective-permute-start(f32[2,64,256]{2,1,0:T(8,128)S(1)} %get-tuple-element.34), channel_id=1, source_target_pairs={{0,32},{2,34},{4,36},{6,38},{8,40},{10,42},{12,44},{14,46},{16,48}... | collective-permute-start | bytes 393224 | tf_op jit(solution)/shard_map/ppermute | solution.py:25
  10.1 16.1 %collective-permute-start.1 = (f32[2,64,256]{2,1,0:T(8,128)S(1)}, f32[2,64,256]{2,1,0:T(8,128)S(1)}, u32[]{:S(2)}, u32[]{:S(2)}) collective-permute-start(f32[2,64,256]{2,1,0:T(8,128)S(1)} %maximum_select_fusion.5), channel_id=1, source_target_pairs={{0,256},{2,258},{4,260},{6,262},{8,264},{10,266},{12,268},{14,270}... | collective-permute-start | bytes 393224 | tf_op jit(solution)/shard_map/ppermute | solution.py:25
  27.1 17.1 %collective-permute-start.2 = (f32[256,1024]{0,1:T(8,128)S(1)}, f32[256,1024]{0,1:T(8,128)S(1)}, u32[]{:S(2)}, u32[]{:S(2)}) collective-permute-start(f32[256,1024]{0,1:T(8,128)S(1)} %bitcast.62), channel_id=1, source_target_pairs={{0,32},{2,34},{4,36},{6,38},{8,40},{10,42},{12,44},{14,46},{16,48}... | collective-permute-start | bytes 3145736 | tf_op jit(solution)/shard_map/ppermute | solution.py:25
  29.0 14.5 %all-to-all-start.1 = ((f32[4,2,64,256]{3,2,1,0:T(8,128)}), f32[4,2,64,256]{3,2,1,0:T(8,128)S(1)}, u32[]{:S(2)}, u32[]{:S(2)}) async-start(f32[4,2,64,256]{3,2,1,0:T(8,128)} %broadcast_in_dim.29), calls=%async_computation.1 | async-start | bytes 1048576 | tf_op jit(solution)/shard_map/all_to_all | solution.py:45
  33.5 17.7 %collective-permute-start.3 = (f32[2,2,64,256]{3,2,1,0:T(8,128)S(1)}, f32[2,2,64,256]{3,2,1,0:T(8,128)S(1)}, u32[]{:S(2)}, u32[]{:S(2)}) collective-permute-start(f32[2,2,64,256]{3,2,1,0:T(8,128)S(1)} %maximum_select_fusion.3), channel_id=1, source_target_pairs={{0,128},{2,130},{4,132},{6,134},{8,136},{10,138},{12,140},{14,142}... | collective-permute-start | bytes 786440 | tf_op jit(solution)/shard_map/ppermute | solution.py:25
  44.9 12.1 %collective-permute-start.4 = (f32[128,1024]{1,0:T(8,128)S(1)}, f32[128,1024]{1,0:T(8,128)S(1)}, u32[]{:S(2)}, u32[]{:S(2)}) collective-permute-start(f32[128,1024]{1,0:T(8,128)S(1)} %convolution_add_fusion), channel_id=1, source_target_pairs={{0,64},{2,66},{4,68},{6,70},{8,72},{10,74},{12,76},{14,78},{16,80}... | collective-permute-start | bytes 1572872 | tf_op jit(solution)/shard_map/ppermute | solution.py:25
  51.2 8.1 %copy-start.2 = (s32[4096]{0:T(1024)S(1)}, s32[4096]{0:T(1024)}, u32[]{:S(2)}) copy-start(s32[4096]{0:T(1024)} %param.9) | copy-start | bytes 49156
  51.2 8.1 %copy-start.3 = (s32[4096]{0:T(1024)S(1)}, s32[4096]{0:T(1024)}, u32[]{:S(2)}) copy-start(s32[4096]{0:T(1024)} %param.8) | copy-start | bytes 49156
  57.1 14.3 %collective-permute-start.5 = (f32[64,1024]{1,0:T(8,128)S(1)}, f32[64,1024]{1,0:T(8,128)S(1)}, u32[]{:S(2)}, u32[]{:S(2)}) collective-permute-start(f32[64,1024]{1,0:T(8,128)S(1)} %get-tuple-element.26), channel_id=1, source_target_pairs={{0,128},{2,130},{4,132},{6,134},{8,136},{10,138},{12,140},{14,142}... | collective-permute-start | bytes 786440 | tf_op jit(solution)/shard_map/ppermute | solution.py:25
  59.3 0.6 copy-start.1
  59.3 0.7 copy-start.4
  71.4 10.9 %collective-permute-start.6 = (f32[32,1024]{1,0:T(8,128)S(1)}, f32[32,1024]{1,0:T(8,128)S(1)}, u32[]{:S(2)}, u32[]{:S(2)}) collective-permute-start(f32[32,1024]{1,0:T(8,128)S(1)} %dynamic-slice_add_fusion.3), channel_id=1, source_target_pairs={{0,256},{2,258},{4,260},{6,262},{8,264},{10,266},{12,268},{14,270}... | collective-permute-start | bytes 393224 | tf_op jit(solution)/shard_map/ppermute | solution.py:25
  75.6 6.7 %dynamic-slice-start = ((f32[4096]{0:T(1024)}, s32[]{:T(128)}), f32[1024]{0:T(1024)S(1)}, s32[]{:S(2)}) async-start(f32[4096]{0:T(1024)} %copy-done.1, s32[]{:T(128)} %select_n.211), calls=%async_computation.6 | async-start | bytes 8704 | tf_op jit(solution)/shard_map/dynamic_slice | solution.py:68
  82.4 10.9 %collective-permute-start.7 = (f32[32,1024]{1,0:T(8,128)S(1)}, f32[32,1024]{1,0:T(8,128)S(1)}, u32[]{:S(2)}, u32[]{:S(2)}) collective-permute-start(f32[32,1024]{1,0:T(8,128)S(1)} %compare_select_fusion), channel_id=1, source_target_pairs={{0,256},{2,258},{4,260},{6,262},{8,264},{10,266},{12,268},{14,270}... | collective-permute-start | bytes 393224 | tf_op jit(solution)/shard_map/ppermute | solution.py:25
  93.3 12.8 %collective-permute-start.8 = (f32[64,1024]{1,0:T(8,128)S(1)}, f32[64,1024]{1,0:T(8,128)S(1)}, u32[]{:S(2)}, u32[]{:S(2)}) collective-permute-start(f32[64,1024]{1,0:T(8,128)S(1)} %maximum_select_fusion.4), channel_id=1, source_target_pairs={{0,128},{2,130},{4,132},{6,134},{8,136},{10,138},{12,140},{14,142}... | collective-permute-start | bytes 786440 | tf_op jit(solution)/shard_map/ppermute | solution.py:25
  98.9 23.4 %all-to-all-start.2 = ((f32[4,2,64,256]{3,2,1,0:T(8,128)}), f32[4,2,64,256]{3,2,1,0:T(8,128)S(1)}, u32[]{:S(2)}, u32[]{:S(2)}) async-start(f32[4,2,64,256]{3,2,1,0:T(8,128)} %fusion.2), calls=%async_computation.2 | async-start | bytes 1048576 | tf_op jit(solution)/shard_map/all_to_all | solution.py:45
  106.1 13.3 %collective-permute-start.9 = (f32[128,1024]{1,0:T(8,128)S(1)}, f32[128,1024]{1,0:T(8,128)S(1)}, u32[]{:S(2)}, u32[]{:S(2)}) collective-permute-start(f32[128,1024]{1,0:T(8,128)S(1)} %maximum_select_fusion.2), channel_id=1, source_target_pairs={{0,64},{2,66},{4,68},{6,70},{8,72},{10,74},{12,76},{14,78},{16,80}... | collective-permute-start | bytes 1572872 | tf_op jit(solution)/shard_map/ppermute | solution.py:25
  122.3 22.3 %collective-permute-start.10 = (f32[4,2,64,256]{3,2,1,0:T(8,128)S(1)}, f32[4,2,64,256]{3,2,1,0:T(8,128)S(1)}, u32[]{:S(2)}, u32[]{:S(2)}) collective-permute-start(f32[4,2,64,256]{3,2,1,0:T(8,128)S(1)} %all-to-all-done.2), channel_id=1, source_target_pairs={{0,64},{2,66},{4,68},{6,70},{8,72},{10,74},{12,76},{14,78},{16,80}... | collective-permute-start | bytes 1572872 | tf_op jit(solution)/shard_map/ppermute | solution.py:25
  126.2 13.8 %all-to-all-start.3 = ((f32[4,128,256]{2,1,0:T(8,128)}), f32[4,128,256]{2,1,0:T(8,128)S(1)}, u32[]{:S(2)}, u32[]{:S(2)}) async-start(f32[4,128,256]{2,1,0:T(8,128)} %bitcast.16), calls=%async_computation.3 | async-start | bytes 1048576 | tf_op jit(solution)/shard_map/all_to_all | solution.py:45
  140.9 13.0 %all-to-all-start.4 = ((f32[4,128,256]{2,1,0:T(8,128)}), f32[4,128,256]{2,1,0:T(8,128)S(1)}, u32[]{:S(2)}, u32[]{:S(2)}) async-start(f32[4,128,256]{2,1,0:T(8,128)} %broadcast_in_dim.58), calls=%async_computation.4 | async-start | bytes 1048576 | tf_op jit(solution)/shard_map/all_to_all | solution.py:45
  154.6 4.6 %collective-permute-start.11 = (f32[4,256,256]{2,1,0:T(8,128)S(1)}, f32[4,256,256]{2,1,0:T(8,128)S(1)}, u32[]{:S(2)}, u32[]{:S(2)}) collective-permute-start(f32[4,256,256]{2,1,0:T(8,128)S(1)} %convolution_bitcast_fusion), channel_id=1, source_target_pairs={{0,32},{2,34},{4,36},{6,38},{8,40},{10,42},{12,44},{14,46},{16,48}... | collective-permute-start | bytes 3145736 | tf_op jit(solution)/shard_map/ppermute | solution.py:25
  160.8 20.1 %all-to-all-start.5 = ((f32[4,256,256]{2,1,0:T(8,128)}), f32[4,256,256]{2,1,0:T(8,128)S(1)}, u32[]{:S(2)}, u32[]{:S(2)}) async-start(f32[4,256,256]{2,1,0:T(8,128)} %fusion), calls=%async_computation.5 | async-start | bytes 2097152 | tf_op jit(solution)/shard_map/all_to_all | solution.py:45
  180.9 25.2 %collective-permute-start.12 = (f32[128,256]{1,0:T(8,128)S(1)}, f32[128,256]{1,0:T(8,128)S(1)}, u32[]{:S(2)}, u32[]{:S(2)}) collective-permute-start(f32[128,256]{1,0:T(8,128)S(1)} %constant_dynamic-slice_fusion.1), channel_id=1, source_target_pairs={{0,1},{2,3},{4,5},{6,7},{8,9},{10,11},{12,13},{14,15},{16,17},{18,... | collective-permute-start | bytes 393224 | tf_op jit(solution)/shard_map/ppermute | solution.py:25
